TPU v7x, 32 devices: a whole 2x2x4 slice. The times are simulated.
32 devices in a mesh: seq: 8 (over y, x, core), head: 4 (over z).
Axes of the slice: x: 2, y: 2, z: 4, core: 2. Of those that a mesh axis runs over, the one named last changes fastest.
Arguments:
- main_query: bfloat16 [1024, 73728], P('seq', 'head'), may hold values from -18 to 18
- latent: bfloat16 [2048, 576], P('seq'), may hold values from -6 to 6
- main_outside: float32 [1024, 128], P('seq', 'head'), may hold values from 5 to 11
- index_query: bfloat16 [1024, 8192], P('seq', 'head'), may hold values from -6 to 6
- index_weights: float32 [1024, 64], P('seq', 'head'), may hold values from -2.4 to 2.4
- index_keys: bfloat16 [2048, 128], P('seq'), may hold values from -6 to 6
- index_outside: float32 [1024], P('seq'), may hold values from 6 to 10
- query_pos: int32 [1024], P('seq'), may hold values from 1 to 4095, as said below
- key_pos: int32 [2048], P('seq'), may hold values from 0 to 4095, as said below
Outputs:
- grad_index_query: bfloat16 [1024, 8192], P('seq', 'head')
- grad_index_weights: float32 [1024, 64], P('seq', 'head')
- grad_index_keys: float32 [2048, 128], P('seq')
Inputs may be any that keep to these rules, and one draw needn't show every extreme that they name: `key_pos`: key j of block b stands at 2 * 256 * b + 2 * j or one more; key 0 of a block at 2 * 256 * b exactly. `query_pos`: queries of block b stand at 2 * 256 * b + 1 to 2 * 256 * b + 2 * 256 - 1.
All inputs are finite; a program needn't handle non-finite values.
Results may differ from a plain program's by a relative error of at most 0.00205.
Values may be sent and summed in bfloat16 or wider, within the bound.
No kernel may reach another device: no remote copies, remote signals or barrier semaphores. Data moves between devices by JAX's collectives and lax.ppermute only.
A program may use at most 128 MiB of HBM per device.

v0:
```python
import jax
import jax.numpy as jnp
from jax import lax
from jax.sharding import PartitionSpec as P

IDIM = 128
KB = 256
STEPS = 4


NEGATIVE = -1e30
SCORE_SCALE = 192.0 ** (-0.5)


def passed_along(block, axis, distance):
    devices = range(lax.axis_size(axis))
    route = [(i - distance, i) for i in devices if i - distance in devices]
    return lax.ppermute(block, axis, route)


def head_mass(scores, visible, outside):
    masked = jnp.where(visible[None], scores, NEGATIVE)
    highest = jnp.maximum(jnp.max(masked, axis=2), outside.T)
    expo = jnp.exp(masked - highest[:, :, None])
    total = jnp.sum(expo, axis=2) + jnp.exp(outside.T - highest)
    return jnp.sum(expo / total[:, :, None], axis=0)


def score_grad(mass, index_score, visible, outside):
    target = mass / jnp.sum(mass, axis=1, keepdims=True)
    masked = jnp.where(visible, index_score, NEGATIVE)
    highest = jnp.maximum(jnp.max(masked, axis=1), outside)
    expo = jnp.exp(masked - highest[:, None])
    total = jnp.sum(expo, axis=1) + jnp.exp(outside - highest)
    return (expo / total[:, None] - target) * (STEPS * KB)


def shards(
    main_query,
    latent,
    main_outside,
    index_query,
    index_weights,
    index_keys,
    index_outside,
    query_pos,
    key_pos,
):
    query_rows = main_query.shape[0]
    block_keys = latent.shape[0]
    width = latent.shape[1]
    local_heads = main_outside.shape[1]
    local_index = index_weights.shape[1]
    index_width = index_keys.shape[1]
    window = STEPS * block_keys
    factor = IDIM ** (-0.5)
    position = lax.axis_index("seq")
    latent_parts = []
    index_parts = []
    for distance in range(STEPS - 1, 0, -1):
        latent_parts.append(passed_along(latent, "seq", distance))
        index_parts.append(passed_along(index_keys, "seq", distance))
    latent_window = jnp.concatenate(latent_parts + [latent], 0)
    key_window = jnp.concatenate(index_parts + [index_keys], 0)
    slot_block = jnp.arange(window, dtype=jnp.int32) // block_keys
    lagging = STEPS - 1 - slot_block
    places_full = jnp.concatenate([jnp.zeros((window - block_keys,), jnp.int32), key_pos], 0)
    causal = (slot_block < STEPS - 1)[None, :] | (places_full[None, :] <= query_pos[:, None])
    visible = (position >= lagging)[None, :] & causal
    queries = main_query.reshape(query_rows, local_heads, width)
    scores = (
        jnp.einsum("qhc,wc->hqw", queries, latent_window, preferred_element_type=jnp.float32)
        * SCORE_SCALE
    )
    mass_part = head_mass(scores, visible, main_outside)
    index_rows = index_query.reshape(query_rows, local_index, index_width)
    activity = (
        jnp.einsum("qjd,wd->jqw", index_rows, key_window, preferred_element_type=jnp.float32)
        * factor
    )
    rectified = jnp.maximum(activity, 0.0)
    index_part = jnp.einsum("qj,jqw->qw", index_weights, rectified)
    mass, index_score = (
        lax.psum_scatter(mass_part, "head", scatter_dimension=0, tiled=True),
        lax.psum_scatter(index_part, "head", scatter_dimension=0, tiled=True),
    )
    share = mass.shape[0]
    start = lax.axis_index("head") * share
    visible_rows = lax.dynamic_slice_in_dim(visible, start, share, 0)
    outside_rows = lax.dynamic_slice_in_dim(index_outside, start, share, 0)
    dscore = lax.all_gather(
        score_grad(mass, index_score, visible_rows, outside_rows), "head", axis=0, tiled=True
    )
    gated = dscore[None] * index_weights.T[:, :, None] * (activity > 0).astype(jnp.float32)
    key_wide = key_window.astype(jnp.float32)
    rows_wide = index_rows.astype(jnp.float32)
    grad_query = (
        jnp.einsum("jqw,wd->qjd", gated, key_wide, precision=lax.Precision.HIGHEST) * factor
    )
    grad_query = grad_query.astype(jnp.bfloat16).reshape(query_rows, local_index * index_width)
    grad_weight = jnp.einsum("qw,jqw->qj", dscore, rectified)
    grad_window = (
        jnp.einsum("jqw,qjd->wd", gated, rows_wide, precision=lax.Precision.HIGHEST) * factor
    )
    grad_parts = grad_window.reshape(STEPS, block_keys, index_width)
    grad_total = grad_parts[STEPS - 1]
    for distance in range(1, STEPS):
        grad_total = grad_total + passed_along(grad_parts[STEPS - 1 - distance], "seq", -distance)
    grad_keys = lax.psum(grad_total, "head")
    return (grad_query, grad_weight, grad_keys)


def solution(mesh):
    in_specs = (
        P("seq", "head"),
        P("seq", None),
        P("seq", "head"),
        P("seq", "head"),
        P("seq", "head"),
        P("seq", None),
        P("seq"),
        P("seq"),
        P("seq"),
    )
    out_specs = (P("seq", "head"), P("seq", "head"), P("seq", None))
    return jax.shard_map(shards, mesh=mesh, in_specs=in_specs, out_specs=out_specs, check_vma=False)
```

profile of v0, /device:TPU:0, one launch (start us, length us, event | category | flops | bytes accessed | tf_op | source)
XLA Modules:
  0.0 175.3 jit_solution(12981892077039269226)
XLA Ops:
  7.2 0.0 copy-start
  7.2 0.0 reduce-scatter.7.cloned.1.call-start
  7.2 2.5 %collective-permute-start.2 = (bf16[256,128]{1,0:T(8,128)(2,1)}, bf16[256,128]{1,0:T(8,128)(2,1)S(1)}, u32[]{:S(2)}, u32[]{:S(2)}) collective-permute-start(bf16[256,128]{1,0:T(8,128)(2,1)} %param.14), channel_id=1, source_target_pairs={{0,4},{4,8},{8,12},{12,16},{16,20},{20,24},{24,28},{1,5},{5,9},{9,... | collective-permute-start | bytes 196616 | tf_op jit(solution)/shard_map/ppermute | solution.py:18
  9.7 4.4 %collective-permute-start.1 = (bf16[256,128]{1,0:T(8,128)(2,1)}, bf16[256,128]{1,0:T(8,128)(2,1)S(1)}, u32[]{:S(2)}, u32[]{:S(2)}) collective-permute-start(bf16[256,128]{1,0:T(8,128)(2,1)} %param.14), channel_id=1, source_target_pairs={{0,8},{4,12},{8,16},{12,20},{16,24},{20,28},{1,9},{5,13},{9,17},{1... | collective-permute-start | bytes 196616 | tf_op jit(solution)/shard_map/ppermute | solution.py:18
  14.2 4.3 %collective-permute-start = (bf16[256,128]{1,0:T(8,128)(2,1)}, bf16[256,128]{1,0:T(8,128)(2,1)S(1)}, u32[]{:S(2)}, u32[]{:S(2)}) collective-permute-start(bf16[256,128]{1,0:T(8,128)(2,1)} %param.14), channel_id=1, source_target_pairs={{0,12},{4,16},{8,20},{12,24},{16,28},{1,13},{5,17},{9,21},{13,25},... | collective-permute-start | bytes 196616 | tf_op jit(solution)/shard_map/ppermute | solution.py:18
  18.5 1.3 collective-permute-start.5
  19.8 2.9 %collective-permute-start.4 = (bf16[256,576]{0,1:T(8,128)(2,1)}, bf16[256,576]{0,1:T(8,128)(2,1)S(1)}, u32[]{:S(2)}, u32[]{:S(2)}) collective-permute-start(bf16[256,576]{0,1:T(8,128)(2,1)} %param.10), channel_id=1, source_target_pairs={{0,8},{4,12},{8,16},{12,20},{16,24},{20,28},{1,9},{5,13},{9,17},{1... | collective-permute-start | bytes 884744 | tf_op jit(solution)/shard_map/ppermute | solution.py:18
  22.8 0.7 concatenate.10
  23.4 0.8 or_and_fusion
  24.3 0.3 copy.34
  24.5 6.6 %copy.35 = bf16[128,18432]{0,1:T(8,128)(2,1)} copy(bf16[128,18432]{1,0:T(8,128)(2,1)} %param.9) | data formatting | bytes 9437184 | tf_op args[0]
  31.2 1.8 %collective-permute-start.3 = (bf16[256,576]{0,1:T(8,128)(2,1)S(1)}, bf16[256,576]{0,1:T(8,128)(2,1)S(1)}, u32[]{:S(2)}, u32[]{:S(2)}) collective-permute-start(bf16[256,576]{0,1:T(8,128)(2,1)S(1)} %copy-done.5), channel_id=1, source_target_pairs={{0,12},{4,16},{8,20},{12,24},{16,28},{1,13},{5,17},{9,21},{13,25},... | collective-permute-start | bytes 884744 | tf_op jit(solution)/shard_map/ppermute | solution.py:18
  33.1 4.2 %multiply_compare_fusion = (pred[1024,128,16]{1,0,2:T(32,128)(4,1)}, f32[1024,128,16]{1,0,2:T(8,128)S(1)}) fusion(bf16[256,128]{1,0:T(8,128)(2,1)S(1)} %copy-done.6, bf16[256,128]{1,0:T(8,128)(2,1)S(1)} %collective-permute-done.2, bf16[256,128]{1,0:T(8,128)(2,1)S(1)} %collective-permute-done.1, bf16[256,128]{1,0:T(8,128)(2,1)S(1)} %collective-permute-done, ...), kind=kOutput, calls=%fused_computation.12 | convolution fusion | flops 542113792 | bytes 11272192 | tf_op jit(solution)/shard_map/qjd,wd->jqw/dot_general | solution.py:78
  37.3 3.2 %copy-done.1 = f32[1024,128,16]{1,0,2:T(8,128)} copy-done((f32[1024,128,16]{1,0,2:T(8,128)}, f32[1024,128,16]{1,0,2:T(8,128)S(1)}, u32[]{:S(2)}) %copy-start.1) | copy-done | bytes 8388632
  40.5 1.2 multiply_reduce_fusion.1
  41.7 1.0 copy.56
  42.7 0.0 reduce-scatter.7.cloned.1.call-update
  42.7 0.2 reduce-scatter.9.cloned.1.call-start
  43.0 0.0 copy-start.2
  43.0 13.2 %fusion.1 = (f32[32,128]{1,0:T(8,128)S(1)}, f32[1024,128,32]{1,0,2:T(8,128)}) fusion(pred[128,1024]{0,1:T(8,128)(4,1)S(1)} %copy.34, bf16[128,32,576]{0,2,1:T(8,128)(2,1)} %bitcast.76, bf16[256,576]{0,1:T(8,128)(2,1)S(1)} %copy-done.5, bf16[256,576]{0,1:T(8,128)(2,1)S(1)} %collective-permute-done.5, bf16[256,576]{0,1:T(8,128)(2,1)S(1)} %collective-permute-done.4, ...), kind=kOutput, calls=%fused_computation.4 | convolution fusion | flops 4849135616 | bytes 22822912 | tf_op jit(solution)/shard_map/qhc,wc->hqw/dot_general | solution.py:72
  56.2 9.3 %fusion = f32[32,128]{1,0:T(8,128)S(1)} fusion(f32[1024,128,32]{1,0,2:T(8,128)} %get-tuple-element.21, f32[32,128]{1,0:T(8,128)S(1)} %bitcast_maximum_fusion, pred[128,1024]{0,1:T(8,128)(4,1)S(1)} %copy.34), kind=kLoop, calls=%fused_computation.3 | loop fusion | flops 16773120 | bytes 16941056 | tf_op jit(solution)/shard_map/reduce_sum | solution.py:25
  65.6 0.0 copy-start.4
  65.6 8.0 %divide_reduce_fusion = f32[128,1024]{0,1:T(8,128)S(1)} fusion(f32[1024,128,32]{1,0,2:T(8,128)} %get-tuple-element.21, f32[32,128]{1,0:T(8,128)S(1)} %fusion.33, f32[32,128]{1,0:T(8,128)S(1)} %bitcast_maximum_fusion, pred[128,1024]{0,1:T(8,128)(4,1)S(1)} %copy.34), kind=kLoop, calls=%fused_computation.2 | loop fusion | flops 20840448 | bytes 17465344 | tf_op jit(solution)/shard_map/reduce_sum | solution.py:26
  73.6 1.0 copy.58
  74.6 0.0 reduce-scatter.9.cloned.1.call-update
  74.7 0.0 all-reduce.3.cloned.1.call-start
  74.7 0.0 reduce-scatter.7.cloned.1.call-done
  74.7 1.0 fusion.31
  75.8 0.1 dynamic-slice_maximum_fusion
  75.9 1.1 fusion.30
  77.0 0.1 exponential_add_fusion
  77.0 18.8 %reduce-scatter.9.cloned.1.call-done = f32[32,1024]{1,0:T(8,128)} async-done(((f32[128,1024]{1,0:T(8,128)}), f32[32,1024]{1,0:T(8,128)}) %reduce-scatter.9.cloned.1.call-update) | async-done | bytes 131088 | tf_op jit(solution)/shard_map/reduce_scatter | solution.py:84
  95.9 1.0 reduce_sum.39
  96.9 1.1 subtract_multiply_fusion
  98.0 16.1 %all_gather.3 = f32[128,1024]{1,0:T(8,128)S(1)} all-gather(f32[32,1024]{1,0:T(8,128)S(1)} %subtract_multiply_fusion), channel_id=1, replica_groups=mesh['seq'=8,'head'=4] {'head'}, dimensions={0}, use_global_device_ids=true | all-gather | bytes 655360 | tf_op jit(solution)/shard_map/all_gather | solution.py:91
  114.1 0.2 copy.37
  114.3 6.4 %fusion.15 = f32[1024,128]{1,0:T(8,128)S(1)} fusion(pred[1024,128,16]{1,0,2:T(32,128)(4,1)} %get-tuple-element.18, f32[16,128]{1,0:T(8,128)S(1)} %bitcast.78, f32[128,1024]{0,1:T(8,128)S(1)} %copy.37, bf16[128,2048]{1,0:T(8,128)(2,1)S(1)} %copy-done), kind=kOutput, calls=%fused_computation.22 | convolution fusion | flops 3225550848 | bytes 3678208 | tf_op jit(solution)/shard_map/jqw,qjd->wd/dot_general | solution.py:103
  120.7 1.3 collective-permute-start.8
  122.0 1.3 collective-permute-start.7
  123.3 1.3 collective-permute-start.6
  124.6 5.1 %multiply_reduce_fusion = f32[128,16]{0,1:T(8,128)} fusion(f32[1024,128,16]{1,0,2:T(8,128)} %copy-done.1, f32[128,1024]{0,1:T(8,128)S(1)} %copy.37), kind=kLoop, calls=%fused_computation.5 | loop fusion | flops 8386560 | bytes 8921088 | tf_op jit(solution)/shard_map/qw,jqw->qj/dot_general | solution.py:101
  129.7 0.5 collective-permute-done.7
  130.2 0.7 fusion.29
  130.9 0.0 all-reduce.3.cloned.1.call-update
  130.9 5.7 %fusion.13 = bf16[128,16,128]{2,0,1:T(8,128)(2,1)S(1)} fusion(pred[1024,128,16]{1,0,2:T(32,128)(4,1)} %get-tuple-element.18, f32[16,128]{1,0:T(8,128)S(1)} %bitcast.79, f32[128,1024]{0,1:T(8,128)S(1)} %copy.37, bf16[256,128]{1,0:T(8,128)(2,1)S(1)} %copy-done.6, bf16[256,128]{1,0:T(8,128)(2,1)S(1)} %collective-permute-done.2, ...), kind=kOutput, calls=%fused_computation.20 | convolution fusion | flops 3226992640 | bytes 3416064 | tf_op jit(solution)/shard_map/jqw,wd->qjd/dot_general | solution.py:98
  136.6 1.0 copy.41
  137.6 29.5 %all-reduce.3.cloned.1.call-done = f32[256,128]{1,0:T(8,128)} async-done(((f32[256,128]{1,0:T(8,128)}), f32[256,128]{1,0:T(8,128)}) %all-reduce.3.cloned.1.call-update) | async-done | bytes 131088 | tf_op jit(solution)/shard_map/psum | solution.py:109
  167.2 1.6 copy.80
  (22 shorter events, 0.1 us)
Async XLA Ops:
  7.2 25.9 %copy-start = (bf16[128,2048]{1,0:T(8,128)(2,1)S(1)}, bf16[128,2048]{1,0:T(8,128)(2,1)}, u32[]{:S(2)}) copy-start(bf16[128,2048]{1,0:T(8,128)(2,1)} %param.12) | copy-start | bytes 1572868
  7.2 25.9 %copy-start.6 = (bf16[256,128]{1,0:T(8,128)(2,1)S(1)}, bf16[256,128]{1,0:T(8,128)(2,1)}, u32[]{:S(2)}) copy-start(bf16[256,128]{1,0:T(8,128)(2,1)} %param.14) | copy-start | bytes 196612
  7.2 24.0 %copy-start.5 = (bf16[256,576]{0,1:T(8,128)(2,1)S(1)}, bf16[256,576]{0,1:T(8,128)(2,1)}, u32[]{:S(2)}) copy-start(bf16[256,576]{0,1:T(8,128)(2,1)} %param.10) | copy-start | bytes 884740
  7.2 67.5 %reduce-scatter.7.cloned.1.call-start = ((), (), s32[]{:S(2)}) async-start(), calls=%async_computation.3 | async-start | bytes 655360 | tf_op jit(solution)/shard_map/reduce_scatter | solution.py:85
  7.2 23.9 %collective-permute-start.2 = (bf16[256,128]{1,0:T(8,128)(2,1)}, bf16[256,128]{1,0:T(8,128)(2,1)S(1)}, u32[]{:S(2)}, u32[]{:S(2)}) collective-permute-start(bf16[256,128]{1,0:T(8,128)(2,1)} %param.14), channel_id=1, source_target_pairs={{0,4},{4,8},{8,12},{12,16},{16,20},{20,24},{24,28},{1,5},{5,9},{9,... | collective-permute-start | bytes 196616 | tf_op jit(solution)/shard_map/ppermute | solution.py:18
  9.7 23.3 %collective-permute-start.1 = (bf16[256,128]{1,0:T(8,128)(2,1)}, bf16[256,128]{1,0:T(8,128)(2,1)S(1)}, u32[]{:S(2)}, u32[]{:S(2)}) collective-permute-start(bf16[256,128]{1,0:T(8,128)(2,1)} %param.14), channel_id=1, source_target_pairs={{0,8},{4,12},{8,16},{12,20},{16,24},{20,28},{1,9},{5,13},{9,17},{1... | collective-permute-start | bytes 196616 | tf_op jit(solution)/shard_map/ppermute | solution.py:18
  14.2 18.9 %collective-permute-start = (bf16[256,128]{1,0:T(8,128)(2,1)}, bf16[256,128]{1,0:T(8,128)(2,1)S(1)}, u32[]{:S(2)}, u32[]{:S(2)}) collective-permute-start(bf16[256,128]{1,0:T(8,128)(2,1)} %param.14), channel_id=1, source_target_pairs={{0,12},{4,16},{8,20},{12,24},{16,28},{1,13},{5,17},{9,21},{13,25},... | collective-permute-start | bytes 196616 | tf_op jit(solution)/shard_map/ppermute | solution.py:18
  18.5 24.5 %collective-permute-start.5 = (bf16[256,576]{0,1:T(8,128)(2,1)}, bf16[256,576]{0,1:T(8,128)(2,1)S(1)}, u32[]{:S(2)}, u32[]{:S(2)}) collective-permute-start(bf16[256,576]{0,1:T(8,128)(2,1)} %param.10), channel_id=1, source_target_pairs={{0,4},{4,8},{8,12},{12,16},{16,20},{20,24},{24,28},{1,5},{5,9},{9,... | collective-permute-start | bytes 884744 | tf_op jit(solution)/shard_map/ppermute | solution.py:18
  19.8 23.2 %collective-permute-start.4 = (bf16[256,576]{0,1:T(8,128)(2,1)}, bf16[256,576]{0,1:T(8,128)(2,1)S(1)}, u32[]{:S(2)}, u32[]{:S(2)}) collective-permute-start(bf16[256,576]{0,1:T(8,128)(2,1)} %param.10), channel_id=1, source_target_pairs={{0,8},{4,12},{8,16},{12,20},{16,24},{20,28},{1,9},{5,13},{9,17},{1... | collective-permute-start | bytes 884744 | tf_op jit(solution)/shard_map/ppermute | solution.py:18
  31.2 9.3 %copy-start.3 = (f32[128,16]{0,1:T(8,128)S(1)}, f32[128,16]{0,1:T(8,128)}, u32[]{:S(2)}) copy-start(f32[128,16]{0,1:T(8,128)} %param.13) | copy-start | bytes 24580
  31.2 11.8 %collective-permute-start.3 = (bf16[256,576]{0,1:T(8,128)(2,1)S(1)}, bf16[256,576]{0,1:T(8,128)(2,1)S(1)}, u32[]{:S(2)}, u32[]{:S(2)}) collective-permute-start(bf16[256,576]{0,1:T(8,128)(2,1)S(1)} %copy-done.5), channel_id=1, source_target_pairs={{0,12},{4,16},{8,20},{12,24},{16,28},{1,13},{5,17},{9,21},{13,25},... | collective-permute-start | bytes 884744 | tf_op jit(solution)/shard_map/ppermute | solution.py:18
  37.3 3.2 %copy-start.1 = (f32[1024,128,16]{1,0,2:T(8,128)}, f32[1024,128,16]{1,0,2:T(8,128)S(1)}, u32[]{:S(2)}) copy-start(f32[1024,128,16]{1,0,2:T(8,128)S(1)} %get-tuple-element.19) | copy-start | bytes 25165828
  42.7 53.1 %reduce-scatter.9.cloned.1.call-start = ((), (), s32[]{:S(2)}) async-start(), calls=%async_computation.4 | async-start | bytes 655360 | tf_op jit(solution)/shard_map/reduce_scatter | solution.py:84
  43.0 13.3 %copy-start.2 = (f32[128,32]{0,1:T(8,128)S(1)}, f32[128,32]{0,1:T(8,128)}, u32[]{:S(2)}) copy-start(f32[128,32]{0,1:T(8,128)} %param.11) | copy-start | bytes 49156
  65.6 10.2 %copy-start.4 = (f32[128]{0:T(128)S(1)}, f32[128]{0:T(128)}, u32[]{:S(2)}) copy-start(f32[128]{0:T(128)} %param.15) | copy-start | bytes 1540
  74.7 92.5 %all-reduce.3.cloned.1.call-start = ((), (), s32[]{:S(2)}) async-start(), calls=%async_computation.2 | async-start | bytes 262144 | tf_op jit(solution)/shard_map/psum | solution.py:109
  120.7 9.0 %collective-permute-start.8 = (f32[256,128]{1,0:T(8,128)S(1)}, f32[256,128]{1,0:T(8,128)S(1)}, u32[]{:S(2)}, u32[]{:S(2)}) collective-permute-start(f32[256,128]{1,0:T(8,128)S(1)} %get-tuple-element.16), channel_id=1, source_target_pairs={{12,0},{16,4},{20,8},{24,12},{28,16},{13,1},{17,5},{21,9},{25,13},... | collective-permute-start | bytes 393224 | tf_op jit(solution)/shard_map/ppermute | solution.py:18
  122.0 8.2 %collective-permute-start.7 = (f32[256,128]{1,0:T(8,128)S(1)}, f32[256,128]{1,0:T(8,128)S(1)}, u32[]{:S(2)}, u32[]{:S(2)}) collective-permute-start(f32[256,128]{1,0:T(8,128)S(1)} %get-tuple-element.17), channel_id=1, source_target_pairs={{8,0},{12,4},{16,8},{20,12},{24,16},{28,20},{9,1},{13,5},{17,9},{2... | collective-permute-start | bytes 393224 | tf_op jit(solution)/shard_map/ppermute | solution.py:18
  123.3 6.9 %collective-permute-start.6 = (f32[256,128]{1,0:T(8,128)S(1)}, f32[256,128]{1,0:T(8,128)S(1)}, u32[]{:S(2)}, u32[]{:S(2)}) collective-permute-start(f32[256,128]{1,0:T(8,128)S(1)} %get-tuple-element.15), channel_id=1, source_target_pairs={{4,0},{8,4},{12,8},{16,12},{20,16},{24,20},{28,24},{5,1},{9,5},{13... | collective-permute-start | bytes 393224 | tf_op jit(solution)/shard_map/ppermute | solution.py:18
Sparse Core Ops, SparseCore 0:
  42.8 20.9 reduce-scatter.6
  74.8 21.0 reduce-scatter.8
  131.0 36.0 all-reduce.2
where the time goes:
time: 176 us; the launch traced here: 175 us
  waiting for transfers between devices  49 us (28%)
  other arithmetic  29.5 us (17%)
  matrix products  29.5 us (17%)
  starting transfers between devices  21.4 us (12%)
  blocking collectives  16.1 us (9%)
  local copies, waits for them, and re-layouts  15.6 us (9%)
  between operations  14 us (8%)
    psum x1, waiting for transfers between devices, shards(): grad_keys = lax.psum(grad_total, 'head')  29.5 us
    ppermute x9, starting transfers between devices, passed_along(): return lax.ppermute(block, axis, route)  21.1 us
    reduce_scatter x1, waiting for transfers between devices, shards(): lax.psum_scatter(mass_part, 'head', scatter_dimension=0, tiled=True)  18.8 us
    all_gather x1, blocking collectives, shards(): lax.all_gather(score_grad(mass, index_score, visible_rows, outside_rows),...  16.1 us
    unnamed x19, local copies, waits for them, and re-layouts  14.5 us
    dot_general x1, matrix products, shards(): jnp.einsum('qhc,wc->hqw', queries, latent_window, preferred_element_type=...  13.2 us
    reduce_sum x1, other arithmetic, head_mass(): total = jnp.sum(expo, axis=2) + jnp.exp(outside.T - highest)  9.34 us
    reduce_sum x1, other arithmetic, head_mass(): return jnp.sum(expo / total[:, :, None], axis=0)  8 us
  transfers between devices with their start and end apart: 12, of which 3 were waited for; matrix products, arithmetic and copies ran while one was open for 35% of the time, Pallas kernels for 0%

commit v1 on v0

--- a/solution.py
+++ b/solution.py
@@ -1,6 +1,10 @@
+import functools
+
 import jax
 import jax.numpy as jnp
 from jax import lax
+from jax.experimental import pallas as pl
+from jax.experimental.pallas import tpu as pltpu
 from jax.sharding import PartitionSpec as P
 
 IDIM = 128
@@ -35,7 +39,7 @@
     return (expo / total[:, None] - target) * (STEPS * KB)
 
 
-def shards(
+def plain_shards(
     main_query,
     latent,
     main_outside,
@@ -110,6 +114,434 @@
     return (grad_query, grad_weight, grad_keys)
 
 
+LOG2E = 1.4426950408889634
+LAT = 576
+PACK = 768
+GROUPS = 4
+SAFE = 1e30
+NT = (((1,), (1,)), ((), ()))
+
+
+def dot(a, b, dims=(((1,), (0,)), ((), ()))):
+    return lax.dot_general(a, b, dims, preferred_element_type=jnp.float32)
+
+
+def slots_of(even):
+    return jnp.where(even, 0, 2), jnp.where(even, 2, 0)
+
+
+def main_kernel(heads, place, q, own, a, b, c, outside, qpos, kpos, *rest):
+    outs, (k_even, k_odd, e, inv, out_exp, mass) = rest[:GROUPS], rest[GROUPS:]
+    step, steps = pl.program_id(0), pl.num_programs(0)
+    z, position = place[0], place[1]
+    rows, kb = q.shape[0], own.shape[0]
+    half = heads // 2
+    window = STEPS * kb
+    present = [jnp.where(position >= STEPS - 1 - i, 1.0, 0.0).astype(jnp.float32) for i in range(STEPS)]
+    now = lax.rem(step, 2)
+
+    @pl.when(step == 0)
+    def _():
+        slot_a, slot_b = slots_of(lax.rem(position, 2) == 0)
+        zeros = jnp.zeros((kb, 64), jnp.bfloat16)
+        for block, slot in ((own, 3), (a, slot_a), (b, slot_b), (c, 1)):
+            at = pl.ds(pl.multiple_of(slot * kb, kb), kb)
+            k_even[at, :] = block[:, :640]
+            k_odd[at, :] = jnp.concatenate([zeros, block[:, :LAT]], 1)
+        mass[...] = jnp.zeros_like(mass)
+        lanes = jnp.concatenate([outside[...], jnp.full((rows, 128 - outside.shape[1]), NEGATIVE, jnp.float32)], 1)
+        out_exp[...] = jnp.exp(lanes)
+
+    def add_mass(buffer):
+        for r in range(0, rows, 32):
+            for w in range(0, window, 256):
+                total = mass[r:r + 32, w:w + 256]
+                for h in range(heads):
+                    scale = inv[buffer, h * rows + r:h * rows + r + 32, :]
+                    part = e[buffer, h * rows + r:h * rows + r + 32, w:w + 256]
+                    total = total + part * jnp.concatenate([scale, scale], 1)
+                mass[r:r + 32, w:w + 256] = total
+
+    @pl.when(step > 0)
+    def _():
+        add_mass(1 - now)
+
+    lane = lax.broadcasted_iota(jnp.int32, (32, 128), 1)
+    worst = jnp.zeros((32, 1), jnp.float32)
+    for parity, keys in ((0, k_even), (1, k_odd)):
+        lhs = jnp.concatenate([q[:, 1152 * i + 512 * parity:1152 * i + 512 * parity + 640] for i in range(half)], 0)
+        base = parity * half * rows
+        e[now, base:base + half * rows, :] = dot(lhs, keys[...], NT)
+    for parity in range(2):
+        for i in range(half):
+            for r in range(0, rows, 32):
+                at = (parity * half + i) * rows + r
+                ex = jnp.exp2(e[now, at:at + 32, :] * (SCORE_SCALE * LOG2E))
+                causal = kpos[...] <= qpos[r:r + 32, :]
+                last = jnp.where(causal, ex[:, window - kb:], 0.0)
+                head = step * heads + 2 * i + parity
+                total = jnp.where(lane == head, out_exp[r:r + 32, :], 0.0)
+                for block in range(STEPS):
+                    piece = last if block == STEPS - 1 else ex[:, block * kb:(block + 1) * kb]
+                    e[now, at:at + 32, block * kb:(block + 1) * kb] = piece
+                    lanes = piece[:, :128]
+                    for k in range(128, kb, 128):
+                        lanes = lanes + piece[:, k:k + 128]
+                    total = total + (lanes if block == STEPS - 1 else lanes * present[block])
+                total = jnp.sum(total, axis=1, keepdims=True)
+                worst = jnp.maximum(worst, total)
+                inv[now, at:at + 32, :] = jnp.broadcast_to(1.0 / total, (32, 128))
+
+    @pl.when(jnp.logical_not(jnp.max(worst) < SAFE))
+    def _():
+        slot = lax.broadcasted_iota(jnp.int32, (rows, window), 1) // kb
+        causal = jnp.concatenate([jnp.ones((rows, window - kb), jnp.bool_), kpos[...] <= qpos[...]], 1)
+        visible = (position >= STEPS - 1 - slot) & causal
+        wide = lax.broadcasted_iota(jnp.int32, (rows, 32), 1)
+        for parity, keys in ((0, k_even), (1, k_odd)):
+
+            def exact(i, carry, parity=parity, keys=keys):
+                at = pl.multiple_of(1152 * i + 512 * parity, 128)
+                scores = dot(q[:, pl.ds(at, 640)], keys[...], NT) * SCORE_SCALE
+                masked = jnp.where(visible, scores, NEGATIVE)
+                head = step * heads + 2 * i + parity
+                mine = jnp.sum(jnp.where(wide == head, outside[...], 0.0), axis=1, keepdims=True)
+                top = jnp.maximum(jnp.max(masked, axis=1, keepdims=True), mine)
+                ex = jnp.exp(masked - top)
+                total = jnp.sum(ex, axis=1, keepdims=True) + jnp.exp(mine - top)
+                row = pl.ds(pl.multiple_of((parity * half + i) * rows, rows), rows)
+                e[now, row, :] = ex
+                inv[now, row, :] = jnp.broadcast_to(1.0 / total, (rows, 128))
+                return carry
+
+            lax.fori_loop(0, half, exact, 0)
+
+    @pl.when(step == steps - 1)
+    def _():
+        add_mass(now)
+        share = rows // GROUPS
+        for d in range(GROUPS):
+            at = pl.ds(pl.multiple_of((z ^ d) * share, share), share)
+            for block in range(STEPS):
+                lanes = slice(block * kb, (block + 1) * kb)
+                outs[d][:, lanes] = mass[at, lanes] * present[block]
+
+
+def gathered_keys(place, blocks, keys):
+    own, a, b, c = blocks
+    kb = own.shape[0]
+    slot_a, slot_b = slots_of(lax.rem(place[1], 2) == 0)
+    for block, slot in ((own, 3), (a, slot_a), (b, slot_b), (c, 1)):
+        keys[pl.ds(pl.multiple_of(slot * kb, kb), kb), :] = block[...]
+
+
+def weights_of(piece, width, count):
+    tail = piece[:, width:].astype(jnp.float32)
+    return tail[:, :count] + tail[:, count:2 * count] + tail[:, 2 * count:3 * count]
+
+
+def heads_of(piece, count):
+    return jnp.concatenate([piece[:, IDIM * j:IDIM * (j + 1)] for j in range(count)], 0)
+
+
+def index_kernel(count, place, own, a, b, c, *rest):
+    pieces, (score, gate, turned), (keys, every) = rest[:GROUPS], rest[GROUPS:GROUPS + 3], rest[GROUPS + 3:]
+    step = pl.program_id(0)
+    share = score.shape[0]
+
+    @pl.when(step == 0)
+    def _():
+        gathered_keys(place, (own, a, b, c), keys)
+        for d in range(GROUPS):
+            every[d] = pieces[d][...]
+        score[...] = jnp.zeros_like(score)
+
+    piece = every[step]
+    weight = weights_of(piece, IDIM * count, count)
+    rows = heads_of(piece, count)
+    act = dot(rows, keys[...], NT)
+    gate[...] = jnp.where(act > 0, 1.0, 0.0).astype(jnp.bfloat16)
+    scaled = weight * (IDIM ** -0.5)
+    total = score[...]
+    for j in range(count):
+        total = total + jnp.maximum(act[j * share:(j + 1) * share], 0.0) * scaled[:, j:j + 1]
+    score[...] = total
+    tall = jnp.concatenate([jnp.broadcast_to(scaled[:, j:j + 1], (share, IDIM)) for j in range(count)], 0)
+    weighted = rows.astype(jnp.float32) * tall
+    high = weighted.astype(jnp.bfloat16)
+    low = (weighted - high.astype(jnp.float32)).astype(jnp.bfloat16)
+    turned[:IDIM, :] = high.T
+    turned[IDIM:, :] = low.T
+
+
+def split(x):
+    high = x.astype(jnp.bfloat16)
+    return high, (x - high.astype(jnp.float32)).astype(jnp.bfloat16)
+
+
+def query_kernel(count, place, own, a, b, c, m0, m1, m2, m3, score, outside, qpos, kpos, gate, *rest):
+    pieces, outs, spread = rest[:GROUPS], rest[GROUPS:2 * GROUPS], rest[2 * GROUPS]
+    keys, every, back = rest[2 * GROUPS + 1:]
+    step, steps = pl.program_id(0), pl.num_programs(0)
+    position = place[1]
+    share, window = score.shape
+    kb = own.shape[0]
+
+    @pl.when(step == 0)
+    def _():
+        gathered_keys(place, (own, a, b, c), keys)
+        for d in range(GROUPS):
+            every[d] = pieces[d][...]
+        mass = (m0[...] + m1[...]) + (m2[...] + m3[...])
+        target = mass / jnp.sum(mass, axis=1, keepdims=True)
+        mine = pl.ds(pl.multiple_of(place[0] * share, share), share)
+        slot = lax.broadcasted_iota(jnp.int32, (share, window), 1) // kb
+        causal = kpos[...] <= qpos[mine, :]
+        masked = jnp.where(position >= STEPS - 1 - slot, score[...], NEGATIVE)
+        masked = jnp.concatenate([masked[:, :window - kb], jnp.where(causal, masked[:, window - kb:], NEGATIVE)], 1)
+        out = outside[mine, :]
+        top = jnp.maximum(jnp.max(masked, axis=1, keepdims=True), out)
+        expo = jnp.exp(masked - top)
+        total = jnp.sum(expo, axis=1, keepdims=True) + jnp.exp(out - top)
+        dscore = (expo / total - target) * float(window)
+        high, low = split(dscore)
+        spread[0] = high
+        spread[1] = low
+
+    piece = every[step]
+    weight = weights_of(piece, IDIM * count, count)
+    mask = gate[...]
+    grad = dot(mask * jnp.concatenate([spread[0]] * count, 0), keys[...])
+    grad = grad + dot(mask * jnp.concatenate([spread[1]] * count, 0), keys[...])
+    lane = lax.broadcasted_iota(jnp.int32, (share, 128), 1)
+    sums = jnp.zeros((share, 128), jnp.float32)
+    factor = IDIM ** -0.5
+    for j in range(count):
+        mine = grad[j * share:(j + 1) * share] * factor
+        lanes = slice(IDIM * j, IDIM * (j + 1))
+        back[step, :, lanes] = (mine * weight[:, j:j + 1]).astype(jnp.bfloat16)
+        product = jnp.sum(mine * piece[:, lanes].astype(jnp.float32), axis=1, keepdims=True)
+        sums = jnp.where(lane == j, product, sums)
+    sums = sums[:, :count]
+    high = sums.astype(jnp.bfloat16)
+    left = sums - high.astype(jnp.float32)
+    middle = left.astype(jnp.bfloat16)
+    low = (left - middle.astype(jnp.float32)).astype(jnp.bfloat16)
+    tail = jnp.concatenate([high, middle, low, jnp.zeros((share, 128 - 3 * count), jnp.bfloat16)], 1)
+    back[step, :, IDIM * count:] = tail
+
+    @pl.when(step == steps - 1)
+    def _():
+        for d in range(GROUPS):
+            outs[d][...] = back[d]
+
+
+def keys_kernel(count, gate, turned, spread, *rest):
+    outs, total = rest[:STEPS], rest[STEPS]
+    step, steps = pl.program_id(0), pl.num_programs(0)
+
+    @pl.when(step == 0)
+    def _():
+        total[...] = jnp.zeros_like(total)
+
+    mask = gate[...]
+    both = dot(turned[...], mask * jnp.concatenate([spread[0]] * count, 0))
+    low = dot(turned[:IDIM, :], mask * jnp.concatenate([spread[1]] * count, 0))
+    total[...] += both[:IDIM] + both[IDIM:] + low
+
+    @pl.when(step == steps - 1)
+    def _():
+        kb = outs[0].shape[0]
+        for i in range(STEPS):
+            outs[i][...] = total[:, i * kb:(i + 1) * kb].T
+
+
+def place_kernel(count, place, *rest):
+    pieces, (grad, weight) = rest[:GROUPS], rest[GROUPS:]
+    share = pieces[0].shape[0]
+    for d in range(GROUPS):
+        at = pl.ds(pl.multiple_of((place[0] ^ d) * share, share), share)
+        grad[at, :] = pieces[d][:, :IDIM * count]
+        weight[at, :] = weights_of(pieces[d][...], IDIM * count, count)
+
+
+SMEM = pl.BlockSpec(memory_space=pltpu.SMEM)
+
+
+def whole(array):
+    rank = len(array.shape)
+    return pl.BlockSpec(array.shape, lambda i: (0,) * rank)
+
+
+def params(mib):
+    return pltpu.CompilerParams(vmem_limit_bytes=mib << 20)
+
+
+def along(x, axis, route):
+    return lax.ppermute(x, axis, [(i, j) for i, j in route if 0 <= j < lax.axis_size(axis)])
+
+
+def shards(
+    main_query,
+    latent,
+    main_outside,
+    index_query,
+    index_weights,
+    index_keys,
+    index_outside,
+    query_pos,
+    key_pos,
+):
+    rows = main_query.shape[0]
+    kb = latent.shape[0]
+    heads = main_outside.shape[1]
+    count = index_weights.shape[1]
+    share = rows // GROUPS
+    window = STEPS * kb
+    n_seq = lax.axis_size("seq")
+    z, position = lax.axis_index("head"), lax.axis_index("seq")
+    place = jnp.stack([z, position]).astype(jnp.int32)
+    bf16, f32 = jnp.bfloat16, jnp.float32
+
+    packed = jnp.concatenate([latent, jnp.zeros((kb, PACK - LAT - IDIM), bf16), index_keys], 1)
+    route_b = along(packed, "seq", [(i, i + (3 if i % 2 == 0 else 1)) for i in range(n_seq)])
+    route_a = along(packed, "seq", [(i, i + (1 if i % 2 == 0 else 3)) for i in range(n_seq)])
+    route_c = along(route_b, "seq", [(i, i ^ 1) for i in range(n_seq)])
+    blocks = (packed, route_a, route_b, route_c)
+
+    high = lax.reduce_precision(index_weights, 8, 7)
+    middle = lax.reduce_precision(index_weights - high, 8, 7)
+    low = index_weights - high - middle
+    tail = jnp.concatenate([high, middle, low, jnp.zeros((rows, 128 - 3 * count), f32)], 1)
+    rows_packed = jnp.concatenate([index_query, tail.astype(bf16)], 1)
+
+    def exchanged(x, d):
+        return along(x, "head", [(i, i ^ d) for i in range(GROUPS)])
+
+    mine = [lax.dynamic_slice_in_dim(rows_packed, (z ^ d) * share, share, 0) for d in range(GROUPS)]
+    pieces = [mine[0]] + [exchanged(mine[d], d) for d in range(1, GROUPS)]
+
+    qpos = query_pos.reshape(rows, 1)
+    kpos = key_pos.reshape(1, kb)
+    outside = index_outside.reshape(rows, 1)
+
+    per_step = 8
+    mass = pl.pallas_call(
+        functools.partial(main_kernel, per_step),
+        grid=(heads // per_step,),
+        in_specs=[SMEM, pl.BlockSpec((rows, per_step * LAT), lambda i: (0, i))]
+        + [whole(x) for x in blocks]
+        + [whole(main_outside), whole(qpos), whole(kpos)],
+        out_specs=[pl.BlockSpec((share, window), lambda i: (0, 0))] * GROUPS,
+        out_shape=[jax.ShapeDtypeStruct((share, window), f32)] * GROUPS,
+        scratch_shapes=[
+            pltpu.VMEM((window, 640), bf16),
+            pltpu.VMEM((window, 640), bf16),
+            pltpu.VMEM((2, per_step * rows, window), f32),
+            pltpu.VMEM((2, per_step * rows, 128), f32),
+            pltpu.VMEM((rows, 128), f32),
+            pltpu.VMEM((rows, window), f32),
+        ],
+        compiler_params=params(48),
+        name="main_mass",
+    )(place, main_query, *blocks, main_outside, qpos, kpos)
+    masses = [mass[0]] + [exchanged(mass[d], d) for d in range(1, GROUPS)]
+
+    tile = count * share
+    key_spec = pl.BlockSpec((kb, IDIM), lambda i: (0, PACK // IDIM - 1))
+    piece_shape = (share, IDIM * count + 128)
+    score, gate, turned = pl.pallas_call(
+        functools.partial(index_kernel, count),
+        grid=(GROUPS,),
+        in_specs=[SMEM] + [key_spec] * 4 + [whole(x) for x in pieces],
+        out_specs=[
+            pl.BlockSpec((share, window), lambda i: (0, 0)),
+            pl.BlockSpec((tile, window), lambda i: (i, 0)),
+            pl.BlockSpec((2 * IDIM, tile), lambda i: (0, i)),
+        ],
+        out_shape=[
+            jax.ShapeDtypeStruct((share, window), f32),
+            jax.ShapeDtypeStruct((GROUPS * tile, window), bf16),
+            jax.ShapeDtypeStruct((2 * IDIM, GROUPS * tile), bf16),
+        ],
+        scratch_shapes=[pltpu.VMEM((window, IDIM), bf16), pltpu.VMEM((GROUPS,) + piece_shape, bf16)],
+        compiler_params=params(32),
+        name="index_scores",
+    )(place, *blocks, *pieces)
+
+    *back, spread = pl.pallas_call(
+        functools.partial(query_kernel, count),
+        grid=(GROUPS,),
+        in_specs=[SMEM] + [key_spec] * 4 + [whole(x) for x in masses]
+        + [whole(score), whole(outside), whole(qpos), whole(kpos)]
+        + [pl.BlockSpec((tile, window), lambda i: (i, 0))]
+        + [whole(x) for x in pieces],
+        out_specs=[pl.BlockSpec(piece_shape, lambda i: (0, 0))] * GROUPS
+        + [pl.BlockSpec((2, share, window), lambda i: (0, 0, 0))],
+        out_shape=[jax.ShapeDtypeStruct(piece_shape, bf16)] * GROUPS
+        + [jax.ShapeDtypeStruct((2, share, window), bf16)],
+        scratch_shapes=[
+            pltpu.VMEM((window, IDIM), bf16),
+            pltpu.VMEM((GROUPS,) + piece_shape, bf16),
+            pltpu.VMEM((GROUPS,) + piece_shape, bf16),
+        ],
+        compiler_params=params(32),
+        name="query_grads",
+    )(place, *blocks, *masses, score, outside, qpos, kpos, gate, *pieces)
+    returned = [back[0]] + [exchanged(back[d], d) for d in range(1, GROUPS)]
+
+    parts = pl.pallas_call(
+        functools.partial(keys_kernel, count),
+        grid=(GROUPS,),
+        in_specs=[
+            pl.BlockSpec((tile, window), lambda i: (i, 0)),
+            pl.BlockSpec((2 * IDIM, tile), lambda i: (0, i)),
+            whole(spread),
+        ],
+        out_specs=[pl.BlockSpec((kb, IDIM), lambda i: (0, 0))] * STEPS,
+        out_shape=[jax.ShapeDtypeStruct((kb, IDIM), f32)] * STEPS,
+        scratch_shapes=[pltpu.VMEM((IDIM, window), f32)],
+        compiler_params=params(32),
+        name="key_grads",
+    )(gate, turned, spread)
+    owned = parts[STEPS - 1]
+    for distance in range(1, STEPS):
+        owned = owned + along(parts[STEPS - 1 - distance], "seq", [(i, i - distance) for i in range(n_seq)])
+    others = [exchanged(owned, d) for d in range(1, GROUPS)]
+    grad_keys = (owned + others[0]) + (others[1] + others[2])
+
+    grad_query, grad_weight = pl.pallas_call(
+        functools.partial(place_kernel, count),
+        grid=(1,),
+        in_specs=[SMEM] + [whole(x) for x in returned],
+        out_specs=[
+            pl.BlockSpec((rows, IDIM * count), lambda i: (0, 0)),
+            pl.BlockSpec((rows, count), lambda i: (0, 0)),
+        ],
+        out_shape=[
+            jax.ShapeDtypeStruct((rows, IDIM * count), bf16),
+            jax.ShapeDtypeStruct((rows, count), f32),
+        ],
+        compiler_params=params(32),
+        name="place_grads",
+    )(place, *returned)
+    return (grad_query, grad_weight, grad_keys)
+
+
+def any_shards(main_query, latent, main_outside, index_query, index_weights, index_keys, *rest):
+    args = (main_query, latent, main_outside, index_query, index_weights, index_keys, *rest)
+    fits = (
+        lax.axis_size("head") == GROUPS
+        and lax.axis_size("seq") % 2 == 0
+        and main_query.shape[0] % (32 * GROUPS) == 0
+        and main_outside.shape[1] % 8 == 0
+        and latent.shape[0] % 256 == 0
+        and latent.shape[1] == LAT
+        and 3 * index_weights.shape[1] <= 128
+    )
+    return shards(*args) if fits else plain_shards(*args)
+
+
 def solution(mesh):
     in_specs = (
         P("seq", "head"),
@@ -123,4 +555,4 @@
         P("seq"),
     )
     out_specs = (P("seq", "head"), P("seq", "head"), P("seq", None))
-    return jax.shard_map(shards, mesh=mesh, in_specs=in_specs, out_specs=out_specs, check_vma=False)
+    return jax.shard_map(any_shards, mesh=mesh, in_specs=in_specs, out_specs=out_specs, check_vma=False)

time: 176 us -> 119 us (0.68)
  the two profiles are of different devices: /device:TPU:0 before, /device:TPU:7 now
where the time goes in v1:
time: 119 us
  Pallas kernels  48 us (40%)
  waiting for transfers between devices  33.2 us (28%)
  starting transfers between devices  26.9 us (23%)
  local copies, waits for them, and re-layouts  7.19 us (6%)
  other arithmetic  2.43 us (2%)
    pallas_call x1, Pallas kernels, shards(): pl.pallas_call(functools.partial(main_kernel, per_step), grid=(heads // p...  35.9 us
    ppermute x18, waiting for transfers between devices, along(): lax.ppermute(x, axis, [(i, j) for i, j in route if 0 <= j < lax.axis_size...  33.2 us
    ppermute x18, starting transfers between devices, along(): lax.ppermute(x, axis, [(i, j) for i, j in route if 0 <= j < lax.axis_size...  26.9 us
    pallas_call x1, Pallas kernels, shards(): pl.pallas_call(functools.partial(query_kernel, count), grid=(GROUPS,), in...  4.69 us
    unnamed x10, local copies, waits for them, and re-layouts  4.12 us
    pallas_call x1, Pallas kernels, shards(): pl.pallas_call(functools.partial(index_kernel, count), grid=(GROUPS,), in...  3.22 us
    pallas_call x1, Pallas kernels, shards(): pl.pallas_call(functools.partial(keys_kernel, count), grid=(GROUPS,), in_...  2.72 us
  transfers between devices with their start and end apart: 18, of which 5 were waited for; matrix products, arithmetic and copies ran while one was open for 5% of the time, Pallas kernels for 34%

profile of v1, /device:TPU:7, one launch (start us, length us, event | category | flops | bytes accessed | tf_op | source)
XLA Modules:
  0.0 118.5 jit_solution(10240899779393517723)
XLA Ops:
  0.6 1.2 copy.20
  1.8 0.1 pad.1.clone
  1.9 0.9 pad_maximum_fusion.own
  2.8 0.0 copy-start.2
  2.8 1.3 %collective-permute-start.1 = (bf16[256,768]{1,0:T(8,128)(2,1)S(1)}, bf16[256,768]{1,0:T(8,128)(2,1)S(1)}, u32[]{:S(2)}, u32[]{:S(2)}) collective-permute-start(bf16[256,768]{1,0:T(8,128)(2,1)S(1)} %pad_maximum_fusion.own), channel_id=1, source_target_pairs={{0,12},{4,8},{8,20},{12,16},{16,28},{20,24},{1,13},{5,9},{9,21},{1... | collective-permute-start | bytes 1179656 | tf_op jit(solution)/shard_map/ppermute | solution.py:381
  4.1 1.3 %collective-permute-start = (bf16[256,768]{1,0:T(8,128)(2,1)S(1)}, bf16[256,768]{1,0:T(8,128)(2,1)S(1)}, u32[]{:S(2)}, u32[]{:S(2)}) collective-permute-start(bf16[256,768]{1,0:T(8,128)(2,1)S(1)} %pad_maximum_fusion.own), channel_id=1, source_target_pairs={{0,4},{4,16},{8,12},{12,24},{16,20},{24,28},{1,5},{5,17},{9,13},{1... | collective-permute-start | bytes 1179656 | tf_op jit(solution)/shard_map/ppermute | solution.py:381
  5.4 0.8 copy.23
  6.2 0.7 fusion.1
  6.9 0.1 copy.25
  7.1 0.1 copy.24
  7.2 1.2 concatenate.10
  8.4 0.0 copy-start.1
  8.4 8.0 %collective-permute-done.1.b = bf16[256,768]{1,0:T(8,128)(2,1)S(1)} collective-permute-done((bf16[256,768]{1,0:T(8,128)(2,1)S(1)}, bf16[256,768]{1,0:T(8,128)(2,1)S(1)}, u32[]{:S(2)}, u32[]{:S(2)}) %collective-permute-start.1) | collective-permute-done | bytes 393248 | tf_op jit(solution)/shard_map/ppermute | solution.py:381
  16.4 0.4 collective-permute-start.2
  16.8 0.7 constant_dynamic-slice_fusion
  17.5 3.3 %collective-permute-start.8 = (bf16[32,2176]{1,0:T(8,128)(2,1)}, bf16[32,2176]{1,0:T(8,128)(2,1)S(1)}, u32[]{:S(2)}, u32[]{:S(2)}) collective-permute-start(bf16[32,2176]{1,0:T(8,128)(2,1)} %get-tuple-element.45), channel_id=1, source_target_pairs={{0,3},{1,2},{2,1},{3,0},{4,7},{5,6},{6,5},{7,4},{8,11},{9,10},{10,... | collective-permute-start | bytes 417800 | tf_op jit(solution)/shard_map/ppermute | solution.py:381
  20.8 0.0 collective-permute-start.7
  20.8 0.3 collective-permute-start.6
  21.1 0.1 pad_add_fusion.place
  21.2 0.8 copy.22.qpos
  21.9 0.8 copy.21.outside
  22.7 0.0 collective-permute-done.2.c
  22.8 0.0 copy-start
  22.8 0.7 copy-done
  23.4 35.9 %main_mass.1 = (f32[32,1024]{1,0:T(8,128)S(1)}, f32[32,1024]{1,0:T(8,128)S(1)}, f32[32,1024]{1,0:T(8,128)S(1)}, f32[32,1024]{1,0:T(8,128)S(1)}) custom-call(s32[2]{0:T(128)S(1)} %pad_add_fusion.place, bf16[128,18432]{1,0:T(8,128)(2,1)} %q.1, bf16[256,768]{1,0:T(8,128)(2,1)S(1)} %pad_maximum_fusion.own, bf16[256,768]{1,0:T(8,128)(2,1)S(1)} %collective-permute-done.a, ...), custom_call_target="tpu_custom_call" | custom-call | tf_op jit(solution)/shard_map/main_mass/pallas_call | solution.py:429
  59.4 1.3 %collective-permute-start.3 = (f32[32,1024]{1,0:T(8,128)S(1)}, f32[32,1024]{1,0:T(8,128)S(1)}, u32[]{:S(2)}, u32[]{:S(2)}) collective-permute-start(f32[32,1024]{1,0:T(8,128)S(1)} %get-tuple-element.22), channel_id=1, source_target_pairs={{0,1},{1,0},{2,3},{3,2},{4,5},{5,4},{6,7},{7,6},{8,9},{9,8},{10,11... | collective-permute-start | bytes 393224 | tf_op jit(solution)/shard_map/ppermute | solution.py:381
  60.6 2.4 %collective-permute-start.4 = (f32[32,1024]{1,0:T(8,128)S(1)}, f32[32,1024]{1,0:T(8,128)S(1)}, u32[]{:S(2)}, u32[]{:S(2)}) collective-permute-start(f32[32,1024]{1,0:T(8,128)S(1)} %get-tuple-element.23), channel_id=1, source_target_pairs={{0,2},{1,3},{2,0},{3,1},{4,6},{5,7},{6,4},{7,5},{8,10},{9,11},{10,... | collective-permute-start | bytes 393224 | tf_op jit(solution)/shard_map/ppermute | solution.py:381
  63.0 0.0 collective-permute-done.8.rest_3_
  63.0 0.1 copy.26.outside
  63.1 0.0 collective-permute-done.7.rest_2_
  63.1 3.2 %index_scores.1 = (f32[32,1024]{1,0:T(8,128)S(1)}, bf16[2048,1024]{1,0:T(8,128)(2,1)S(1)}, bf16[256,2048]{1,0:T(8,128)(2,1)S(1)}) custom-call(s32[2]{0:T(128)S(1)} %pad_add_fusion.place, bf16[256,768]{1,0:T(8,128)(2,1)S(1)} %pad_maximum_fusion.own, bf16[256,768]{1,0:T(8,128)(2,1)S(1)} %collective-permute-done.a, ...), custom_call_target="tpu_custom_call" | custom-call | tf_op jit(solution)/shard_map/index_scores/pallas_call | solution.py:453
  66.4 0.0 collective-permute-done.4.m2
  66.4 4.9 %collective-permute-done.5.m3 = f32[32,1024]{1,0:T(8,128)S(1)} collective-permute-done((f32[32,1024]{1,0:T(8,128)S(1)}, f32[32,1024]{1,0:T(8,128)S(1)}, u32[]{:S(2)}, u32[]{:S(2)}) %collective-permute-start.5) | collective-permute-done | bytes 131104 | tf_op jit(solution)/shard_map/ppermute | solution.py:381
  71.3 4.7 %query_grads.1 = (bf16[32,2176]{1,0:T(8,128)(2,1)S(1)}, bf16[32,2176]{1,0:T(8,128)(2,1)S(1)}, bf16[32,2176]{1,0:T(8,128)(2,1)S(1)}, bf16[32,2176]{1,0:T(8,128)(2,1)S(1)}, bf16[2,32,1024]{2,1,0:T(8,128)(2,1)S(1)}) custom-call(s32[2]{0:T(128)S(1)} %pad_add_fusion.place, bf16[256,768]{1,0:T(8,128)(2,1)S(1)} %pad_maximum_fusion.own, ...), custom_call_target="tpu_custom_call" | custom-call | tf_op jit(solution)/shard_map/query_grads/pallas_call | solution.py:472
  76.0 2.7 %key_grads.1 = (f32[256,128]{1,0:T(8,128)S(1)}, f32[256,128]{1,0:T(8,128)S(1)}, f32[256,128]{1,0:T(8,128)S(1)}, f32[256,128]{1,0:T(8,128)S(1)}) custom-call(bf16[2048,1024]{1,0:T(8,128)(2,1)S(1)} %get-tuple-element.26.gate, bf16[256,2048]{1,0:T(8,128)(2,1)S(1)} %get-tuple-element.33.turned, bf16[2,32,1024]{2,1,0:T(8,128)(2,1)S(1)} %get-tuple-element.34.spread), custom_call_target="tpu_custom_call" | custom-call | tf_op jit(solution)/shard_map/key_grads/pallas_call | solution.py:493
  78.7 5.2 %collective-permute-start.12 = (f32[256,128]{1,0:T(8,128)S(1)}, f32[256,128]{1,0:T(8,128)S(1)}, u32[]{:S(2)}, u32[]{:S(2)}) collective-permute-start(f32[256,128]{1,0:T(8,128)S(1)} %get-tuple-element.36), channel_id=1, source_target_pairs={{4,0},{8,4},{12,8},{16,12},{20,16},{24,20},{28,24},{5,1},{9,5},{13... | collective-permute-start | bytes 393224 | tf_op jit(solution)/shard_map/ppermute | solution.py:381
  83.9 3.1 %collective-permute-start.13 = (f32[256,128]{1,0:T(8,128)S(1)}, f32[256,128]{1,0:T(8,128)S(1)}, u32[]{:S(2)}, u32[]{:S(2)}) collective-permute-start(f32[256,128]{1,0:T(8,128)S(1)} %get-tuple-element.37), channel_id=1, source_target_pairs={{8,0},{12,4},{16,8},{20,12},{24,16},{28,20},{9,1},{13,5},{17,9},{2... | collective-permute-start | bytes 393224 | tf_op jit(solution)/shard_map/ppermute | solution.py:381
  87.0 2.3 %collective-permute-start.14 = (f32[256,128]{1,0:T(8,128)S(1)}, f32[256,128]{1,0:T(8,128)S(1)}, u32[]{:S(2)}, u32[]{:S(2)}) collective-permute-start(f32[256,128]{1,0:T(8,128)S(1)} %get-tuple-element.38), channel_id=1, source_target_pairs={{12,0},{16,4},{20,8},{24,12},{28,16},{13,1},{17,5},{21,9},{25,13},... | collective-permute-start | bytes 393224 | tf_op jit(solution)/shard_map/ppermute | solution.py:381
  89.3 1.8 %collective-permute-start.9 = (bf16[32,2176]{1,0:T(8,128)(2,1)S(1)}, bf16[32,2176]{1,0:T(8,128)(2,1)S(1)}, u32[]{:S(2)}, u32[]{:S(2)}) collective-permute-start(bf16[32,2176]{1,0:T(8,128)(2,1)S(1)} %get-tuple-element.28), channel_id=1, source_target_pairs={{0,1},{1,0},{2,3},{3,2},{4,5},{5,4},{6,7},{7,6},{8,9},{9,8},{10,11... | collective-permute-start | bytes 417800 | tf_op jit(solution)/shard_map/ppermute | solution.py:381
  91.0 1.1 collective-permute-start.10
  92.1 1.1 collective-permute-start.11
  93.3 2.2 %collective-permute-start.17 = (f32[256,128]{1,0:T(8,128)S(1)}, f32[256,128]{1,0:T(8,128)S(1)}, u32[]{:S(2)}, u32[]{:S(2)}) collective-permute-start(f32[256,128]{1,0:T(8,128)S(1)} %add_add_fusion.1), channel_id=1, source_target_pairs={{0,3},{1,2},{2,1},{3,0},{4,7},{5,6},{6,5},{7,4},{8,11},{9,10},{10,... | collective-permute-start | bytes 393224 | tf_op jit(solution)/shard_map/ppermute | solution.py:381
  95.5 1.8 %collective-permute-done.9.rest_1_ = bf16[32,2176]{1,0:T(8,128)(2,1)S(1)} collective-permute-done((bf16[32,2176]{1,0:T(8,128)(2,1)S(1)}, bf16[32,2176]{1,0:T(8,128)(2,1)S(1)}, u32[]{:S(2)}, u32[]{:S(2)}) %collective-permute-start.9) | collective-permute-done | bytes 139296 | tf_op jit(solution)/shard_map/ppermute | solution.py:381
  97.3 11.9 %collective-permute-done.10.rest_2_ = bf16[32,2176]{1,0:T(8,128)(2,1)S(1)} collective-permute-done((bf16[32,2176]{1,0:T(8,128)(2,1)S(1)}, bf16[32,2176]{1,0:T(8,128)(2,1)S(1)}, u32[]{:S(2)}, u32[]{:S(2)}) %collective-permute-start.10) | collective-permute-done | bytes 139296 | tf_op jit(solution)/shard_map/ppermute | solution.py:381
  109.2 1.4 %place_grads.1 = (bf16[128,2048]{1,0:T(8,128)(2,1)}, f32[128,16]{1,0:T(8,128)S(1)}) custom-call(s32[2]{0:T(128)S(1)} %pad_add_fusion.place, bf16[32,2176]{1,0:T(8,128)(2,1)S(1)} %get-tuple-element.27.rest_0_, bf16[32,2176]{1,0:T(8,128)(2,1)S(1)} %collective-permute-done.9.rest_1_, bf16[32,2176]{1,0:T(8,128)(2,1)S(1)} %collective-permute-done.10.rest_2_, ...), custom_call_target="tpu_custom_call" | custom-call | tf_op jit(solution)/shard_map/place_grads/pallas_call | solution.py:513
  110.6 0.7 copy.28
  111.3 6.5 %collective-permute-done.16 = f32[256,128]{1,0:T(8,128)S(1)} collective-permute-done((f32[256,128]{1,0:T(8,128)S(1)}, f32[256,128]{1,0:T(8,128)S(1)}, u32[]{:S(2)}, u32[]{:S(2)}) %collective-permute-start.16) | collective-permute-done | bytes 131104 | tf_op jit(solution)/shard_map/ppermute | solution.py:381
  117.8 0.7 add_add_fusion
  (18 shorter events, 0.1 us)
Async XLA Ops:
  2.8 60.2 %copy-start.2 = (f32[128]{0:T(128)S(1)}, f32[128]{0:T(128)}, u32[]{:S(2)}) copy-start(f32[128]{0:T(128)} %param.15) | copy-start | bytes 1540
  2.8 13.6 %collective-permute-start.1 = (bf16[256,768]{1,0:T(8,128)(2,1)S(1)}, bf16[256,768]{1,0:T(8,128)(2,1)S(1)}, u32[]{:S(2)}, u32[]{:S(2)}) collective-permute-start(bf16[256,768]{1,0:T(8,128)(2,1)S(1)} %pad_maximum_fusion.own), channel_id=1, source_target_pairs={{0,12},{4,8},{8,20},{12,16},{16,28},{20,24},{1,13},{5,9},{9,21},{1... | collective-permute-start | bytes 1179656 | tf_op jit(solution)/shard_map/ppermute | solution.py:381
  4.1 18.6 %collective-permute-start = (bf16[256,768]{1,0:T(8,128)(2,1)S(1)}, bf16[256,768]{1,0:T(8,128)(2,1)S(1)}, u32[]{:S(2)}, u32[]{:S(2)}) collective-permute-start(bf16[256,768]{1,0:T(8,128)(2,1)S(1)} %pad_maximum_fusion.own), channel_id=1, source_target_pairs={{0,4},{4,16},{8,12},{12,24},{16,20},{24,28},{1,5},{5,17},{9,13},{1... | collective-permute-start | bytes 1179656 | tf_op jit(solution)/shard_map/ppermute | solution.py:381
  8.4 62.9 %copy-start.1 = (s32[256]{0:T(256)S(1)}, s32[256]{0:T(256)}, u32[]{:S(2)}) copy-start(s32[256]{0:T(256)} %param.17) | copy-start | bytes 3076
  16.4 6.4 %collective-permute-start.2 = (bf16[256,768]{1,0:T(8,128)(2,1)S(1)}, bf16[256,768]{1,0:T(8,128)(2,1)S(1)}, u32[]{:S(2)}, u32[]{:S(2)}) collective-permute-start(bf16[256,768]{1,0:T(8,128)(2,1)S(1)} %collective-permute-done.1.b), channel_id=1, source_target_pairs={{0,4},{4,0},{8,12},{12,8},{16,20},{20,16},{24,28},{28,24},{1,5},{5... | collective-permute-start | bytes 1179656 | tf_op jit(solution)/shard_map/ppermute | solution.py:381
  17.5 45.5 %collective-permute-start.8 = (bf16[32,2176]{1,0:T(8,128)(2,1)}, bf16[32,2176]{1,0:T(8,128)(2,1)S(1)}, u32[]{:S(2)}, u32[]{:S(2)}) collective-permute-start(bf16[32,2176]{1,0:T(8,128)(2,1)} %get-tuple-element.45), channel_id=1, source_target_pairs={{0,3},{1,2},{2,1},{3,0},{4,7},{5,6},{6,5},{7,4},{8,11},{9,10},{10,... | collective-permute-start | bytes 417800 | tf_op jit(solution)/shard_map/ppermute | solution.py:381
  20.8 42.3 %collective-permute-start.7 = (bf16[32,2176]{1,0:T(8,128)(2,1)S(1)}, bf16[32,2176]{1,0:T(8,128)(2,1)S(1)}, u32[]{:S(2)}, u32[]{:S(2)}) collective-permute-start(bf16[32,2176]{1,0:T(8,128)(2,1)S(1)} %get-tuple-element.46), channel_id=1, source_target_pairs={{0,2},{1,3},{2,0},{3,1},{4,6},{5,7},{6,4},{7,5},{8,10},{9,11},{10,... | collective-permute-start | bytes 417800 | tf_op jit(solution)/shard_map/ppermute | solution.py:381
  20.8 42.3 %collective-permute-start.6 = (bf16[32,2176]{1,0:T(8,128)(2,1)S(1)}, bf16[32,2176]{1,0:T(8,128)(2,1)S(1)}, u32[]{:S(2)}, u32[]{:S(2)}) collective-permute-start(bf16[32,2176]{1,0:T(8,128)(2,1)S(1)} %get-tuple-element.47), channel_id=1, source_target_pairs={{0,1},{1,0},{2,3},{3,2},{4,5},{5,4},{6,7},{7,6},{8,9},{9,8},{10,11... | collective-permute-start | bytes 417800 | tf_op jit(solution)/shard_map/ppermute | solution.py:381
  22.8 0.7 copy-start
  59.4 7.0 %collective-permute-start.3 = (f32[32,1024]{1,0:T(8,128)S(1)}, f32[32,1024]{1,0:T(8,128)S(1)}, u32[]{:S(2)}, u32[]{:S(2)}) collective-permute-start(f32[32,1024]{1,0:T(8,128)S(1)} %get-tuple-element.22), channel_id=1, source_target_pairs={{0,1},{1,0},{2,3},{3,2},{4,5},{5,4},{6,7},{7,6},{8,9},{9,8},{10,11... | collective-permute-start | bytes 393224 | tf_op jit(solution)/shard_map/ppermute | solution.py:381
  60.6 5.7 %collective-permute-start.4 = (f32[32,1024]{1,0:T(8,128)S(1)}, f32[32,1024]{1,0:T(8,128)S(1)}, u32[]{:S(2)}, u32[]{:S(2)}) collective-permute-start(f32[32,1024]{1,0:T(8,128)S(1)} %get-tuple-element.23), channel_id=1, source_target_pairs={{0,2},{1,3},{2,0},{3,1},{4,6},{5,7},{6,4},{7,5},{8,10},{9,11},{10,... | collective-permute-start | bytes 393224 | tf_op jit(solution)/shard_map/ppermute | solution.py:381
  63.0 8.2 %collective-permute-start.5 = (f32[32,1024]{1,0:T(8,128)S(1)}, f32[32,1024]{1,0:T(8,128)S(1)}, u32[]{:S(2)}, u32[]{:S(2)}) collective-permute-start(f32[32,1024]{1,0:T(8,128)S(1)} %get-tuple-element.24), channel_id=1, source_target_pairs={{0,3},{1,2},{2,1},{3,0},{4,7},{5,6},{6,5},{7,4},{8,11},{9,10},{10,... | collective-permute-start | bytes 393224 | tf_op jit(solution)/shard_map/ppermute | solution.py:381
  78.7 13.4 %collective-permute-start.12 = (f32[256,128]{1,0:T(8,128)S(1)}, f32[256,128]{1,0:T(8,128)S(1)}, u32[]{:S(2)}, u32[]{:S(2)}) collective-permute-start(f32[256,128]{1,0:T(8,128)S(1)} %get-tuple-element.36), channel_id=1, source_target_pairs={{4,0},{8,4},{12,8},{16,12},{20,16},{24,20},{28,24},{5,1},{9,5},{13... | collective-permute-start | bytes 393224 | tf_op jit(solution)/shard_map/ppermute | solution.py:381
  83.9 9.3 %collective-permute-start.13 = (f32[256,128]{1,0:T(8,128)S(1)}, f32[256,128]{1,0:T(8,128)S(1)}, u32[]{:S(2)}, u32[]{:S(2)}) collective-permute-start(f32[256,128]{1,0:T(8,128)S(1)} %get-tuple-element.37), channel_id=1, source_target_pairs={{8,0},{12,4},{16,8},{20,12},{24,16},{28,20},{9,1},{13,5},{17,9},{2... | collective-permute-start | bytes 393224 | tf_op jit(solution)/shard_map/ppermute | solution.py:381
  87.0 6.2 %collective-permute-start.14 = (f32[256,128]{1,0:T(8,128)S(1)}, f32[256,128]{1,0:T(8,128)S(1)}, u32[]{:S(2)}, u32[]{:S(2)}) collective-permute-start(f32[256,128]{1,0:T(8,128)S(1)} %get-tuple-element.38), channel_id=1, source_target_pairs={{12,0},{16,4},{20,8},{24,12},{28,16},{13,1},{17,5},{21,9},{25,13},... | collective-permute-start | bytes 393224 | tf_op jit(solution)/shard_map/ppermute | solution.py:381
  89.3 8.0 %collective-permute-start.9 = (bf16[32,2176]{1,0:T(8,128)(2,1)S(1)}, bf16[32,2176]{1,0:T(8,128)(2,1)S(1)}, u32[]{:S(2)}, u32[]{:S(2)}) collective-permute-start(bf16[32,2176]{1,0:T(8,128)(2,1)S(1)} %get-tuple-element.28), channel_id=1, source_target_pairs={{0,1},{1,0},{2,3},{3,2},{4,5},{5,4},{6,7},{7,6},{8,9},{9,8},{10,11... | collective-permute-start | bytes 417800 | tf_op jit(solution)/shard_map/ppermute | solution.py:381
  91.0 18.2 %collective-permute-start.10 = (bf16[32,2176]{1,0:T(8,128)(2,1)S(1)}, bf16[32,2176]{1,0:T(8,128)(2,1)S(1)}, u32[]{:S(2)}, u32[]{:S(2)}) collective-permute-start(bf16[32,2176]{1,0:T(8,128)(2,1)S(1)} %get-tuple-element.29), channel_id=1, source_target_pairs={{0,2},{1,3},{2,0},{3,1},{4,6},{5,7},{6,4},{7,5},{8,10},{9,11},{10,... | collective-permute-start | bytes 417800 | tf_op jit(solution)/shard_map/ppermute | solution.py:381
  92.1 17.1 %collective-permute-start.11 = (bf16[32,2176]{1,0:T(8,128)(2,1)S(1)}, bf16[32,2176]{1,0:T(8,128)(2,1)S(1)}, u32[]{:S(2)}, u32[]{:S(2)}) collective-permute-start(bf16[32,2176]{1,0:T(8,128)(2,1)S(1)} %get-tuple-element.30), channel_id=1, source_target_pairs={{0,3},{1,2},{2,1},{3,0},{4,7},{5,6},{6,5},{7,4},{8,11},{9,10},{10,... | collective-permute-start | bytes 417800 | tf_op jit(solution)/shard_map/ppermute | solution.py:381
  93.3 18.0 %collective-permute-start.17 = (f32[256,128]{1,0:T(8,128)S(1)}, f32[256,128]{1,0:T(8,128)S(1)}, u32[]{:S(2)}, u32[]{:S(2)}) collective-permute-start(f32[256,128]{1,0:T(8,128)S(1)} %add_add_fusion.1), channel_id=1, source_target_pairs={{0,3},{1,2},{2,1},{3,0},{4,7},{5,6},{6,5},{7,4},{8,11},{9,10},{10,... | collective-permute-start | bytes 393224 | tf_op jit(solution)/shard_map/ppermute | solution.py:381
  95.5 22.3 %collective-permute-start.16 = (f32[256,128]{1,0:T(8,128)S(1)}, f32[256,128]{1,0:T(8,128)S(1)}, u32[]{:S(2)}, u32[]{:S(2)}) collective-permute-start(f32[256,128]{1,0:T(8,128)S(1)} %add_add_fusion.1), channel_id=1, source_target_pairs={{0,2},{1,3},{2,0},{3,1},{4,6},{5,7},{6,4},{7,5},{8,10},{9,11},{10,... | collective-permute-start | bytes 393224 | tf_op jit(solution)/shard_map/ppermute | solution.py:381
  97.3 20.6 %collective-permute-start.15 = (f32[256,128]{1,0:T(8,128)S(1)}, f32[256,128]{1,0:T(8,128)S(1)}, u32[]{:S(2)}, u32[]{:S(2)}) collective-permute-start(f32[256,128]{1,0:T(8,128)S(1)} %add_add_fusion.1), channel_id=1, source_target_pairs={{0,1},{1,0},{2,3},{3,2},{4,5},{5,4},{6,7},{7,6},{8,9},{9,8},{10,11... | collective-permute-start | bytes 393224 | tf_op jit(solution)/shard_map/ppermute | solution.py:381

commit v2 on v0

--- a/solution.py
+++ b/solution.py
@@ -1,6 +1,10 @@
+import functools
+
 import jax
 import jax.numpy as jnp
 from jax import lax
+from jax.experimental import pallas as pl
+from jax.experimental.pallas import tpu as pltpu
 from jax.sharding import PartitionSpec as P
 
 IDIM = 128
@@ -35,7 +39,7 @@
     return (expo / total[:, None] - target) * (STEPS * KB)
 
 
-def shards(
+def plain_shards(
     main_query,
     latent,
     main_outside,
@@ -110,6 +114,614 @@
     return (grad_query, grad_weight, grad_keys)
 
 
+LOG2E = 1.4426950408889634
+LAT = 576
+GROUPS = 4
+BUFFERS = 4
+PER_STEP = 8
+SAFE = 1e30
+LEVELS = 32000.0
+NN = (((1,), (0,)), ((), ()))
+NT = (((1,), (1,)), ((), ()))
+
+
+def dot(a, b, dims=NN):
+    return lax.dot_general(a, b, dims, preferred_element_type=jnp.float32)
+
+
+def split(x):
+    high = x.astype(jnp.bfloat16)
+    return high, (x - high.astype(jnp.float32)).astype(jnp.bfloat16)
+
+
+def coded(x, axis):
+    top = jnp.max(jnp.abs(x), axis=axis, keepdims=True)
+    power = jnp.ceil(8.0 * jnp.log2(jnp.maximum(top, 1e-30)))
+    code = jnp.floor(x * (LEVELS * jnp.exp2(power * -0.125)) + 0.5)
+    return code.astype(jnp.int32).astype(jnp.int16), power.astype(jnp.int32).astype(jnp.int16)
+
+
+def scale_of(power):
+    return jnp.exp2(power.astype(jnp.float32) * 0.125) * (1.0 / LEVELS)
+
+
+def coded_rows(ref, x):
+    code, power = coded(x, 1)
+    ref[:, :x.shape[1]] = code
+    ref[:, x.shape[1]:] = jnp.broadcast_to(power.astype(jnp.int32), (x.shape[0], 128)).astype(jnp.int16)
+
+
+def restored_rows(ref, window):
+    return ref[:, :window].astype(jnp.float32) * scale_of(ref[:, window:])[:, :1]
+
+
+def coded_columns(ref, x):
+    code, power = coded(x, 0)
+    ref[:x.shape[0], :] = code
+    ref[x.shape[0]:, :] = jnp.broadcast_to(power.astype(jnp.int32), (16, x.shape[1])).astype(jnp.int16)
+
+
+def restored_columns(ref, count):
+    return ref[:count, :].astype(jnp.float32) * scale_of(ref[count:, :])[:1, :]
+
+
+def column(row, first, count):
+    lane = lax.broadcasted_iota(jnp.int32, (count, 128), 1)
+    line = lax.broadcasted_iota(jnp.int32, (count, 128), 0) + first
+    wide = jnp.broadcast_to(row.astype(jnp.float32), (count, 128))
+    return jnp.sum(jnp.where(lane == line, wide, 0.0), axis=1, keepdims=True)
+
+
+def turned_tall(x, value=0.0):
+    fill = jnp.full((128 - x.shape[0], 128), value, jnp.float32)
+    return jnp.concatenate([x, fill], 0).T
+
+
+def slots_of(position):
+    even = lax.rem(position, 2) == 0
+    return 3, jnp.where(even, 0, 2), jnp.where(even, 2, 0), 1
+
+
+def gathered(position, blocks, kept, first):
+    kb = blocks[0].shape[1]
+    for block, slot in zip(blocks, slots_of(position)):
+        at = pl.ds(pl.multiple_of(slot * kb, kb), kb)
+        kept[first:first + block.shape[0], at] = block[...]
+
+
+def heads_at(q, parity):
+    starts = [1152 * i + 512 * parity for i in range(q.shape[1] // 1152)]
+    return jnp.concatenate([q[:, s:s + 640] for s in starts], 0)
+
+
+def pack_kernel(place, latent, keys, query, weight, packed, *rest):
+    outs, (kept, keys_here, weight_here, sems) = rest[:GROUPS], rest[GROUPS:]
+    share = outs[0].shape[0]
+    width, count = query.shape[1], weight.shape[0]
+    copies = [
+        pltpu.make_async_copy(latent, packed.at[pl.ds(0, LAT), :], sems.at[0]),
+        pltpu.make_async_copy(keys, keys_here, sems.at[1]),
+        pltpu.make_async_copy(weight, weight_here, sems.at[2]),
+    ]
+    for d in range(GROUPS):
+        at = pl.ds(pl.multiple_of((place[0] ^ d) * share, share), share)
+        here = outs[d].at[:, pl.ds(0, width)]
+        copies.append(pltpu.make_async_copy(query.at[at, :], here, sems.at[3 + d]))
+    for copy in copies:
+        copy.start()
+    copies[1].wait()
+    packed[LAT:, :] = keys_here[...].T
+    copies[2].wait()
+    tall = turned_tall(weight_here[...])[:, :count]
+    high = tall.astype(jnp.bfloat16)
+    middle, low = split(tall - high.astype(jnp.float32))
+    kept[...] = jnp.concatenate([high, middle, low, jnp.zeros((128, 128 - 3 * count), jnp.bfloat16)], 1)
+    for d in range(GROUPS):
+        at = pl.ds(pl.multiple_of((place[0] ^ d) * share, share), share)
+        outs[d][:, width:] = kept[at, :]
+    copies[0].wait()
+    for copy in copies[3:]:
+        copy.wait()
+
+
+def weights_of(piece, width, count):
+    tail = piece[:, width:].astype(jnp.float32)
+    return tail[:, :count] + tail[:, count:2 * count] + tail[:, 2 * count:3 * count]
+
+
+def chunk_rows(q, j, half):
+    parity, pair = j % 2, half * (j // 2)
+    starts = [1152 * (pair + i) + 512 * parity for i in range(half)]
+    return jnp.concatenate([q[:, s:s + 640] for s in starts], 0), 64 - 64 * parity
+
+
+def own_kernel(half, q, own, qpos, kpos, out, keys, here, places, sems):
+    rows, kb = q.shape[0], own.shape[1]
+    chunks = q.shape[1] // (half * LAT)
+    parts = chunks // 2
+    copies = [
+        pltpu.make_async_copy(qpos, places.at[0:1, pl.ds(0, rows)], sems.at[parts]),
+        pltpu.make_async_copy(kpos, places.at[1:2, :], sems.at[parts + 1]),
+    ]
+    for i in range(parts):
+        lanes = pl.ds(i * 2 * half * LAT, 2 * half * LAT)
+        copies.append(pltpu.make_async_copy(q.at[:, lanes], here.at[:, lanes], sems.at[i]))
+    for copy in copies:
+        copy.start()
+    keys[:64, :] = jnp.zeros((64, kb), jnp.bfloat16)
+    keys[64:64 + LAT, :] = own[:LAT, :]
+    keys[64 + LAT:, :] = jnp.zeros((64, kb), jnp.bfloat16)
+    copies[0].wait()
+    copies[1].wait()
+    causal = places[1:2, :].astype(jnp.float32) <= column(places[0:1, :rows], 0, rows)
+    for j in range(chunks):
+        if j % 2 == 0:
+            copies[2 + j // 2].wait()
+        lhs, first = chunk_rows(here, j, half)
+        s = dot(lhs, keys[first:first + 640, :])
+        for i in range(half):
+            ex = jnp.exp2(s[i * rows:(i + 1) * rows] * (SCORE_SCALE * LOG2E))
+            at = (j * half + i) * rows
+            out[at:at + rows, :] = jnp.where(causal, ex, 0.0)
+
+
+def main_kernel(half, place, q, own, a, b, c, own_exp, outside, qpos, kpos, *rest):
+    outs, rest = rest[:GROUPS], rest[GROUPS:]
+    e, inv, (keys, out_exp, mass) = rest[:BUFFERS], rest[BUFFERS:2 * BUFFERS], rest[2 * BUFFERS:]
+    z, position = place[0], place[1]
+    rows, kb = q.shape[0], own.shape[1]
+    chunks = q.shape[1] // (half * LAT)
+    window = STEPS * kb
+    front = window - kb
+    present = [jnp.where(position >= STEPS - 1 - i, 1.0, 0.0).astype(jnp.float32) for i in range(STEPS)]
+    lane = lax.broadcasted_iota(jnp.int32, (32, 128), 1)
+
+    keys[:64, :] = jnp.zeros((64, window), jnp.bfloat16)
+    keys[64 + LAT:, :] = jnp.zeros((64, window), jnp.bfloat16)
+    for block, slot in zip((own, a, b, c), slots_of(position)):
+        keys[64:64 + LAT, pl.ds(pl.multiple_of(slot * kb, kb), kb)] = block[:LAT, :]
+    out_exp[...] = jnp.exp(turned_tall(outside[...], NEGATIVE))
+    mass[...] = jnp.zeros_like(mass)
+    worst = [jnp.zeros((32, 1), jnp.float32)]
+
+    def exp_unit(j, i, r):
+        buffer, at = j % BUFFERS, i * rows + r
+        own_rows = slice(j * half * rows + at, j * half * rows + at + 32)
+        head = (j - j % 2) * half + 2 * i + j % 2
+        total = jnp.where(lane == head, out_exp[r:r + 32, :], 0.0)
+        for block in range(STEPS):
+            piece = own_exp[own_rows, :] if block == STEPS - 1 else e[buffer][at:at + 32, block * kb:(block + 1) * kb]
+            sums = piece[:, :128]
+            for k in range(128, kb, 128):
+                sums = sums + piece[:, k:k + 128]
+            total = total + (sums if block == STEPS - 1 else sums * present[block])
+        total = jnp.sum(total, axis=1, keepdims=True)
+        inv[buffer][at:at + 32, :] = jnp.broadcast_to(1.0 / total, (32, 128))
+        worst[0] = jnp.maximum(worst[0], total)
+
+    def mass_unit(j, r, w):
+        buffer = j % BUFFERS
+        total = mass[r:r + 32, w:w + 256]
+        for i in range(half):
+            at = i * rows + r
+            if w < front:
+                piece = e[buffer][at:at + 32, w:w + 256]
+            else:
+                first = j * half * rows + at
+                piece = own_exp[first:first + 32, w - front:w - front + 256]
+            scale = inv[buffer][at:at + 32, :]
+            total = total + piece * jnp.concatenate([scale, scale], 1)
+        mass[r:r + 32, w:w + 256] = total
+
+    exps = [(i, r) for i in range(half) for r in range(0, rows, 32)]
+    sums = [(r, w) for r in range(0, rows, 32) for w in range(0, window, 256)]
+    thirds = STEPS - 1
+    for j in range(chunks + 2):
+        if j < chunks:
+            lhs, first = chunk_rows(q, j, half)
+        for n in range(thirds):
+            if j < chunks:
+                lanes = slice(n * kb, (n + 1) * kb)
+                s = dot(lhs, keys[first:first + 640, lanes])
+                e[j % BUFFERS][:, lanes] = jnp.exp2(s * (SCORE_SCALE * LOG2E))
+            if 1 <= j <= chunks:
+                for i, r in exps[n * len(exps) // thirds:(n + 1) * len(exps) // thirds]:
+                    exp_unit(j - 1, i, r)
+            if j >= 2:
+                for r, w in sums[n * len(sums) // thirds:(n + 1) * len(sums) // thirds]:
+                    mass_unit(j - 2, r, w)
+
+    @pl.when(jnp.logical_not(jnp.max(worst[0]) < SAFE))
+    def _():
+        slot = lax.broadcasted_iota(jnp.int32, (rows, window), 1) // kb
+        causal = kpos[...].astype(jnp.float32) <= column(qpos[...], 0, rows)
+        causal = jnp.concatenate([jnp.ones((rows, front), jnp.float32), jnp.where(causal, 1.0, 0.0)], 1) > 0
+        visible = (position >= STEPS - 1 - slot) & causal
+        line = lax.broadcasted_iota(jnp.int32, outside.shape, 0)
+        mass[...] = jnp.zeros_like(mass)
+        for parity in range(2):
+
+            def exact(i, carry, parity=parity):
+                first = 64 - 64 * parity
+                at = pl.multiple_of(1152 * i + 512 * parity, 128)
+                scores = dot(q[:, pl.ds(at, 640)], keys[first:first + 640, :]) * SCORE_SCALE
+                masked = jnp.where(visible, scores, NEGATIVE)
+                mine = jnp.sum(jnp.where(line == 2 * i + parity, outside[...], 0.0), axis=0, keepdims=True)
+                mine = column(mine, 0, rows)
+                top = jnp.maximum(jnp.max(masked, axis=1, keepdims=True), mine)
+                ex = jnp.exp(masked - top)
+                total = jnp.sum(ex, axis=1, keepdims=True) + jnp.exp(mine - top)
+                mass[...] += ex * (1.0 / total)
+                return carry
+
+            lax.fori_loop(0, outside.shape[0] // 2, exact, 0)
+
+    for block in range(STEPS - 1):
+        lanes = slice(block * kb, (block + 1) * kb)
+        mass[:, lanes] = mass[:, lanes] * present[block]
+    share = rows // GROUPS
+    for d in range(GROUPS):
+        at = pl.ds(pl.multiple_of((z ^ d) * share, share), share)
+        if d == 0:
+            outs[d][...] = mass[at, :]
+        else:
+            coded_rows(outs[d], mass[at, :])
+
+
+def heads_of(piece, count):
+    return jnp.concatenate([piece[:, IDIM * j:IDIM * (j + 1)] for j in range(count)], 0)
+
+
+def index_kernel(count, place, own, a, b, c, *rest):
+    pieces, (score, gate, turned, keys) = rest[:GROUPS], rest[GROUPS:]
+    share = score.shape[0]
+    tile = count * share
+    gathered(place[1], (own, a, b, c), keys, 0)
+    total = jnp.zeros(score.shape, jnp.float32)
+    for d in range(GROUPS):
+        piece = pieces[d][...]
+        scaled = weights_of(piece, IDIM * count, count) * (IDIM ** -0.5)
+        rows = heads_of(piece, count)
+        act = dot(rows, keys[...])
+        gate[d * tile:(d + 1) * tile, :] = jnp.where(act > 0, 1.0, 0.0).astype(jnp.bfloat16)
+        for j in range(count):
+            total = total + jnp.maximum(act[j * share:(j + 1) * share], 0.0) * scaled[:, j:j + 1]
+        tall = jnp.concatenate([jnp.broadcast_to(scaled[:, j:j + 1], (share, IDIM)) for j in range(count)], 0)
+        high, low = split(rows.astype(jnp.float32) * tall)
+        turned[:IDIM, d * tile:(d + 1) * tile] = high.T
+        turned[IDIM:, d * tile:(d + 1) * tile] = low.T
+    score[...] = total
+
+
+def dscore_kernel(place, m0, m1, m2, m3, score, outside, qpos, kpos, spread, code):
+    z, position = place[0], place[1]
+    share, window = score.shape
+    kb = kpos.shape[1]
+    mass = (m0[...] + restored_rows(m1, window)) + (restored_rows(m2, window) + restored_rows(m3, window))
+    target = mass / jnp.sum(mass, axis=1, keepdims=True)
+    slot = lax.broadcasted_iota(jnp.int32, (share, window), 1) // kb
+    causal = kpos[...].astype(jnp.float32) <= column(qpos[...], z * share, share)
+    masked = jnp.where(position >= STEPS - 1 - slot, score[...], NEGATIVE)
+    masked = jnp.concatenate([masked[:, :window - kb], jnp.where(causal, masked[:, window - kb:], NEGATIVE)], 1)
+    out = column(outside[...], z * share, share)
+    top = jnp.maximum(jnp.max(masked, axis=1, keepdims=True), out)
+    expo = jnp.exp(masked - top)
+    total = jnp.sum(expo, axis=1, keepdims=True) + jnp.exp(out - top)
+    dscore = (expo / total - target) * float(window)
+    spread[0], spread[1] = split(dscore)
+    coded_rows(code, dscore)
+
+
+def keys_kernel(count, gate, turned, spread, *outs):
+    tile = count * spread.shape[1]
+    total = None
+    for d in range(GROUPS):
+        rows = slice(d * tile, (d + 1) * tile)
+        mask = gate[rows, :]
+        both = dot(turned[:, rows], mask * jnp.concatenate([spread[0]] * count, 0))
+        low = dot(turned[:IDIM, rows], mask * jnp.concatenate([spread[1]] * count, 0))
+        part = both[:IDIM] + both[IDIM:] + low
+        total = part if total is None else total + part
+    kb = outs[STEPS - 1].shape[0]
+    for i in range(STEPS):
+        part = total[:, i * kb:(i + 1) * kb].T
+        if i < STEPS - 1:
+            coded_columns(outs[i], part)
+        else:
+            outs[i][...] = part
+
+
+def query_kernel(heads, group, place, own, a, b, c, query, weight, c0, c1, c2, c3, *rest):
+    first = heads[0]
+    if first:
+        (done, before), rest = rest[:2], rest[2:]
+    grad, out, keys, turned, high, low, scale, tall = rest
+    share, rows = c0.shape[0], query.shape[0]
+    window = keys.shape[1]
+    gathered(place[1], (own, a, b, c), keys, 0)
+    turned[...] = keys[...].T
+    for d, code in enumerate((c0, c1, c2, c3)):
+        at = pl.ds(pl.multiple_of((place[0] ^ d) * share, share), share)
+        high[at, :], low[at, :] = split(code[:, :window].astype(jnp.float32))
+        scale[at, :] = scale_of(code[:, window:]) * (IDIM ** -0.5)
+    tall[...] = turned_tall(weight[...])
+    lane = lax.broadcasted_iota(jnp.int32, (rows, 128), 1)
+    total = before[...] if first else jnp.zeros((rows, 128), jnp.float32)
+    if first:
+        grad[:, :IDIM * first] = done[:, :IDIM * first]
+    for g in range(*heads, group):
+        tile = heads_of(query[:, IDIM * g:IDIM * (g + group)], group)
+        mask = jnp.where(dot(tile, keys[...]) > 0, 1.0, 0.0).astype(jnp.bfloat16)
+        part = dot(mask * jnp.concatenate([high[...]] * group, 0), turned[...])
+        part = part + dot(mask * jnp.concatenate([low[...]] * group, 0), turned[...])
+        for j in range(g, g + group):
+            lanes = slice(IDIM * j, IDIM * (j + 1))
+            mine = part[(j - g) * rows:(j - g + 1) * rows] * scale[...]
+            grad[:, lanes] = (mine * tall[:, j:j + 1]).astype(jnp.bfloat16)
+            product = jnp.sum(mine * query[:, lanes].astype(jnp.float32), axis=1, keepdims=True)
+            total = jnp.where(lane == j, product, total)
+    out[...] = total.T[:out.shape[0], :] if first else total
+
+
+def owned_kernel(p0, c1, c2, c3, after, code):
+    kb = p0.shape[0]
+    moved = [restored_columns(c, kb) for c in (c1, c2, c3)]
+    coded_columns(code, (p0[...] + moved[0]) + (moved[1] + moved[2]))
+
+
+def total_kernel(c0, c1, c2, c3, out):
+    parts = [restored_columns(c, out.shape[0]) for c in (c0, c1, c2, c3)]
+    out[...] = (parts[0] + parts[1]) + (parts[2] + parts[3])
+
+
+SMEM = pl.BlockSpec(memory_space=pltpu.SMEM)
+HBM = pl.BlockSpec(memory_space=pltpu.HBM)
+
+
+def held(array):
+    return pltpu.with_memory_space_constraint(array, pltpu.HBM)
+
+
+def whole(array):
+    rank = len(array.shape)
+    return pl.BlockSpec(array.shape, lambda i: (0,) * rank)
+
+
+def params(mib):
+    return pltpu.CompilerParams(vmem_limit_bytes=mib << 20)
+
+
+def cost(flops, size):
+    return pl.CostEstimate(flops=1, bytes_accessed=1, transcendentals=0)
+
+
+def along(x, axis, route):
+    return lax.ppermute(x, axis, [(i, j) for i, j in route if 0 <= j < lax.axis_size(axis)])
+
+
+def shards(
+    main_query,
+    latent,
+    main_outside,
+    index_query,
+    index_weights,
+    index_keys,
+    index_outside,
+    query_pos,
+    key_pos,
+):
+    rows = main_query.shape[0]
+    kb = latent.shape[0]
+    heads = main_outside.shape[1]
+    count = index_weights.shape[1]
+    share = rows // GROUPS
+    window = STEPS * kb
+    n_seq = lax.axis_size("seq")
+    z, position = lax.axis_index("head"), lax.axis_index("seq")
+    place = jnp.stack([z, position]).astype(jnp.int32)
+    bf16, f32, int16 = jnp.bfloat16, jnp.float32, jnp.int16
+
+    def shape(dims, kind):
+        return jax.ShapeDtypeStruct(dims, kind)
+
+    def exchanged(x, d):
+        return along(x, "head", [(i, i ^ d) for i in range(GROUPS)])
+
+    weights = index_weights.T
+    outsides = main_outside.T
+    qpos = query_pos.reshape(1, rows)
+    kpos = key_pos.reshape(1, kb)
+    outside = index_outside.reshape(1, rows)
+    piece_shape = (share, IDIM * count + 128)
+    pack_shape = (LAT + IDIM, kb)
+    packed, *mine = pl.pallas_call(
+        pack_kernel,
+        grid=(1,),
+        in_specs=[SMEM] + [HBM] * 4,
+        out_specs=[pl.BlockSpec(pack_shape, lambda i: (0, 0))]
+        + [pl.BlockSpec(piece_shape, lambda i: (0, 0))] * GROUPS,
+        out_shape=[shape(pack_shape, bf16)] + [shape(piece_shape, bf16)] * GROUPS,
+        scratch_shapes=[
+            pltpu.VMEM((rows, 128), bf16),
+            pltpu.VMEM((kb, IDIM), bf16),
+            pltpu.VMEM((count, rows), f32),
+            pltpu.SemaphoreType.DMA((3 + GROUPS,)),
+        ],
+        compiler_params=params(16),
+        cost_estimate=cost(0, 4 * rows * count * IDIM),
+        name="pack_rows",
+    )(place, *[held(x) for x in (latent.T, index_keys, index_query, weights)])
+    route_b = along(packed, "seq", [(i, i + (3 if i % 2 == 0 else 1)) for i in range(n_seq)])
+    route_a = along(packed, "seq", [(i, i + (1 if i % 2 == 0 else 3)) for i in range(n_seq)])
+    pieces = [mine[0]] + [exchanged(mine[d], d) for d in range(1, GROUPS)]
+
+    half = PER_STEP // 2
+    own_exp = pl.pallas_call(
+        functools.partial(own_kernel, half),
+        grid=(1,),
+        in_specs=[HBM, whole(packed), HBM, HBM],
+        out_specs=pl.BlockSpec((heads * rows, kb), lambda i: (0, 0)),
+        out_shape=shape((heads * rows, kb), f32),
+        scratch_shapes=[
+            pltpu.VMEM((704, kb), bf16),
+            pltpu.VMEM(main_query.shape, bf16),
+            pltpu.VMEM((8, kb), jnp.int32),
+            pltpu.SemaphoreType.DMA((heads // PER_STEP + 2,)),
+        ],
+        compiler_params=params(24),
+        cost_estimate=cost(2 * heads * rows * kb * LAT, heads * rows * (2 * LAT + 4 * kb)),
+        name="own_block",
+    )(held(main_query), packed, held(qpos), held(kpos))
+
+    route_b, own_exp, pieces[1], pieces[2] = lax.optimization_barrier((route_b, own_exp, pieces[1], pieces[2]))
+    route_c = along(route_b, "seq", [(i, i ^ 1) for i in range(n_seq)])
+    blocks = (packed, route_a, route_b, route_c)
+    code_shape = (share, window + 128)
+    mass = pl.pallas_call(
+        functools.partial(main_kernel, half),
+        grid=(1,),
+        in_specs=[SMEM] + [whole(x) for x in (main_query, *blocks, own_exp, outsides, qpos, kpos)],
+        out_specs=[pl.BlockSpec((share, window), lambda i: (0, 0))]
+        + [pl.BlockSpec(code_shape, lambda i: (0, 0))] * (GROUPS - 1),
+        out_shape=[shape((share, window), f32)] + [shape(code_shape, int16)] * (GROUPS - 1),
+        scratch_shapes=[pltpu.VMEM((half * rows, window - kb), f32)] * BUFFERS
+        + [pltpu.VMEM((half * rows, 128), f32)] * BUFFERS
+        + [
+            pltpu.VMEM((704, window), bf16),
+            pltpu.VMEM((rows, 128), f32),
+            pltpu.VMEM((rows, window), f32),
+        ],
+        compiler_params=params(32),
+        cost_estimate=cost(2 * heads * rows * window * LAT, heads * rows * 2 * LAT),
+        name="main_mass",
+    )(place, main_query, *blocks, own_exp, outsides, qpos, kpos)
+    masses = [mass[0]] + [exchanged(mass[d], d) for d in range(1, GROUPS)]
+
+    tile = count * share
+    key_spec = pl.BlockSpec((IDIM, kb), lambda i: (0, 0))
+    key_rows = [x[LAT:] for x in blocks]
+    score, gate, turned = pl.pallas_call(
+        functools.partial(index_kernel, count),
+        grid=(1,),
+        in_specs=[SMEM] + [key_spec] * 4 + [whole(x) for x in pieces],
+        out_specs=[
+            pl.BlockSpec((share, window), lambda i: (0, 0)),
+            pl.BlockSpec((GROUPS * tile, window), lambda i: (0, 0)),
+            pl.BlockSpec((2 * IDIM, GROUPS * tile), lambda i: (0, 0)),
+        ],
+        out_shape=[
+            shape((share, window), f32),
+            shape((GROUPS * tile, window), bf16),
+            shape((2 * IDIM, GROUPS * tile), bf16),
+        ],
+        scratch_shapes=[pltpu.VMEM((IDIM, window), bf16)],
+        compiler_params=params(24),
+        cost_estimate=cost(4 * GROUPS * tile * window * IDIM, GROUPS * tile * window * 2),
+        name="index_scores",
+    )(place, *key_rows, *pieces)
+
+    spread, code = pl.pallas_call(
+        dscore_kernel,
+        grid=(1,),
+        in_specs=[SMEM] + [whole(x) for x in (*masses, score, outside, qpos, kpos)],
+        out_specs=[
+            pl.BlockSpec((2, share, window), lambda i: (0, 0, 0)),
+            pl.BlockSpec(code_shape, lambda i: (0, 0)),
+        ],
+        out_shape=[shape((2, share, window), bf16), shape(code_shape, int16)],
+        compiler_params=params(16),
+        cost_estimate=cost(0, 12 * share * window),
+        name="dscores",
+    )(place, *masses, score, outside, qpos, kpos)
+    codes = [code] + [exchanged(code, d) for d in range(1, GROUPS)]
+
+    sum_shape = (kb + 16, IDIM)
+    parts = pl.pallas_call(
+        functools.partial(keys_kernel, count),
+        grid=(1,),
+        in_specs=[whole(gate), whole(turned), whole(spread)],
+        out_specs=[pl.BlockSpec(sum_shape, lambda i: (0, 0))] * (STEPS - 1)
+        + [pl.BlockSpec((kb, IDIM), lambda i: (0, 0))],
+        out_shape=[shape(sum_shape, int16)] * (STEPS - 1) + [shape((kb, IDIM), f32)],
+        compiler_params=params(24),
+        cost_estimate=cost(8 * GROUPS * tile * window * IDIM, GROUPS * tile * window * 2),
+        name="key_grads",
+    )(gate, turned, spread)
+    sent = [parts[STEPS - 1 - distance] for distance in range(1, STEPS)]
+    sent[-1], *codes = lax.optimization_barrier((sent[-1], *codes))
+    moved = [along(x, "seq", [(i, i - d - 1) for i in range(n_seq)]) for d, x in enumerate(sent)]
+
+    group = count // 4
+
+    def query_grads(first, last, before):
+        sums_shape = (count, rows) if first else (rows, 128)
+        return pl.pallas_call(
+            functools.partial(query_kernel, (first, last), group),
+            grid=(1,),
+            in_specs=[SMEM] + [key_spec] * 4
+            + [whole(x) for x in (index_query, weights, *codes)]
+            + [whole(x) for x in before],
+            out_specs=[
+                pl.BlockSpec((rows, IDIM * count), lambda i: (0, 0)),
+                pl.BlockSpec(sums_shape, lambda i: (0, 0)),
+            ],
+            out_shape=[shape((rows, IDIM * count), bf16), shape(sums_shape, f32)],
+            scratch_shapes=[
+                pltpu.VMEM((IDIM, window), bf16),
+                pltpu.VMEM((window, IDIM), bf16),
+                pltpu.VMEM((rows, window), bf16),
+                pltpu.VMEM((rows, window), bf16),
+                pltpu.VMEM((rows, 128), f32),
+                pltpu.VMEM((rows, 128), f32),
+            ],
+            compiler_params=params(24),
+            cost_estimate=cost(8 * rows * (last - first) * window * IDIM, 8 * rows * count * IDIM),
+            name="query_grads",
+        )(place, *key_rows, index_query, weights, *codes, *before)
+
+    begun = query_grads(0, group, ())
+    grad_query, grad_weight = query_grads(group, count, begun)
+
+    owned = pl.pallas_call(
+        owned_kernel,
+        grid=(1,),
+        in_specs=[whole(x) for x in (parts[STEPS - 1], *moved, begun[1])],
+        out_specs=pl.BlockSpec(sum_shape, lambda i: (0, 0)),
+        out_shape=shape(sum_shape, int16),
+        compiler_params=params(16),
+        cost_estimate=cost(0, 20 * kb * IDIM),
+        name="owned_keys",
+    )(parts[STEPS - 1], *moved, begun[1])
+    owners = [owned] + [exchanged(owned, d) for d in range(1, GROUPS)]
+    grad_keys = pl.pallas_call(
+        total_kernel,
+        grid=(1,),
+        in_specs=[whole(x) for x in owners],
+        out_specs=pl.BlockSpec((kb, IDIM), lambda i: (0, 0)),
+        out_shape=shape((kb, IDIM), f32),
+        compiler_params=params(16),
+        cost_estimate=cost(0, 12 * kb * IDIM),
+        name="total_keys",
+    )(*owners)
+    return (grad_query, grad_weight.T, grad_keys)
+
+
+def any_shards(main_query, latent, main_outside, index_query, index_weights, index_keys, *rest):
+    args = (main_query, latent, main_outside, index_query, index_weights, index_keys, *rest)
+    fits = (
+        lax.axis_size("head") == GROUPS
+        and lax.axis_size("seq") % 2 == 0
+        and main_query.shape[0] == 128
+        and main_outside.shape[1] % PER_STEP == 0
+        and main_outside.shape[1] <= 128
+        and latent.shape[0] % 256 == 0
+        and latent.shape[1] == LAT
+        and 3 * index_weights.shape[1] <= 128
+        and index_weights.shape[1] % 16 == 0
+    )
+    return shards(*args) if fits else plain_shards(*args)
+
+
 def solution(mesh):
     in_specs = (
         P("seq", "head"),
@@ -123,4 +735,4 @@
         P("seq"),
     )
     out_specs = (P("seq", "head"), P("seq", "head"), P("seq", None))
-    return jax.shard_map(shards, mesh=mesh, in_specs=in_specs, out_specs=out_specs, check_vma=False)
+    return jax.shard_map(any_shards, mesh=mesh, in_specs=in_specs, out_specs=out_specs, check_vma=False)

time: 176 us -> 86 us (0.49)
  Pallas kernels: 0 us -> 45.2 us
  waiting for transfers between devices: 49 us -> 9.16 us
  matrix products: 29.5 us -> 0 us
  other arithmetic: 29.5 us -> 0.08 us
  blocking collectives: 16.1 us -> 0 us
  local copies, waits for them, and re-layouts: 15.6 us -> 0.07 us
  between operations: 14 us -> 0.92 us
  starting transfers between devices: 21.4 us -> 30.3 us
    pallas_call x0 -> x10, Pallas kernels: none -> 45.2 us  [the longest x1 26.5 us: shards(): pl.pallas_call(functools.partial(main_kernel, half), grid=(1,), in_specs=...]
    dot_general x4 -> x0, matrix products: 29.5 us -> none  [the longest x1 13.2 us: shards(): jnp.einsum('qhc,wc->hqw', queries, latent_window, preferred_element_type=...]
    psum x1 -> x0, waiting for transfers between devices: 29.5 us -> none  [shards(): grad_keys = lax.psum(grad_total, 'head')]
    reduce_sum x4 -> x0, other arithmetic: 19.5 us -> none  [the longest x1 9.34 us: head_mass(): total = jnp.sum(expo, axis=2) + jnp.exp(outside.T - highest)]
    reduce_scatter x2 -> x0, waiting for transfers between devices: 18.8 us -> none  [the longest x1 18.8 us: shards(): lax.psum_scatter(mass_part, 'head', scatter_dimension=0, tiled=True)]
    all_gather x1 -> x0, blocking collectives: 16.1 us -> none  [shards(): lax.all_gather(score_grad(mass, index_score, visible_rows, outside_rows),...]
    unnamed x19 -> x16, local copies, waits for them, and re-layouts: 14.5 us -> 0.05 us
    ppermute x9 -> x18, starting transfers between devices: 21.1 us -> 30.3 us  [along(): lax.ppermute(x, axis, [(i, j) for i, j in route if 0 <= j < lax.axis_size...]
  transfers between devices with their start and end apart: 12 -> 18, of which waited for: 3 -> 7; matrix products, arithmetic and copies ran while one was open for 35% -> 0% of each run, Pallas kernels for 0% -> 48%
where the time goes in v2:
time: 86 us; the launch traced here: 85.8 us
  Pallas kernels  45.2 us (53%)
  starting transfers between devices  30.3 us (35%)
  waiting for transfers between devices  9.16 us (11%)
  between operations  0.92 us (1%)
    ppermute x18, starting transfers between devices, along(): lax.ppermute(x, axis, [(i, j) for i, j in route if 0 <= j < lax.axis_size...  30.3 us
    pallas_call x1, Pallas kernels, shards(): pl.pallas_call(functools.partial(main_kernel, half), grid=(1,), in_specs=...  26.5 us
    ppermute x18, waiting for transfers between devices, along(): lax.ppermute(x, axis, [(i, j) for i, j in route if 0 <= j < lax.axis_size...  9.16 us
    pallas_call x2, Pallas kernels, query_grads(): pl.pallas_call(functools.partial(query_kernel, (first, last), group), gri...  6.37 us
    pallas_call x1, Pallas kernels, shards(): pl.pallas_call(functools.partial(own_kernel, half), grid=(1,), in_specs=[...  3.74 us
    pallas_call x1, Pallas kernels, shards(): pl.pallas_call(functools.partial(index_kernel, count), grid=(1,), in_spec...  2.73 us
    pallas_call x1, Pallas kernels, shards(): pl.pallas_call(pack_kernel, grid=(1,), in_specs=[SMEM] + [HBM] * 4, out_s...  2.07 us
    pallas_call x1, Pallas kernels, shards(): pl.pallas_call(functools.partial(keys_kernel, count), grid=(1,), in_specs...  1.95 us
  transfers between devices with their start and end apart: 18, of which 7 were waited for; matrix products, arithmetic and copies ran while one was open for 0% of the time, Pallas kernels for 48%

profile of v2, /device:TPU:0, one launch (start us, length us, event | category | flops | bytes accessed | tf_op | source)
XLA Modules:
  0.0 85.8 jit_solution(12169131077599207349)
XLA Ops:
  0.6 0.1 pad_add_fusion.place
  0.7 2.1 %pack_rows.1 = (bf16[704,256]{1,0:T(8,128)(2,1)S(1)}, bf16[32,2176]{1,0:T(8,128)(2,1)S(1)}, bf16[32,2176]{1,0:T(8,128)(2,1)S(1)}, bf16[32,2176]{1,0:T(8,128)(2,1)S(1)}, bf16[32,2176]{1,0:T(8,128)(2,1)S(1)}) custom-call(s32[2]{0:T(128)S(1)} %pad_add_fusion.place, bf16[576,256]{1,0:T(8,128)(2,1)} %bitcast.22, bf16[256,128]{1,0:T(8,128)(2,1)} %keys.1, ...), custom_call_target="tpu_custom_call" | custom-call | flops 1 | bytes 1 | tf_op jit(solution)/shard_map/pack_rows/pallas_call | solution.py:537
  2.8 4.3 %collective-permute-start.1 = (bf16[704,256]{1,0:T(8,128)(2,1)S(1)}, bf16[704,256]{1,0:T(8,128)(2,1)S(1)}, u32[]{:S(2)}, u32[]{:S(2)}) collective-permute-start(bf16[704,256]{1,0:T(8,128)(2,1)S(1)} %get-tuple-element.34.own), channel_id=1, source_target_pairs={{0,12},{4,8},{8,20},{12,16},{16,28},{20,24},{1,13},{5,9},{9,21},{1... | collective-permute-start | bytes 1081352 | tf_op jit(solution)/shard_map/ppermute | solution.py:499
  7.1 1.6 %collective-permute-start.2 = (bf16[32,2176]{1,0:T(8,128)(2,1)S(1)}, bf16[32,2176]{1,0:T(8,128)(2,1)S(1)}, u32[]{:S(2)}, u32[]{:S(2)}) collective-permute-start(bf16[32,2176]{1,0:T(8,128)(2,1)S(1)} %get-tuple-element.35), channel_id=1, source_target_pairs={{0,1},{1,0},{2,3},{3,2},{4,5},{5,4},{6,7},{7,6},{8,9},{9,8},{10,11... | collective-permute-start | bytes 417800 | tf_op jit(solution)/shard_map/ppermute | solution.py:499
  8.7 2.6 %collective-permute-start.3 = (bf16[32,2176]{1,0:T(8,128)(2,1)S(1)}, bf16[32,2176]{1,0:T(8,128)(2,1)S(1)}, u32[]{:S(2)}, u32[]{:S(2)}) collective-permute-start(bf16[32,2176]{1,0:T(8,128)(2,1)S(1)} %get-tuple-element.36), channel_id=1, source_target_pairs={{0,2},{1,3},{2,0},{3,1},{4,6},{5,7},{6,4},{7,5},{8,10},{9,11},{10,... | collective-permute-start | bytes 417800 | tf_op jit(solution)/shard_map/ppermute | solution.py:499
  11.3 2.1 %collective-permute-start = (bf16[704,256]{1,0:T(8,128)(2,1)S(1)}, bf16[704,256]{1,0:T(8,128)(2,1)S(1)}, u32[]{:S(2)}, u32[]{:S(2)}) collective-permute-start(bf16[704,256]{1,0:T(8,128)(2,1)S(1)} %get-tuple-element.34.own), channel_id=1, source_target_pairs={{0,4},{4,16},{8,12},{12,24},{16,20},{24,28},{1,5},{5,17},{9,13},{1... | collective-permute-start | bytes 1081352 | tf_op jit(solution)/shard_map/ppermute | solution.py:499
  13.4 0.0 slice-start.1
  13.4 0.0 copy-start.2
  13.4 0.0 copy-start.3
  13.4 0.0 copy-start.4
  13.5 3.7 %own_block.1.own_exp = f32[4096,256]{1,0:T(8,128)S(1)} custom-call(bf16[128,18432]{1,0:T(8,128)(2,1)} %q.3, bf16[704,256]{1,0:T(8,128)(2,1)S(1)} %get-tuple-element.34.own, s32[1,128]{1,0:T(1,128)} %bitcast.18, s32[1,256]{1,0:T(1,128)} %bitcast.15), custom_call_target="tpu_custom_call" | custom-call | flops 1 | bytes 1 | tf_op jit(solution)/shard_map/own_block/pallas_call | solution.py:559
  17.2 0.0 collective-permute-done.2.rest_1_
  17.2 1.5 %collective-permute-done.3.rest_2_ = bf16[32,2176]{1,0:T(8,128)(2,1)S(1)} collective-permute-done((bf16[32,2176]{1,0:T(8,128)(2,1)S(1)}, bf16[32,2176]{1,0:T(8,128)(2,1)S(1)}, u32[]{:S(2)}, u32[]{:S(2)}) %collective-permute-start.3) | collective-permute-done | bytes 139296 | tf_op jit(solution)/shard_map/ppermute | solution.py:499
  18.7 0.0 collective-permute-done.1.b
  18.7 0.1 collective-permute-start.4
  18.7 2.4 %collective-permute-start.5 = (bf16[32,2176]{1,0:T(8,128)(2,1)S(1)}, bf16[32,2176]{1,0:T(8,128)(2,1)S(1)}, u32[]{:S(2)}, u32[]{:S(2)}) collective-permute-start(bf16[32,2176]{1,0:T(8,128)(2,1)S(1)} %get-tuple-element.41), channel_id=1, source_target_pairs={{0,3},{1,2},{2,1},{3,0},{4,7},{5,6},{6,5},{7,4},{8,11},{9,10},{10,... | collective-permute-start | bytes 417800 | tf_op jit(solution)/shard_map/ppermute | solution.py:499
  21.2 0.0 copy-start.5
  21.2 26.5 %main_mass.1 = (f32[32,1024]{1,0:T(8,128)S(1)}, s16[32,1152]{1,0:T(8,128)(2,1)S(1)}, s16[32,1152]{1,0:T(8,128)(2,1)S(1)}, s16[32,1152]{1,0:T(8,128)(2,1)S(1)}) custom-call(s32[2]{0:T(128)S(1)} %pad_add_fusion.place, bf16[128,18432]{1,0:T(8,128)(2,1)S(1)} %bitcast.10, bf16[704,256]{1,0:T(8,128)(2,1)S(1)} %get-tuple-element.34.own, ...), custom_call_target="tpu_custom_call" | custom-call | flops 1 | bytes 1 | tf_op jit(solution)/shard_map/main_mass/pallas_call | solution.py:580
  47.8 0.0 copy-start
  47.8 0.0 copy-start.1
  47.8 0.1 collective-permute-start.6
  47.9 2.2 %collective-permute-start.7 = (s16[32,1152]{1,0:T(8,128)(2,1)S(1)}, s16[32,1152]{1,0:T(8,128)(2,1)S(1)}, u32[]{:S(2)}, u32[]{:S(2)}) collective-permute-start(s16[32,1152]{1,0:T(8,128)(2,1)S(1)} %get-tuple-element.47), channel_id=1, source_target_pairs={{0,2},{1,3},{2,0},{3,1},{4,6},{5,7},{6,4},{7,5},{8,10},{9,11},{10,... | collective-permute-start | bytes 221192 | tf_op jit(solution)/shard_map/ppermute | solution.py:499
  50.1 2.2 %collective-permute-start.8 = (s16[32,1152]{1,0:T(8,128)(2,1)S(1)}, s16[32,1152]{1,0:T(8,128)(2,1)S(1)}, u32[]{:S(2)}, u32[]{:S(2)}) collective-permute-start(s16[32,1152]{1,0:T(8,128)(2,1)S(1)} %get-tuple-element.48), channel_id=1, source_target_pairs={{0,3},{1,2},{2,1},{3,0},{4,7},{5,6},{6,5},{7,4},{8,11},{9,10},{10,... | collective-permute-start | bytes 221192 | tf_op jit(solution)/shard_map/ppermute | solution.py:499
  52.3 0.0 collective-permute-done.5.rest_3_
  52.3 2.7 %index_scores.1 = (f32[32,1024]{1,0:T(8,128)S(1)}, bf16[2048,1024]{1,0:T(8,128)(2,1)S(1)}, bf16[256,2048]{1,0:T(8,128)(2,1)S(1)}) custom-call(s32[2]{0:T(128)S(1)} %pad_add_fusion.place, bf16[128,256]{1,0:T(8,128)(2,1)S(1)} %slice.12.own, bf16[128,256]{1,0:T(8,128)(2,1)S(1)} %slice.16.a, bf16[128,256]{1,0:T(8,128)(2,1)S(1)} %slice.14.b, ...), custom_call_target="tpu_custom_call" | custom-call | flops 1 | bytes 1 | tf_op jit(solution)/shard_map/index_scores/pallas_call | solution.py:603
  55.1 0.0 collective-permute-done.6.m1
  55.1 2.1 %collective-permute-done.7.m2 = s16[32,1152]{1,0:T(8,128)(2,1)S(1)} collective-permute-done((s16[32,1152]{1,0:T(8,128)(2,1)S(1)}, s16[32,1152]{1,0:T(8,128)(2,1)S(1)}, u32[]{:S(2)}, u32[]{:S(2)}) %collective-permute-start.7) | collective-permute-done | bytes 73760 | tf_op jit(solution)/shard_map/ppermute | solution.py:499
  57.2 0.0 collective-permute-done.8.m3
  57.2 1.0 %dscores.1 = (bf16[2,32,1024]{2,1,0:T(8,128)(2,1)S(1)}, s16[32,1152]{1,0:T(8,128)(2,1)S(1)}) custom-call(s32[2]{0:T(128)S(1)} %pad_add_fusion.place, f32[32,1024]{1,0:T(8,128)S(1)} %get-tuple-element.45.m0, s16[32,1152]{1,0:T(8,128)(2,1)S(1)} %collective-permute-done.6.m1, s16[32,1152]{1,0:T(8,128)(2,1)S(1)} %collective-permute-done.7.m2, ...), custom_call_target="tpu_custom_call" | custom-call | flops 1 | bytes 1 | tf_op jit(solution)/shard_map/dscores/pallas_call | solution.py:623
  58.1 2.0 %collective-permute-start.10 = (s16[32,1152]{1,0:T(8,128)(2,1)S(1)}, s16[32,1152]{1,0:T(8,128)(2,1)S(1)}, u32[]{:S(2)}, u32[]{:S(2)}) collective-permute-start(s16[32,1152]{1,0:T(8,128)(2,1)S(1)} %get-tuple-element.53.c0), channel_id=1, source_target_pairs={{0,2},{1,3},{2,0},{3,1},{4,6},{5,7},{6,4},{7,5},{8,10},{9,11},{10,... | collective-permute-start | bytes 221192 | tf_op jit(solution)/shard_map/ppermute | solution.py:499
  60.2 2.4 %collective-permute-start.11 = (s16[32,1152]{1,0:T(8,128)(2,1)S(1)}, s16[32,1152]{1,0:T(8,128)(2,1)S(1)}, u32[]{:S(2)}, u32[]{:S(2)}) collective-permute-start(s16[32,1152]{1,0:T(8,128)(2,1)S(1)} %get-tuple-element.53.c0), channel_id=1, source_target_pairs={{0,3},{1,2},{2,1},{3,0},{4,7},{5,6},{6,5},{7,4},{8,11},{9,10},{10,... | collective-permute-start | bytes 221192 | tf_op jit(solution)/shard_map/ppermute | solution.py:499
  62.5 2.0 %key_grads.1 = (s16[272,128]{1,0:T(8,128)(2,1)S(1)}, s16[272,128]{1,0:T(8,128)(2,1)S(1)}, s16[272,128]{1,0:T(8,128)(2,1)S(1)}, f32[256,128]{1,0:T(8,128)S(1)}) custom-call(bf16[2048,1024]{1,0:T(8,128)(2,1)S(1)} %get-tuple-element.42.gate, bf16[256,2048]{1,0:T(8,128)(2,1)S(1)} %get-tuple-element.43.turned, bf16[2,32,1024]{2,1,0:T(8,128)(2,1)S(1)} %get-tuple-element.50.spread), custom_call_target="tpu_custom_call" | custom-call | flops 1 | bytes 1 | tf_op jit(solution)/shard_map/key_grads/pallas_call | solution.py:639
  64.5 1.3 %collective-permute-start.12 = (s16[272,128]{1,0:T(8,128)(2,1)S(1)}, s16[272,128]{1,0:T(8,128)(2,1)S(1)}, u32[]{:S(2)}, u32[]{:S(2)}) collective-permute-start(s16[272,128]{1,0:T(8,128)(2,1)S(1)} %get-tuple-element.62), channel_id=1, source_target_pairs={{4,0},{8,4},{12,8},{16,12},{20,16},{24,20},{28,24},{5,1},{9,5},{13... | collective-permute-start | bytes 208904 | tf_op jit(solution)/shard_map/ppermute | solution.py:499
  65.8 1.3 %collective-permute-start.13 = (s16[272,128]{1,0:T(8,128)(2,1)S(1)}, s16[272,128]{1,0:T(8,128)(2,1)S(1)}, u32[]{:S(2)}, u32[]{:S(2)}) collective-permute-start(s16[272,128]{1,0:T(8,128)(2,1)S(1)} %get-tuple-element.63), channel_id=1, source_target_pairs={{8,0},{12,4},{16,8},{20,12},{24,16},{28,20},{9,1},{13,5},{17,9},{2... | collective-permute-start | bytes 208904 | tf_op jit(solution)/shard_map/ppermute | solution.py:499
  67.1 0.2 collective-permute-done.10.c2
  67.2 0.0 collective-permute-done.11.c3
  67.3 0.9 %collective-permute-done.9.c1 = s16[32,1152]{1,0:T(8,128)(2,1)S(1)} collective-permute-done((s16[32,1152]{1,0:T(8,128)(2,1)S(1)}, s16[32,1152]{1,0:T(8,128)(2,1)S(1)}, u32[]{:S(2)}, u32[]{:S(2)}) %collective-permute-start.9) | collective-permute-done | bytes 73760 | tf_op jit(solution)/shard_map/ppermute | solution.py:499
  68.1 1.3 %collective-permute-start.14 = (s16[272,128]{1,0:T(8,128)(2,1)S(1)}, s16[272,128]{1,0:T(8,128)(2,1)S(1)}, u32[]{:S(2)}, u32[]{:S(2)}) collective-permute-start(s16[272,128]{1,0:T(8,128)(2,1)S(1)} %get-tuple-element.64), channel_id=1, source_target_pairs={{12,0},{16,4},{20,8},{24,12},{28,16},{13,1},{17,5},{21,9},{25,13},... | collective-permute-start | bytes 208904 | tf_op jit(solution)/shard_map/ppermute | solution.py:499
  69.4 2.0 %query_grads.2 = (bf16[128,2048]{1,0:T(8,128)(2,1)S(1)}, f32[128,128]{1,0:T(8,128)S(1)}) custom-call(s32[2]{0:T(128)S(1)} %pad_add_fusion.place, bf16[128,256]{1,0:T(8,128)(2,1)S(1)} %slice.12.own, bf16[128,256]{1,0:T(8,128)(2,1)S(1)} %slice.16.a, bf16[128,256]{1,0:T(8,128)(2,1)S(1)} %slice.14.b, bf16[128,256]{1,0:T(8,128)(2,1)S(1)} %slice.17.c, ...), custom_call_target="tpu_custom_call" | custom-call | flops 1 | bytes 1 | tf_op jit(solution)/shard_map/query_grads/pallas_call | solution.py:658
  71.4 1.1 %collective-permute-done.13.c2 = s16[272,128]{1,0:T(8,128)(2,1)S(1)} collective-permute-done((s16[272,128]{1,0:T(8,128)(2,1)S(1)}, s16[272,128]{1,0:T(8,128)(2,1)S(1)}, u32[]{:S(2)}, u32[]{:S(2)}) %collective-permute-start.13) | collective-permute-done | bytes 69664 | tf_op jit(solution)/shard_map/ppermute | solution.py:499
  72.6 1.5 %collective-permute-done.14.c3 = s16[272,128]{1,0:T(8,128)(2,1)S(1)} collective-permute-done((s16[272,128]{1,0:T(8,128)(2,1)S(1)}, s16[272,128]{1,0:T(8,128)(2,1)S(1)}, u32[]{:S(2)}, u32[]{:S(2)}) %collective-permute-start.14) | collective-permute-done | bytes 69664 | tf_op jit(solution)/shard_map/ppermute | solution.py:499
  74.1 0.1 owned_keys.1.c0
  74.2 2.1 %collective-permute-start.15 = (s16[272,128]{1,0:T(8,128)(2,1)S(1)}, s16[272,128]{1,0:T(8,128)(2,1)S(1)}, u32[]{:S(2)}, u32[]{:S(2)}) collective-permute-start(s16[272,128]{1,0:T(8,128)(2,1)S(1)} %owned_keys.1.c0), channel_id=1, source_target_pairs={{0,1},{1,0},{2,3},{3,2},{4,5},{5,4},{6,7},{7,6},{8,9},{9,8},{10,11... | collective-permute-start | bytes 208904 | tf_op jit(solution)/shard_map/ppermute | solution.py:499
  76.3 0.1 collective-permute-start.16
  76.4 2.4 %collective-permute-start.17 = (s16[272,128]{1,0:T(8,128)(2,1)S(1)}, s16[272,128]{1,0:T(8,128)(2,1)S(1)}, u32[]{:S(2)}, u32[]{:S(2)}) collective-permute-start(s16[272,128]{1,0:T(8,128)(2,1)S(1)} %owned_keys.1.c0), channel_id=1, source_target_pairs={{0,3},{1,2},{2,1},{3,0},{4,7},{5,6},{6,5},{7,4},{8,11},{9,10},{10,... | collective-permute-start | bytes 208904 | tf_op jit(solution)/shard_map/ppermute | solution.py:499
  78.8 4.4 %query_grads.3 = (bf16[128,2048]{1,0:T(8,128)(2,1)}, f32[16,128]{1,0:T(8,128)}) custom-call(s32[2]{0:T(128)S(1)} %pad_add_fusion.place, bf16[128,256]{1,0:T(8,128)(2,1)S(1)} %slice.12.own, bf16[128,256]{1,0:T(8,128)(2,1)S(1)} %slice.16.a, bf16[128,256]{1,0:T(8,128)(2,1)S(1)} %slice.14.b, bf16[128,256]{1,0:T(8,128)(2,1)S(1)} %slice.17.c, ...), custom_call_target="tpu_custom_call" | custom-call | flops 1 | bytes 1 | tf_op jit(solution)/shard_map/query_grads/pallas_call | solution.py:658
  83.2 1.9 %collective-permute-done.16.c2 = s16[272,128]{1,0:T(8,128)(2,1)S(1)} collective-permute-done((s16[272,128]{1,0:T(8,128)(2,1)S(1)}, s16[272,128]{1,0:T(8,128)(2,1)S(1)}, u32[]{:S(2)}, u32[]{:S(2)}) %collective-permute-start.16) | collective-permute-done | bytes 69664 | tf_op jit(solution)/shard_map/ppermute | solution.py:499
  85.0 0.7 total_keys.1
  (20 shorter events, 0.1 us)
Async XLA Ops:
  0.7 20.5 %slice-start = ((s8[4718592]{0:T(1024)(128)(4,1)}), s8[4194304]{0:T(1024)(128)(4,1)S(1)}, s32[]{:S(2)}) async-start(s8[4718592]{0:T(1024)(128)(4,1)} %bitcast.9), calls=%async_computation | async-start | bytes 8388608
  2.8 15.9 %collective-permute-start.1 = (bf16[704,256]{1,0:T(8,128)(2,1)S(1)}, bf16[704,256]{1,0:T(8,128)(2,1)S(1)}, u32[]{:S(2)}, u32[]{:S(2)}) collective-permute-start(bf16[704,256]{1,0:T(8,128)(2,1)S(1)} %get-tuple-element.34.own), channel_id=1, source_target_pairs={{0,12},{4,8},{8,20},{12,16},{16,28},{20,24},{1,13},{5,9},{9,21},{1... | collective-permute-start | bytes 1081352 | tf_op jit(solution)/shard_map/ppermute | solution.py:499
  7.1 10.1 %collective-permute-start.2 = (bf16[32,2176]{1,0:T(8,128)(2,1)S(1)}, bf16[32,2176]{1,0:T(8,128)(2,1)S(1)}, u32[]{:S(2)}, u32[]{:S(2)}) collective-permute-start(bf16[32,2176]{1,0:T(8,128)(2,1)S(1)} %get-tuple-element.35), channel_id=1, source_target_pairs={{0,1},{1,0},{2,3},{3,2},{4,5},{5,4},{6,7},{7,6},{8,9},{9,8},{10,11... | collective-permute-start | bytes 417800 | tf_op jit(solution)/shard_map/ppermute | solution.py:499
  8.7 9.9 %collective-permute-start.3 = (bf16[32,2176]{1,0:T(8,128)(2,1)S(1)}, bf16[32,2176]{1,0:T(8,128)(2,1)S(1)}, u32[]{:S(2)}, u32[]{:S(2)}) collective-permute-start(bf16[32,2176]{1,0:T(8,128)(2,1)S(1)} %get-tuple-element.36), channel_id=1, source_target_pairs={{0,2},{1,3},{2,0},{3,1},{4,6},{5,7},{6,4},{7,5},{8,10},{9,11},{10,... | collective-permute-start | bytes 417800 | tf_op jit(solution)/shard_map/ppermute | solution.py:499
  11.3 9.8 %collective-permute-start = (bf16[704,256]{1,0:T(8,128)(2,1)S(1)}, bf16[704,256]{1,0:T(8,128)(2,1)S(1)}, u32[]{:S(2)}, u32[]{:S(2)}) collective-permute-start(bf16[704,256]{1,0:T(8,128)(2,1)S(1)} %get-tuple-element.34.own), channel_id=1, source_target_pairs={{0,4},{4,16},{8,12},{12,24},{16,20},{24,28},{1,5},{5,17},{9,13},{1... | collective-permute-start | bytes 1081352 | tf_op jit(solution)/shard_map/ppermute | solution.py:499
  13.4 7.8 %slice-start.1 = ((s8[4718592]{0:T(1024)(128)(4,1)}), s8[524288]{0:T(1024)(128)(4,1)S(1)}, s32[]{:S(2)}) async-start(s8[4718592]{0:T(1024)(128)(4,1)} %bitcast.9), calls=%async_computation.1 | async-start | bytes 1048576
  13.4 7.8 %copy-start.2 = (f32[128,32]{0,1:T(8,128)S(1)}, f32[128,32]{0,1:T(8,128)}, u32[]{:S(2)}) copy-start(f32[128,32]{0,1:T(8,128)} %param.11) | copy-start | bytes 49156
  13.4 7.8 %copy-start.3 = (s32[256]{0:T(256)S(1)}, s32[256]{0:T(256)}, u32[]{:S(2)}) copy-start(s32[256]{0:T(256)} %param.17) | copy-start | bytes 3076
  13.4 7.8 %copy-start.4 = (s32[128]{0:T(128)S(1)}, s32[128]{0:T(128)}, u32[]{:S(2)}) copy-start(s32[128]{0:T(128)} %param.16) | copy-start | bytes 1540
  18.7 2.5 %collective-permute-start.4 = (bf16[704,256]{1,0:T(8,128)(2,1)S(1)}, bf16[704,256]{1,0:T(8,128)(2,1)S(1)}, u32[]{:S(2)}, u32[]{:S(2)}) collective-permute-start(bf16[704,256]{1,0:T(8,128)(2,1)S(1)} %collective-permute-done.1.b), channel_id=1, source_target_pairs={{0,4},{4,0},{8,12},{12,8},{16,20},{20,16},{24,28},{28,24},{1,5},{5... | collective-permute-start | bytes 1081352 | tf_op jit(solution)/shard_map/ppermute | solution.py:499
  18.7 33.6 %collective-permute-start.5 = (bf16[32,2176]{1,0:T(8,128)(2,1)S(1)}, bf16[32,2176]{1,0:T(8,128)(2,1)S(1)}, u32[]{:S(2)}, u32[]{:S(2)}) collective-permute-start(bf16[32,2176]{1,0:T(8,128)(2,1)S(1)} %get-tuple-element.41), channel_id=1, source_target_pairs={{0,3},{1,2},{2,1},{3,0},{4,7},{5,6},{6,5},{7,4},{8,11},{9,10},{10,... | collective-permute-start | bytes 417800 | tf_op jit(solution)/shard_map/ppermute | solution.py:499
  21.2 35.9 %copy-start.5 = (f32[128]{0:T(128)S(1)}, f32[128]{0:T(128)}, u32[]{:S(2)}) copy-start(f32[128]{0:T(128)} %param.15) | copy-start | bytes 1540
  47.8 21.6 %copy-start = (bf16[128,2048]{1,0:T(8,128)(2,1)S(1)}, bf16[128,2048]{1,0:T(8,128)(2,1)}, u32[]{:S(2)}) copy-start(bf16[128,2048]{1,0:T(8,128)(2,1)} %query.5) | copy-start | bytes 1572868
  47.8 21.6 %copy-start.1 = (f32[128,16]{0,1:T(8,128)S(1)}, f32[128,16]{0,1:T(8,128)}, u32[]{:S(2)}) copy-start(f32[128,16]{0,1:T(8,128)} %param.13) | copy-start | bytes 24580
  47.8 7.2 %collective-permute-start.6 = (s16[32,1152]{1,0:T(8,128)(2,1)S(1)}, s16[32,1152]{1,0:T(8,128)(2,1)S(1)}, u32[]{:S(2)}, u32[]{:S(2)}) collective-permute-start(s16[32,1152]{1,0:T(8,128)(2,1)S(1)} %get-tuple-element.46), channel_id=1, source_target_pairs={{0,1},{1,0},{2,3},{3,2},{4,5},{5,4},{6,7},{7,6},{8,9},{9,8},{10,11... | collective-permute-start | bytes 221192 | tf_op jit(solution)/shard_map/ppermute | solution.py:499
  47.9 9.3 %collective-permute-start.7 = (s16[32,1152]{1,0:T(8,128)(2,1)S(1)}, s16[32,1152]{1,0:T(8,128)(2,1)S(1)}, u32[]{:S(2)}, u32[]{:S(2)}) collective-permute-start(s16[32,1152]{1,0:T(8,128)(2,1)S(1)} %get-tuple-element.47), channel_id=1, source_target_pairs={{0,2},{1,3},{2,0},{3,1},{4,6},{5,7},{6,4},{7,5},{8,10},{9,11},{10,... | collective-permute-start | bytes 221192 | tf_op jit(solution)/shard_map/ppermute | solution.py:499
  50.1 7.1 %collective-permute-start.8 = (s16[32,1152]{1,0:T(8,128)(2,1)S(1)}, s16[32,1152]{1,0:T(8,128)(2,1)S(1)}, u32[]{:S(2)}, u32[]{:S(2)}) collective-permute-start(s16[32,1152]{1,0:T(8,128)(2,1)S(1)} %get-tuple-element.48), channel_id=1, source_target_pairs={{0,3},{1,2},{2,1},{3,0},{4,7},{5,6},{6,5},{7,4},{8,11},{9,10},{10,... | collective-permute-start | bytes 221192 | tf_op jit(solution)/shard_map/ppermute | solution.py:499
  58.1 9.1 %collective-permute-start.10 = (s16[32,1152]{1,0:T(8,128)(2,1)S(1)}, s16[32,1152]{1,0:T(8,128)(2,1)S(1)}, u32[]{:S(2)}, u32[]{:S(2)}) collective-permute-start(s16[32,1152]{1,0:T(8,128)(2,1)S(1)} %get-tuple-element.53.c0), channel_id=1, source_target_pairs={{0,2},{1,3},{2,0},{3,1},{4,6},{5,7},{6,4},{7,5},{8,10},{9,11},{10,... | collective-permute-start | bytes 221192 | tf_op jit(solution)/shard_map/ppermute | solution.py:499
  60.2 7.1 %collective-permute-start.11 = (s16[32,1152]{1,0:T(8,128)(2,1)S(1)}, s16[32,1152]{1,0:T(8,128)(2,1)S(1)}, u32[]{:S(2)}, u32[]{:S(2)}) collective-permute-start(s16[32,1152]{1,0:T(8,128)(2,1)S(1)} %get-tuple-element.53.c0), channel_id=1, source_target_pairs={{0,3},{1,2},{2,1},{3,0},{4,7},{5,6},{6,5},{7,4},{8,11},{9,10},{10,... | collective-permute-start | bytes 221192 | tf_op jit(solution)/shard_map/ppermute | solution.py:499
  62.5 5.6 %collective-permute-start.9 = (s16[32,1152]{1,0:T(8,128)(2,1)S(1)}, s16[32,1152]{1,0:T(8,128)(2,1)S(1)}, u32[]{:S(2)}, u32[]{:S(2)}) collective-permute-start(s16[32,1152]{1,0:T(8,128)(2,1)S(1)} %get-tuple-element.53.c0), channel_id=1, source_target_pairs={{0,1},{1,0},{2,3},{3,2},{4,5},{5,4},{6,7},{7,6},{8,9},{9,8},{10,11... | collective-permute-start | bytes 221192 | tf_op jit(solution)/shard_map/ppermute | solution.py:499
  64.5 7.0 %collective-permute-start.12 = (s16[272,128]{1,0:T(8,128)(2,1)S(1)}, s16[272,128]{1,0:T(8,128)(2,1)S(1)}, u32[]{:S(2)}, u32[]{:S(2)}) collective-permute-start(s16[272,128]{1,0:T(8,128)(2,1)S(1)} %get-tuple-element.62), channel_id=1, source_target_pairs={{4,0},{8,4},{12,8},{16,12},{20,16},{24,20},{28,24},{5,1},{9,5},{13... | collective-permute-start | bytes 208904 | tf_op jit(solution)/shard_map/ppermute | solution.py:499
  65.8 6.8 %collective-permute-start.13 = (s16[272,128]{1,0:T(8,128)(2,1)S(1)}, s16[272,128]{1,0:T(8,128)(2,1)S(1)}, u32[]{:S(2)}, u32[]{:S(2)}) collective-permute-start(s16[272,128]{1,0:T(8,128)(2,1)S(1)} %get-tuple-element.63), channel_id=1, source_target_pairs={{8,0},{12,4},{16,8},{20,12},{24,16},{28,20},{9,1},{13,5},{17,9},{2... | collective-permute-start | bytes 208904 | tf_op jit(solution)/shard_map/ppermute | solution.py:499
  68.1 6.0 %collective-permute-start.14 = (s16[272,128]{1,0:T(8,128)(2,1)S(1)}, s16[272,128]{1,0:T(8,128)(2,1)S(1)}, u32[]{:S(2)}, u32[]{:S(2)}) collective-permute-start(s16[272,128]{1,0:T(8,128)(2,1)S(1)} %get-tuple-element.64), channel_id=1, source_target_pairs={{12,0},{16,4},{20,8},{24,12},{28,16},{13,1},{17,5},{21,9},{25,13},... | collective-permute-start | bytes 208904 | tf_op jit(solution)/shard_map/ppermute | solution.py:499
  74.2 8.9 %collective-permute-start.15 = (s16[272,128]{1,0:T(8,128)(2,1)S(1)}, s16[272,128]{1,0:T(8,128)(2,1)S(1)}, u32[]{:S(2)}, u32[]{:S(2)}) collective-permute-start(s16[272,128]{1,0:T(8,128)(2,1)S(1)} %owned_keys.1.c0), channel_id=1, source_target_pairs={{0,1},{1,0},{2,3},{3,2},{4,5},{5,4},{6,7},{7,6},{8,9},{9,8},{10,11... | collective-permute-start | bytes 208904 | tf_op jit(solution)/shard_map/ppermute | solution.py:499
  76.3 8.7 %collective-permute-start.16 = (s16[272,128]{1,0:T(8,128)(2,1)S(1)}, s16[272,128]{1,0:T(8,128)(2,1)S(1)}, u32[]{:S(2)}, u32[]{:S(2)}) collective-permute-start(s16[272,128]{1,0:T(8,128)(2,1)S(1)} %owned_keys.1.c0), channel_id=1, source_target_pairs={{0,2},{1,3},{2,0},{3,1},{4,6},{5,7},{6,4},{7,5},{8,10},{9,11},{10,... | collective-permute-start | bytes 208904 | tf_op jit(solution)/shard_map/ppermute | solution.py:499
  76.4 8.6 %collective-permute-start.17 = (s16[272,128]{1,0:T(8,128)(2,1)S(1)}, s16[272,128]{1,0:T(8,128)(2,1)S(1)}, u32[]{:S(2)}, u32[]{:S(2)}) collective-permute-start(s16[272,128]{1,0:T(8,128)(2,1)S(1)} %owned_keys.1.c0), channel_id=1, source_target_pairs={{0,3},{1,2},{2,1},{3,0},{4,7},{5,6},{6,5},{7,4},{8,11},{9,10},{10,... | collective-permute-start | bytes 208904 | tf_op jit(solution)/shard_map/ppermute | solution.py:499

commit v3 on v2

--- a/solution.py
+++ b/solution.py
@@ -265,36 +265,53 @@
             out[at:at + rows, :] = jnp.where(causal, ex, 0.0)
 
 
-def main_kernel(half, place, q, own, a, b, c, own_exp, outside, qpos, kpos, *rest):
+def block_kernel(half, q, block, out, keys):
+    rows, kb = q.shape[0], block.shape[1]
+    keys[:64, :] = jnp.zeros((64, kb), jnp.bfloat16)
+    keys[64:64 + LAT, :] = block[:LAT, :]
+    keys[64 + LAT:, :] = jnp.zeros((64, kb), jnp.bfloat16)
+    size = half * rows
+    for j in range(q.shape[1] // (half * LAT)):
+        lhs, first = chunk_rows(q, j, half)
+        out[j * size:(j + 1) * size, :] = jnp.exp2(dot(lhs, keys[first:first + 640, :]) * (SCORE_SCALE * LOG2E))
+
+
+def main_kernel(half, place, q, own, a, b, c, own_exp, b_exp, outside, qpos, kpos, *rest):
     outs, rest = rest[:GROUPS], rest[GROUPS:]
     e, inv, (keys, out_exp, mass) = rest[:BUFFERS], rest[BUFFERS:2 * BUFFERS], rest[2 * BUFFERS:]
     z, position = place[0], place[1]
     rows, kb = q.shape[0], own.shape[1]
     chunks = q.shape[1] // (half * LAT)
     window = STEPS * kb
-    front = window - kb
-    present = [jnp.where(position >= STEPS - 1 - i, 1.0, 0.0).astype(jnp.float32) for i in range(STEPS)]
+    own_slot, a_slot, b_slot, c_slot = slots_of(position)
+    slots = (a_slot, c_slot, b_slot, own_slot)
+    present = [position >= STEPS - 1 - slot for slot in slots]
+    later = 2
+    done = {later: b_exp, later + 1: own_exp}
     lane = lax.broadcasted_iota(jnp.int32, (32, 128), 1)
 
     keys[:64, :] = jnp.zeros((64, window), jnp.bfloat16)
     keys[64 + LAT:, :] = jnp.zeros((64, window), jnp.bfloat16)
-    for block, slot in zip((own, a, b, c), slots_of(position)):
-        keys[64:64 + LAT, pl.ds(pl.multiple_of(slot * kb, kb), kb)] = block[:LAT, :]
+    for i, block in enumerate((a, c, b, own)):
+        keys[64:64 + LAT, i * kb:(i + 1) * kb] = block[:LAT, :]
     out_exp[...] = jnp.exp(turned_tall(outside[...], NEGATIVE))
     mass[...] = jnp.zeros_like(mass)
     worst = [jnp.zeros((32, 1), jnp.float32)]
 
     def exp_unit(j, i, r):
         buffer, at = j % BUFFERS, i * rows + r
-        own_rows = slice(j * half * rows + at, j * half * rows + at + 32)
+        done_rows = slice(j * half * rows + at, j * half * rows + at + 32)
         head = (j - j % 2) * half + 2 * i + j % 2
         total = jnp.where(lane == head, out_exp[r:r + 32, :], 0.0)
         for block in range(STEPS):
-            piece = own_exp[own_rows, :] if block == STEPS - 1 else e[buffer][at:at + 32, block * kb:(block + 1) * kb]
+            if block in done:
+                piece = done[block][done_rows, :]
+            else:
+                piece = e[buffer][at:at + 32, block * kb:(block + 1) * kb]
             sums = piece[:, :128]
             for k in range(128, kb, 128):
                 sums = sums + piece[:, k:k + 128]
-            total = total + (sums if block == STEPS - 1 else sums * present[block])
+            total = total + (sums if block == STEPS - 1 else jnp.where(present[block], sums, 0.0))
         total = jnp.sum(total, axis=1, keepdims=True)
         inv[buffer][at:at + 32, :] = jnp.broadcast_to(1.0 / total, (32, 128))
         worst[0] = jnp.maximum(worst[0], total)
@@ -304,18 +321,18 @@
         total = mass[r:r + 32, w:w + 256]
         for i in range(half):
             at = i * rows + r
-            if w < front:
+            if w // kb in done:
+                first = j * half * rows + at
+                piece = done[w // kb][first:first + 32, w % kb:w % kb + 256]
+            else:
                 piece = e[buffer][at:at + 32, w:w + 256]
-            else:
-                first = j * half * rows + at
-                piece = own_exp[first:first + 32, w - front:w - front + 256]
             scale = inv[buffer][at:at + 32, :]
             total = total + piece * jnp.concatenate([scale, scale], 1)
         mass[r:r + 32, w:w + 256] = total
 
     exps = [(i, r) for i in range(half) for r in range(0, rows, 32)]
     sums = [(r, w) for r in range(0, rows, 32) for w in range(0, window, 256)]
-    thirds = STEPS - 1
+    thirds = later
     for j in range(chunks + 2):
         if j < chunks:
             lhs, first = chunk_rows(q, j, half)
@@ -333,10 +350,9 @@
 
     @pl.when(jnp.logical_not(jnp.max(worst[0]) < SAFE))
     def _():
-        slot = lax.broadcasted_iota(jnp.int32, (rows, window), 1) // kb
         causal = kpos[...].astype(jnp.float32) <= column(qpos[...], 0, rows)
-        causal = jnp.concatenate([jnp.ones((rows, front), jnp.float32), jnp.where(causal, 1.0, 0.0)], 1) > 0
-        visible = (position >= STEPS - 1 - slot) & causal
+        seen = [jnp.where(p, jnp.ones((rows, kb), jnp.float32), 0.0) for p in present[:STEPS - 1]]
+        visible = jnp.concatenate(seen + [jnp.where(causal, 1.0, 0.0)], 1) > 0
         line = lax.broadcasted_iota(jnp.int32, outside.shape, 0)
         mass[...] = jnp.zeros_like(mass)
         for parity in range(2):
@@ -356,9 +372,10 @@
 
             lax.fori_loop(0, outside.shape[0] // 2, exact, 0)
 
-    for block in range(STEPS - 1):
-        lanes = slice(block * kb, (block + 1) * kb)
-        mass[:, lanes] = mass[:, lanes] * present[block]
+    ordered = [mass[:, i * kb:(i + 1) * kb] for i in range(STEPS)]
+    ordered = [x if i == STEPS - 1 else jnp.where(present[i], x, 0.0) for i, x in enumerate(ordered)]
+    for slot, x in zip(slots, ordered):
+        mass[:, pl.ds(pl.multiple_of(slot * kb, kb), kb)] = x
     share = rows // GROUPS
     for d in range(GROUPS):
         at = pl.ds(pl.multiple_of((z ^ d) * share, share), share)
@@ -393,7 +410,7 @@
     score[...] = total
 
 
-def dscore_kernel(place, m0, m1, m2, m3, score, outside, qpos, kpos, spread, code):
+def dscore_kernel(place, m0, m3, m2, m1, score, outside, qpos, kpos, spread, code):
     z, position = place[0], place[1]
     share, window = score.shape
     kb = kpos.shape[1]
@@ -496,7 +513,8 @@
 
 
 def along(x, axis, route):
-    return lax.ppermute(x, axis, [(i, j) for i, j in route if 0 <= j < lax.axis_size(axis)])
+    size = lax.axis_size(axis)
+    return lax.ppermute(x, axis, [(i, j % size) for i, j in route])
 
 
 def shards(
@@ -574,17 +592,28 @@
     )(held(main_query), packed, held(qpos), held(kpos))
 
     route_b, own_exp, pieces[1], pieces[2] = lax.optimization_barrier((route_b, own_exp, pieces[1], pieces[2]))
+    b_exp = pl.pallas_call(
+        functools.partial(block_kernel, half),
+        grid=(1,),
+        in_specs=[whole(main_query), whole(route_b)],
+        out_specs=pl.BlockSpec((heads * rows, kb), lambda i: (0, 0)),
+        out_shape=shape((heads * rows, kb), f32),
+        scratch_shapes=[pltpu.VMEM((704, kb), bf16)],
+        compiler_params=params(16),
+        cost_estimate=cost(2 * heads * rows * kb * LAT, heads * rows * (2 * LAT + 4 * kb)),
+        name="next_block",
+    )(main_query, route_b)
     route_c = along(route_b, "seq", [(i, i ^ 1) for i in range(n_seq)])
     blocks = (packed, route_a, route_b, route_c)
     code_shape = (share, window + 128)
     mass = pl.pallas_call(
         functools.partial(main_kernel, half),
         grid=(1,),
-        in_specs=[SMEM] + [whole(x) for x in (main_query, *blocks, own_exp, outsides, qpos, kpos)],
+        in_specs=[SMEM] + [whole(x) for x in (main_query, *blocks, own_exp, b_exp, outsides, qpos, kpos)],
         out_specs=[pl.BlockSpec((share, window), lambda i: (0, 0))]
         + [pl.BlockSpec(code_shape, lambda i: (0, 0))] * (GROUPS - 1),
         out_shape=[shape((share, window), f32)] + [shape(code_shape, int16)] * (GROUPS - 1),
-        scratch_shapes=[pltpu.VMEM((half * rows, window - kb), f32)] * BUFFERS
+        scratch_shapes=[pltpu.VMEM((half * rows, 2 * kb), f32)] * BUFFERS
         + [pltpu.VMEM((half * rows, 128), f32)] * BUFFERS
         + [
             pltpu.VMEM((704, window), bf16),
@@ -594,7 +623,7 @@
         compiler_params=params(32),
         cost_estimate=cost(2 * heads * rows * window * LAT, heads * rows * 2 * LAT),
         name="main_mass",
-    )(place, main_query, *blocks, own_exp, outsides, qpos, kpos)
+    )(place, main_query, *blocks, own_exp, b_exp, outsides, qpos, kpos)
     masses = [mass[0]] + [exchanged(mass[d], d) for d in range(1, GROUPS)]
 
     tile = count * share
@@ -623,7 +652,7 @@
     spread, code = pl.pallas_call(
         dscore_kernel,
         grid=(1,),
-        in_specs=[SMEM] + [whole(x) for x in (*masses, score, outside, qpos, kpos)],
+        in_specs=[SMEM] + [whole(x) for x in (masses[0], *masses[:0:-1], score, outside, qpos, kpos)],
         out_specs=[
             pl.BlockSpec((2, share, window), lambda i: (0, 0, 0)),
             pl.BlockSpec(code_shape, lambda i: (0, 0)),
@@ -632,7 +661,7 @@
         compiler_params=params(16),
         cost_estimate=cost(0, 12 * share * window),
         name="dscores",
-    )(place, *masses, score, outside, qpos, kpos)
+    )(place, masses[0], *masses[:0:-1], score, outside, qpos, kpos)
     codes = [code] + [exchanged(code, d) for d in range(1, GROUPS)]
 
     sum_shape = (kb + 16, IDIM)
@@ -648,7 +677,7 @@
         name="key_grads",
     )(gate, turned, spread)
     sent = [parts[STEPS - 1 - distance] for distance in range(1, STEPS)]
-    sent[-1], *codes = lax.optimization_barrier((sent[-1], *codes))
+    sent[-1], codes[2] = lax.optimization_barrier((sent[-1], codes[2]))
     moved = [along(x, "seq", [(i, i - d - 1) for i in range(n_seq)]) for d, x in enumerate(sent)]
 
     group = count // 4

time: 86 us -> 78.9 us (0.917)
  starting transfers between devices: 30.3 us -> 23.9 us
  waiting for transfers between devices: 9.16 us -> 7.94 us
    ppermute x18, starting transfers between devices: 30.3 us -> 23.9 us  [along(): return lax.ppermute(x, axis, [(i, j % size) for i, j in route])]
    pallas_call x0 -> x1, Pallas kernels: none -> 1.8 us  [shards(): pl.pallas_call(functools.partial(block_kernel, half), grid=(1,), in_specs...]
    ppermute x18, waiting for transfers between devices: 9.16 us -> 7.94 us  [along(): return lax.ppermute(x, axis, [(i, j % size) for i, j in route])]
    pallas_call x1, Pallas kernels: 26.5 us -> 25.5 us  [shards(): pl.pallas_call(functools.partial(main_kernel, half), grid=(1,), in_specs=...]
  transfers between devices with their start and end apart: 18 -> 18, of which waited for: 7 -> 7; matrix products, arithmetic and copies ran while one was open for 0% -> 0% of each run, Pallas kernels for 48% -> 53%
where the time goes in v3:
time: 78.9 us; the launch traced here: 78.8 us
  Pallas kernels  46 us (58%)
  starting transfers between devices  23.9 us (30%)
  waiting for transfers between devices  7.94 us (10%)
  between operations  0.85 us (1%)
    pallas_call x1, Pallas kernels, shards(): pl.pallas_call(functools.partial(main_kernel, half), grid=(1,), in_specs=...  25.5 us
    ppermute x18, starting transfers between devices, along(): return lax.ppermute(x, axis, [(i, j % size) for i, j in route])  23.9 us
    ppermute x18, waiting for transfers between devices, along(): return lax.ppermute(x, axis, [(i, j % size) for i, j in route])  7.94 us
    pallas_call x2, Pallas kernels, query_grads(): pl.pallas_call(functools.partial(query_kernel, (first, last), group), gri...  6.37 us
    pallas_call x1, Pallas kernels, shards(): pl.pallas_call(functools.partial(own_kernel, half), grid=(1,), in_specs=[...  3.74 us
    pallas_call x1, Pallas kernels, shards(): pl.pallas_call(functools.partial(index_kernel, count), grid=(1,), in_spec...  2.74 us
    pallas_call x1, Pallas kernels, shards(): pl.pallas_call(pack_kernel, grid=(1,), in_specs=[SMEM] + [HBM] * 4, out_s...  2.07 us
    pallas_call x1, Pallas kernels, shards(): pl.pallas_call(functools.partial(keys_kernel, count), grid=(1,), in_specs...  1.96 us
  transfers between devices with their start and end apart: 18, of which 7 were waited for; matrix products, arithmetic and copies ran while one was open for 0% of the time, Pallas kernels for 53%

profile of v3, /device:TPU:0, one launch (start us, length us, event | category | flops | bytes accessed | tf_op | source)
XLA Modules:
  0.0 78.8 jit_solution(4113429932793692701)
XLA Ops:
  0.6 0.1 pad_add_fusion.place
  0.7 2.1 %pack_rows.1 = (bf16[704,256]{1,0:T(8,128)(2,1)S(1)}, bf16[32,2176]{1,0:T(8,128)(2,1)S(1)}, bf16[32,2176]{1,0:T(8,128)(2,1)S(1)}, bf16[32,2176]{1,0:T(8,128)(2,1)S(1)}, bf16[32,2176]{1,0:T(8,128)(2,1)S(1)}) custom-call(s32[2]{0:T(128)S(1)} %pad_add_fusion.place, bf16[576,256]{1,0:T(8,128)(2,1)} %bitcast.22, bf16[256,128]{1,0:T(8,128)(2,1)} %keys.1, ...), custom_call_target="tpu_custom_call" | custom-call | flops 1 | bytes 1 | tf_op jit(solution)/shard_map/pack_rows/pallas_call | solution.py:555
  2.8 2.4 %collective-permute-start.1 = (bf16[704,256]{1,0:T(8,128)(2,1)S(1)}, bf16[704,256]{1,0:T(8,128)(2,1)S(1)}, u32[]{:S(2)}, u32[]{:S(2)}) collective-permute-start(bf16[704,256]{1,0:T(8,128)(2,1)S(1)} %get-tuple-element.31.own), channel_id=1, source_target_pairs={{0,12},{4,8},{8,20},{12,16},{16,28},{20,24},{24,4},{28,0},{1,13},{... | collective-permute-start | bytes 1081352 | tf_op jit(solution)/shard_map/ppermute | solution.py:517
  5.2 1.6 %collective-permute-start.2 = (bf16[32,2176]{1,0:T(8,128)(2,1)S(1)}, bf16[32,2176]{1,0:T(8,128)(2,1)S(1)}, u32[]{:S(2)}, u32[]{:S(2)}) collective-permute-start(bf16[32,2176]{1,0:T(8,128)(2,1)S(1)} %get-tuple-element.32), channel_id=1, source_target_pairs={{0,1},{1,0},{2,3},{3,2},{4,5},{5,4},{6,7},{7,6},{8,9},{9,8},{10,11... | collective-permute-start | bytes 417800 | tf_op jit(solution)/shard_map/ppermute | solution.py:517
  6.8 2.6 %collective-permute-start.3 = (bf16[32,2176]{1,0:T(8,128)(2,1)S(1)}, bf16[32,2176]{1,0:T(8,128)(2,1)S(1)}, u32[]{:S(2)}, u32[]{:S(2)}) collective-permute-start(bf16[32,2176]{1,0:T(8,128)(2,1)S(1)} %get-tuple-element.33), channel_id=1, source_target_pairs={{0,2},{1,3},{2,0},{3,1},{4,6},{5,7},{6,4},{7,5},{8,10},{9,11},{10,... | collective-permute-start | bytes 417800 | tf_op jit(solution)/shard_map/ppermute | solution.py:517
  9.4 0.1 collective-permute-start
  9.5 3.7 %own_block.1.own_exp = f32[4096,256]{1,0:T(8,128)S(1)} custom-call(bf16[128,18432]{1,0:T(8,128)(2,1)} %q.5, bf16[704,256]{1,0:T(8,128)(2,1)S(1)} %get-tuple-element.31.own, s32[1,128]{1,0:T(1,128)} %bitcast.18, s32[1,256]{1,0:T(1,128)} %bitcast.15), custom_call_target="tpu_custom_call" | custom-call | flops 1 | bytes 1 | tf_op jit(solution)/shard_map/own_block/pallas_call | solution.py:577
  13.3 1.0 %collective-permute-done.2.rest_1_ = bf16[32,2176]{1,0:T(8,128)(2,1)S(1)} collective-permute-done((bf16[32,2176]{1,0:T(8,128)(2,1)S(1)}, bf16[32,2176]{1,0:T(8,128)(2,1)S(1)}, u32[]{:S(2)}, u32[]{:S(2)}) %collective-permute-start.2) | collective-permute-done | bytes 139296 | tf_op jit(solution)/shard_map/ppermute | solution.py:517
  14.3 2.4 %collective-permute-done.3.rest_2_ = bf16[32,2176]{1,0:T(8,128)(2,1)S(1)} collective-permute-done((bf16[32,2176]{1,0:T(8,128)(2,1)S(1)}, bf16[32,2176]{1,0:T(8,128)(2,1)S(1)}, u32[]{:S(2)}, u32[]{:S(2)}) %collective-permute-start.3) | collective-permute-done | bytes 139296 | tf_op jit(solution)/shard_map/ppermute | solution.py:517
  16.7 0.0 collective-permute-done.1.block.b
  16.7 0.0 copy-start.3
  16.8 0.0 copy-start.4
  16.8 2.8 %collective-permute-start.8 = (bf16[32,2176]{1,0:T(8,128)(2,1)S(1)}, bf16[32,2176]{1,0:T(8,128)(2,1)S(1)}, u32[]{:S(2)}, u32[]{:S(2)}) collective-permute-start(bf16[32,2176]{1,0:T(8,128)(2,1)S(1)} %get-tuple-element.43), channel_id=1, source_target_pairs={{0,3},{1,2},{2,1},{3,0},{4,7},{5,6},{6,5},{7,4},{8,11},{9,10},{10,... | collective-permute-start | bytes 417800 | tf_op jit(solution)/shard_map/ppermute | solution.py:517
  19.6 1.8 %next_block.1.b_exp = f32[4096,256]{1,0:T(8,128)S(1)} custom-call(bf16[128,18432]{1,0:T(8,128)(2,1)S(1)} %bitcast.10, bf16[704,256]{1,0:T(8,128)(2,1)S(1)} %collective-permute-done.1.block.b), custom_call_target="tpu_custom_call" | custom-call | flops 1 | bytes 1 | tf_op jit(solution)/shard_map/next_block/pallas_call | solution.py:595
  21.4 0.0 collective-permute-done.4.c
  21.5 0.0 copy-start.5
  21.5 25.5 %main_mass.1 = (f32[32,1024]{1,0:T(8,128)S(1)}, s16[32,1152]{1,0:T(8,128)(2,1)S(1)}, s16[32,1152]{1,0:T(8,128)(2,1)S(1)}, s16[32,1152]{1,0:T(8,128)(2,1)S(1)}) custom-call(s32[2]{0:T(128)S(1)} %pad_add_fusion.place, bf16[128,18432]{1,0:T(8,128)(2,1)S(1)} %bitcast.10, bf16[704,256]{1,0:T(8,128)(2,1)S(1)} %get-tuple-element.31.own, ...), custom_call_target="tpu_custom_call" | custom-call | flops 1 | bytes 1 | tf_op jit(solution)/shard_map/main_mass/pallas_call | solution.py:609
  47.0 0.0 copy-start
  47.0 0.0 copy-start.1
  47.0 2.0 %collective-permute-start.5 = (s16[32,1152]{1,0:T(8,128)(2,1)S(1)}, s16[32,1152]{1,0:T(8,128)(2,1)S(1)}, u32[]{:S(2)}, u32[]{:S(2)}) collective-permute-start(s16[32,1152]{1,0:T(8,128)(2,1)S(1)} %get-tuple-element.37), channel_id=1, source_target_pairs={{0,3},{1,2},{2,1},{3,0},{4,7},{5,6},{6,5},{7,4},{8,11},{9,10},{10,... | collective-permute-start | bytes 221192 | tf_op jit(solution)/shard_map/ppermute | solution.py:517
  49.0 0.0 collective-permute-start.6
  49.0 2.4 %collective-permute-start.7 = (s16[32,1152]{1,0:T(8,128)(2,1)S(1)}, s16[32,1152]{1,0:T(8,128)(2,1)S(1)}, u32[]{:S(2)}, u32[]{:S(2)}) collective-permute-start(s16[32,1152]{1,0:T(8,128)(2,1)S(1)} %get-tuple-element.39), channel_id=1, source_target_pairs={{0,1},{1,0},{2,3},{3,2},{4,5},{5,4},{6,7},{7,6},{8,9},{9,8},{10,11... | collective-permute-start | bytes 221192 | tf_op jit(solution)/shard_map/ppermute | solution.py:517
  51.5 0.0 collective-permute-done.8.rest_3_
  51.5 2.7 %index_scores.1 = (f32[32,1024]{1,0:T(8,128)S(1)}, bf16[2048,1024]{1,0:T(8,128)(2,1)S(1)}, bf16[256,2048]{1,0:T(8,128)(2,1)S(1)}) custom-call(s32[2]{0:T(128)S(1)} %pad_add_fusion.place, bf16[128,256]{1,0:T(8,128)(2,1)S(1)} %slice.12.own, bf16[128,256]{1,0:T(8,128)(2,1)S(1)} %slice.16.a, bf16[128,256]{1,0:T(8,128)(2,1)S(1)} %slice.14.b, ...), custom_call_target="tpu_custom_call" | custom-call | flops 1 | bytes 1 | tf_op jit(solution)/shard_map/index_scores/pallas_call | solution.py:632
  54.3 2.0 %collective-permute-done.6.m2 = s16[32,1152]{1,0:T(8,128)(2,1)S(1)} collective-permute-done((s16[32,1152]{1,0:T(8,128)(2,1)S(1)}, s16[32,1152]{1,0:T(8,128)(2,1)S(1)}, u32[]{:S(2)}, u32[]{:S(2)}) %collective-permute-start.6) | collective-permute-done | bytes 73760 | tf_op jit(solution)/shard_map/ppermute | solution.py:517
  56.3 1.0 %dscores.1 = (bf16[2,32,1024]{2,1,0:T(8,128)(2,1)S(1)}, s16[32,1152]{1,0:T(8,128)(2,1)S(1)}) custom-call(s32[2]{0:T(128)S(1)} %pad_add_fusion.place, f32[32,1024]{1,0:T(8,128)S(1)} %get-tuple-element.36.m0, s16[32,1152]{1,0:T(8,128)(2,1)S(1)} %collective-permute-done.5.m3, s16[32,1152]{1,0:T(8,128)(2,1)S(1)} %collective-permute-done.6.m2, ...), custom_call_target="tpu_custom_call" | custom-call | flops 1 | bytes 1 | tf_op jit(solution)/shard_map/dscores/pallas_call | solution.py:652
  57.2 0.8 collective-permute-start.10
  58.0 1.6 %collective-permute-start.11 = (s16[32,1152]{1,0:T(8,128)(2,1)S(1)}, s16[32,1152]{1,0:T(8,128)(2,1)S(1)}, u32[]{:S(2)}, u32[]{:S(2)}) collective-permute-start(s16[32,1152]{1,0:T(8,128)(2,1)S(1)} %get-tuple-element.45.c0), channel_id=1, source_target_pairs={{0,3},{1,2},{2,1},{3,0},{4,7},{5,6},{6,5},{7,4},{8,11},{9,10},{10,... | collective-permute-start | bytes 221192 | tf_op jit(solution)/shard_map/ppermute | solution.py:517
  59.6 1.2 %collective-permute-start.9 = (s16[32,1152]{1,0:T(8,128)(2,1)S(1)}, s16[32,1152]{1,0:T(8,128)(2,1)S(1)}, u32[]{:S(2)}, u32[]{:S(2)}) collective-permute-start(s16[32,1152]{1,0:T(8,128)(2,1)S(1)} %get-tuple-element.45.c0), channel_id=1, source_target_pairs={{0,1},{1,0},{2,3},{3,2},{4,5},{5,4},{6,7},{7,6},{8,9},{9,8},{10,11... | collective-permute-start | bytes 221192 | tf_op jit(solution)/shard_map/ppermute | solution.py:517
  60.8 2.0 %key_grads.1 = (s16[272,128]{1,0:T(8,128)(2,1)S(1)}, s16[272,128]{1,0:T(8,128)(2,1)S(1)}, s16[272,128]{1,0:T(8,128)(2,1)S(1)}, f32[256,128]{1,0:T(8,128)S(1)}) custom-call(bf16[2048,1024]{1,0:T(8,128)(2,1)S(1)} %get-tuple-element.46.gate, bf16[256,2048]{1,0:T(8,128)(2,1)S(1)} %get-tuple-element.47.turned, bf16[2,32,1024]{2,1,0:T(8,128)(2,1)S(1)} %get-tuple-element.48.spread), custom_call_target="tpu_custom_call" | custom-call | flops 1 | bytes 1 | tf_op jit(solution)/shard_map/key_grads/pallas_call | solution.py:668
  62.7 0.1 collective-permute-start.12
  62.8 1.5 %collective-permute-start.13 = (s16[272,128]{1,0:T(8,128)(2,1)S(1)}, s16[272,128]{1,0:T(8,128)(2,1)S(1)}, u32[]{:S(2)}, u32[]{:S(2)}) collective-permute-start(s16[272,128]{1,0:T(8,128)(2,1)S(1)} %get-tuple-element.57), channel_id=1, source_target_pairs={{0,24},{4,28},{8,0},{12,4},{16,8},{20,12},{24,16},{28,20},{1,25},{... | collective-permute-start | bytes 208904 | tf_op jit(solution)/shard_map/ppermute | solution.py:517
  64.4 0.8 %collective-permute-done.10.c2 = s16[32,1152]{1,0:T(8,128)(2,1)S(1)} collective-permute-done((s16[32,1152]{1,0:T(8,128)(2,1)S(1)}, s16[32,1152]{1,0:T(8,128)(2,1)S(1)}, u32[]{:S(2)}, u32[]{:S(2)}) %collective-permute-start.10) | collective-permute-done | bytes 73760 | tf_op jit(solution)/shard_map/ppermute | solution.py:517
  65.2 0.3 collective-permute-start.14
  65.4 0.0 collective-permute-done.11.c3
  65.4 0.0 collective-permute-done.9.c1
  65.4 2.0 %query_grads.2 = (bf16[128,2048]{1,0:T(8,128)(2,1)S(1)}, f32[128,128]{1,0:T(8,128)S(1)}) custom-call(s32[2]{0:T(128)S(1)} %pad_add_fusion.place, bf16[128,256]{1,0:T(8,128)(2,1)S(1)} %slice.12.own, bf16[128,256]{1,0:T(8,128)(2,1)S(1)} %slice.16.a, bf16[128,256]{1,0:T(8,128)(2,1)S(1)} %slice.14.b, bf16[128,256]{1,0:T(8,128)(2,1)S(1)} %slice.17.c, ...), custom_call_target="tpu_custom_call" | custom-call | flops 1 | bytes 1 | tf_op jit(solution)/shard_map/query_grads/pallas_call | solution.py:687
  67.4 0.5 collective-permute-done.13.c2
  67.9 1.0 %collective-permute-done.14.c3 = s16[272,128]{1,0:T(8,128)(2,1)S(1)} collective-permute-done((s16[272,128]{1,0:T(8,128)(2,1)S(1)}, s16[272,128]{1,0:T(8,128)(2,1)S(1)}, u32[]{:S(2)}, u32[]{:S(2)}) %collective-permute-start.14) | collective-permute-done | bytes 69664 | tf_op jit(solution)/shard_map/ppermute | solution.py:517
  68.9 0.1 owned_keys.1.c0
  69.0 2.0 %collective-permute-start.17 = (s16[272,128]{1,0:T(8,128)(2,1)S(1)}, s16[272,128]{1,0:T(8,128)(2,1)S(1)}, u32[]{:S(2)}, u32[]{:S(2)}) collective-permute-start(s16[272,128]{1,0:T(8,128)(2,1)S(1)} %owned_keys.1.c0), channel_id=1, source_target_pairs={{0,3},{1,2},{2,1},{3,0},{4,7},{5,6},{6,5},{7,4},{8,11},{9,10},{10,... | collective-permute-start | bytes 208904 | tf_op jit(solution)/shard_map/ppermute | solution.py:517
  71.1 0.0 collective-permute-start.16
  71.1 2.4 %collective-permute-start.15 = (s16[272,128]{1,0:T(8,128)(2,1)S(1)}, s16[272,128]{1,0:T(8,128)(2,1)S(1)}, u32[]{:S(2)}, u32[]{:S(2)}) collective-permute-start(s16[272,128]{1,0:T(8,128)(2,1)S(1)} %owned_keys.1.c0), channel_id=1, source_target_pairs={{0,1},{1,0},{2,3},{3,2},{4,5},{5,4},{6,7},{7,6},{8,9},{9,8},{10,11... | collective-permute-start | bytes 208904 | tf_op jit(solution)/shard_map/ppermute | solution.py:517
  73.5 4.4 %query_grads.3 = (bf16[128,2048]{1,0:T(8,128)(2,1)}, f32[16,128]{1,0:T(8,128)}) custom-call(s32[2]{0:T(128)S(1)} %pad_add_fusion.place, bf16[128,256]{1,0:T(8,128)(2,1)S(1)} %slice.12.own, bf16[128,256]{1,0:T(8,128)(2,1)S(1)} %slice.16.a, bf16[128,256]{1,0:T(8,128)(2,1)S(1)} %slice.14.b, bf16[128,256]{1,0:T(8,128)(2,1)S(1)} %slice.17.c, ...), custom_call_target="tpu_custom_call" | custom-call | flops 1 | bytes 1 | tf_op jit(solution)/shard_map/query_grads/pallas_call | solution.py:687
  77.9 0.0 collective-permute-done.17.c3
  77.9 0.2 collective-permute-done.16.c2
  78.1 0.0 collective-permute-done.15.c1
  78.1 0.7 total_keys.1
  (21 shorter events, 0.1 us)
Async XLA Ops:
  0.7 18.9 %slice-start = ((s8[4718592]{0:T(1024)(128)(4,1)}), s8[4194304]{0:T(1024)(128)(4,1)S(1)}, s32[]{:S(2)}) async-start(s8[4718592]{0:T(1024)(128)(4,1)} %bitcast.9), calls=%async_computation | async-start | bytes 8388608
  2.8 13.9 %collective-permute-start.1 = (bf16[704,256]{1,0:T(8,128)(2,1)S(1)}, bf16[704,256]{1,0:T(8,128)(2,1)S(1)}, u32[]{:S(2)}, u32[]{:S(2)}) collective-permute-start(bf16[704,256]{1,0:T(8,128)(2,1)S(1)} %get-tuple-element.31.own), channel_id=1, source_target_pairs={{0,12},{4,8},{8,20},{12,16},{16,28},{20,24},{24,4},{28,0},{1,13},{... | collective-permute-start | bytes 1081352 | tf_op jit(solution)/shard_map/ppermute | solution.py:517
  5.2 9.1 %collective-permute-start.2 = (bf16[32,2176]{1,0:T(8,128)(2,1)S(1)}, bf16[32,2176]{1,0:T(8,128)(2,1)S(1)}, u32[]{:S(2)}, u32[]{:S(2)}) collective-permute-start(bf16[32,2176]{1,0:T(8,128)(2,1)S(1)} %get-tuple-element.32), channel_id=1, source_target_pairs={{0,1},{1,0},{2,3},{3,2},{4,5},{5,4},{6,7},{7,6},{8,9},{9,8},{10,11... | collective-permute-start | bytes 417800 | tf_op jit(solution)/shard_map/ppermute | solution.py:517
  6.8 9.9 %collective-permute-start.3 = (bf16[32,2176]{1,0:T(8,128)(2,1)S(1)}, bf16[32,2176]{1,0:T(8,128)(2,1)S(1)}, u32[]{:S(2)}, u32[]{:S(2)}) collective-permute-start(bf16[32,2176]{1,0:T(8,128)(2,1)S(1)} %get-tuple-element.33), channel_id=1, source_target_pairs={{0,2},{1,3},{2,0},{3,1},{4,6},{5,7},{6,4},{7,5},{8,10},{9,11},{10,... | collective-permute-start | bytes 417800 | tf_op jit(solution)/shard_map/ppermute | solution.py:517
  9.4 12.0 %collective-permute-start = (bf16[704,256]{1,0:T(8,128)(2,1)S(1)}, bf16[704,256]{1,0:T(8,128)(2,1)S(1)}, u32[]{:S(2)}, u32[]{:S(2)}) collective-permute-start(bf16[704,256]{1,0:T(8,128)(2,1)S(1)} %get-tuple-element.31.own), channel_id=1, source_target_pairs={{0,4},{4,16},{8,12},{12,24},{16,20},{20,0},{24,28},{28,8},{1,5},{5... | collective-permute-start | bytes 1081352 | tf_op jit(solution)/shard_map/ppermute | solution.py:517
  9.5 10.1 %slice-start.1 = ((s8[4718592]{0:T(1024)(128)(4,1)}), s8[524288]{0:T(1024)(128)(4,1)S(1)}, s32[]{:S(2)}) async-start(s8[4718592]{0:T(1024)(128)(4,1)} %bitcast.9), calls=%async_computation.1 | async-start | bytes 1048576
  16.7 4.7 %collective-permute-start.4 = (bf16[704,256]{1,0:T(8,128)(2,1)S(1)}, bf16[704,256]{1,0:T(8,128)(2,1)S(1)}, u32[]{:S(2)}, u32[]{:S(2)}) collective-permute-start(bf16[704,256]{1,0:T(8,128)(2,1)S(1)} %collective-permute-done.1.block.b), channel_id=1, source_target_pairs={{0,4},{4,0},{8,12},{12,8},{16,20},{20,16},{24,28},{28,24},{1,5},{5... | collective-permute-start | bytes 1081352 | tf_op jit(solution)/shard_map/ppermute | solution.py:517
  16.7 4.7 %copy-start.2 = (f32[128,32]{0,1:T(8,128)S(1)}, f32[128,32]{0,1:T(8,128)}, u32[]{:S(2)}) copy-start(f32[128,32]{0,1:T(8,128)} %param.11) | copy-start | bytes 49156
  16.7 4.7 %copy-start.3 = (s32[256]{0:T(256)S(1)}, s32[256]{0:T(256)}, u32[]{:S(2)}) copy-start(s32[256]{0:T(256)} %param.17) | copy-start | bytes 3076
  16.8 4.7 %copy-start.4 = (s32[128]{0:T(128)S(1)}, s32[128]{0:T(128)}, u32[]{:S(2)}) copy-start(s32[128]{0:T(128)} %param.16) | copy-start | bytes 1540
  16.8 34.7 %collective-permute-start.8 = (bf16[32,2176]{1,0:T(8,128)(2,1)S(1)}, bf16[32,2176]{1,0:T(8,128)(2,1)S(1)}, u32[]{:S(2)}, u32[]{:S(2)}) collective-permute-start(bf16[32,2176]{1,0:T(8,128)(2,1)S(1)} %get-tuple-element.43), channel_id=1, source_target_pairs={{0,3},{1,2},{2,1},{3,0},{4,7},{5,6},{6,5},{7,4},{8,11},{9,10},{10,... | collective-permute-start | bytes 417800 | tf_op jit(solution)/shard_map/ppermute | solution.py:517
  21.5 34.8 %copy-start.5 = (f32[128]{0:T(128)S(1)}, f32[128]{0:T(128)}, u32[]{:S(2)}) copy-start(f32[128]{0:T(128)} %param.15) | copy-start | bytes 1540
  47.0 18.4 %copy-start = (bf16[128,2048]{1,0:T(8,128)(2,1)S(1)}, bf16[128,2048]{1,0:T(8,128)(2,1)}, u32[]{:S(2)}) copy-start(bf16[128,2048]{1,0:T(8,128)(2,1)} %query.5) | copy-start | bytes 1572868
  47.0 18.4 %copy-start.1 = (f32[128,16]{0,1:T(8,128)S(1)}, f32[128,16]{0,1:T(8,128)}, u32[]{:S(2)}) copy-start(f32[128,16]{0,1:T(8,128)} %param.13) | copy-start | bytes 24580
  47.0 7.3 %collective-permute-start.5 = (s16[32,1152]{1,0:T(8,128)(2,1)S(1)}, s16[32,1152]{1,0:T(8,128)(2,1)S(1)}, u32[]{:S(2)}, u32[]{:S(2)}) collective-permute-start(s16[32,1152]{1,0:T(8,128)(2,1)S(1)} %get-tuple-element.37), channel_id=1, source_target_pairs={{0,3},{1,2},{2,1},{3,0},{4,7},{5,6},{6,5},{7,4},{8,11},{9,10},{10,... | collective-permute-start | bytes 221192 | tf_op jit(solution)/shard_map/ppermute | solution.py:517
  49.0 7.2 %collective-permute-start.6 = (s16[32,1152]{1,0:T(8,128)(2,1)S(1)}, s16[32,1152]{1,0:T(8,128)(2,1)S(1)}, u32[]{:S(2)}, u32[]{:S(2)}) collective-permute-start(s16[32,1152]{1,0:T(8,128)(2,1)S(1)} %get-tuple-element.38), channel_id=1, source_target_pairs={{0,2},{1,3},{2,0},{3,1},{4,6},{5,7},{6,4},{7,5},{8,10},{9,11},{10,... | collective-permute-start | bytes 221192 | tf_op jit(solution)/shard_map/ppermute | solution.py:517
  49.0 7.2 %collective-permute-start.7 = (s16[32,1152]{1,0:T(8,128)(2,1)S(1)}, s16[32,1152]{1,0:T(8,128)(2,1)S(1)}, u32[]{:S(2)}, u32[]{:S(2)}) collective-permute-start(s16[32,1152]{1,0:T(8,128)(2,1)S(1)} %get-tuple-element.39), channel_id=1, source_target_pairs={{0,1},{1,0},{2,3},{3,2},{4,5},{5,4},{6,7},{7,6},{8,9},{9,8},{10,11... | collective-permute-start | bytes 221192 | tf_op jit(solution)/shard_map/ppermute | solution.py:517
  57.2 7.9 %collective-permute-start.10 = (s16[32,1152]{1,0:T(8,128)(2,1)S(1)}, s16[32,1152]{1,0:T(8,128)(2,1)S(1)}, u32[]{:S(2)}, u32[]{:S(2)}) collective-permute-start(s16[32,1152]{1,0:T(8,128)(2,1)S(1)} %get-tuple-element.45.c0), channel_id=1, source_target_pairs={{0,2},{1,3},{2,0},{3,1},{4,6},{5,7},{6,4},{7,5},{8,10},{9,11},{10,... | collective-permute-start | bytes 221192 | tf_op jit(solution)/shard_map/ppermute | solution.py:517
  58.0 7.4 %collective-permute-start.11 = (s16[32,1152]{1,0:T(8,128)(2,1)S(1)}, s16[32,1152]{1,0:T(8,128)(2,1)S(1)}, u32[]{:S(2)}, u32[]{:S(2)}) collective-permute-start(s16[32,1152]{1,0:T(8,128)(2,1)S(1)} %get-tuple-element.45.c0), channel_id=1, source_target_pairs={{0,3},{1,2},{2,1},{3,0},{4,7},{5,6},{6,5},{7,4},{8,11},{9,10},{10,... | collective-permute-start | bytes 221192 | tf_op jit(solution)/shard_map/ppermute | solution.py:517
  59.6 5.9 %collective-permute-start.9 = (s16[32,1152]{1,0:T(8,128)(2,1)S(1)}, s16[32,1152]{1,0:T(8,128)(2,1)S(1)}, u32[]{:S(2)}, u32[]{:S(2)}) collective-permute-start(s16[32,1152]{1,0:T(8,128)(2,1)S(1)} %get-tuple-element.45.c0), channel_id=1, source_target_pairs={{0,1},{1,0},{2,3},{3,2},{4,5},{5,4},{6,7},{7,6},{8,9},{9,8},{10,11... | collective-permute-start | bytes 221192 | tf_op jit(solution)/shard_map/ppermute | solution.py:517
  62.7 4.7 %collective-permute-start.12 = (s16[272,128]{1,0:T(8,128)(2,1)S(1)}, s16[272,128]{1,0:T(8,128)(2,1)S(1)}, u32[]{:S(2)}, u32[]{:S(2)}) collective-permute-start(s16[272,128]{1,0:T(8,128)(2,1)S(1)} %get-tuple-element.56), channel_id=1, source_target_pairs={{0,28},{4,0},{8,4},{12,8},{16,12},{20,16},{24,20},{28,24},{1,29},{... | collective-permute-start | bytes 208904 | tf_op jit(solution)/shard_map/ppermute | solution.py:517
  62.8 5.1 %collective-permute-start.13 = (s16[272,128]{1,0:T(8,128)(2,1)S(1)}, s16[272,128]{1,0:T(8,128)(2,1)S(1)}, u32[]{:S(2)}, u32[]{:S(2)}) collective-permute-start(s16[272,128]{1,0:T(8,128)(2,1)S(1)} %get-tuple-element.57), channel_id=1, source_target_pairs={{0,24},{4,28},{8,0},{12,4},{16,8},{20,12},{24,16},{28,20},{1,25},{... | collective-permute-start | bytes 208904 | tf_op jit(solution)/shard_map/ppermute | solution.py:517
  65.2 3.7 %collective-permute-start.14 = (s16[272,128]{1,0:T(8,128)(2,1)S(1)}, s16[272,128]{1,0:T(8,128)(2,1)S(1)}, u32[]{:S(2)}, u32[]{:S(2)}) collective-permute-start(s16[272,128]{1,0:T(8,128)(2,1)S(1)} %get-tuple-element.58), channel_id=1, source_target_pairs={{0,20},{4,24},{8,28},{12,0},{16,4},{20,8},{24,12},{28,16},{1,21},{... | collective-permute-start | bytes 208904 | tf_op jit(solution)/shard_map/ppermute | solution.py:517
  69.0 8.8 %collective-permute-start.17 = (s16[272,128]{1,0:T(8,128)(2,1)S(1)}, s16[272,128]{1,0:T(8,128)(2,1)S(1)}, u32[]{:S(2)}, u32[]{:S(2)}) collective-permute-start(s16[272,128]{1,0:T(8,128)(2,1)S(1)} %owned_keys.1.c0), channel_id=1, source_target_pairs={{0,3},{1,2},{2,1},{3,0},{4,7},{5,6},{6,5},{7,4},{8,11},{9,10},{10,... | collective-permute-start | bytes 208904 | tf_op jit(solution)/shard_map/ppermute | solution.py:517
  71.1 7.0 %collective-permute-start.16 = (s16[272,128]{1,0:T(8,128)(2,1)S(1)}, s16[272,128]{1,0:T(8,128)(2,1)S(1)}, u32[]{:S(2)}, u32[]{:S(2)}) collective-permute-start(s16[272,128]{1,0:T(8,128)(2,1)S(1)} %owned_keys.1.c0), channel_id=1, source_target_pairs={{0,2},{1,3},{2,0},{3,1},{4,6},{5,7},{6,4},{7,5},{8,10},{9,11},{10,... | collective-permute-start | bytes 208904 | tf_op jit(solution)/shard_map/ppermute | solution.py:517
  71.1 7.0 %collective-permute-start.15 = (s16[272,128]{1,0:T(8,128)(2,1)S(1)}, s16[272,128]{1,0:T(8,128)(2,1)S(1)}, u32[]{:S(2)}, u32[]{:S(2)}) collective-permute-start(s16[272,128]{1,0:T(8,128)(2,1)S(1)} %owned_keys.1.c0), channel_id=1, source_target_pairs={{0,1},{1,0},{2,3},{3,2},{4,5},{5,4},{6,7},{7,6},{8,9},{9,8},{10,11... | collective-permute-start | bytes 208904 | tf_op jit(solution)/shard_map/ppermute | solution.py:517

commit v4 on v3

--- a/solution.py
+++ b/solution.py
@@ -182,36 +182,33 @@
     return 3, jnp.where(even, 0, 2), jnp.where(even, 2, 0), 1
 
 
-def gathered(position, blocks, kept, first):
+def gathered(position, blocks, kept):
     kb = blocks[0].shape[1]
     for block, slot in zip(blocks, slots_of(position)):
         at = pl.ds(pl.multiple_of(slot * kb, kb), kb)
-        kept[first:first + block.shape[0], at] = block[...]
-
-
-def heads_at(q, parity):
-    starts = [1152 * i + 512 * parity for i in range(q.shape[1] // 1152)]
-    return jnp.concatenate([q[:, s:s + 640] for s in starts], 0)
-
-
-def pack_kernel(place, latent, keys, query, weight, packed, *rest):
-    outs, (kept, keys_here, weight_here, sems) = rest[:GROUPS], rest[GROUPS:]
+        kept[:, at] = block[block.shape[0] - IDIM:, :]
+
+
+def pack_kernel(place, latent, keys, query, weight, packed, turned_keys, *rest):
+    outs, (kept, weight_here, keys_here, sems) = rest[:GROUPS], rest[GROUPS:]
     share = outs[0].shape[0]
     width, count = query.shape[1], weight.shape[0]
     copies = [
-        pltpu.make_async_copy(latent, packed.at[pl.ds(0, LAT), :], sems.at[0]),
-        pltpu.make_async_copy(keys, keys_here, sems.at[1]),
-        pltpu.make_async_copy(weight, weight_here, sems.at[2]),
+        pltpu.make_async_copy(weight, weight_here, sems.at[GROUPS]),
+        pltpu.make_async_copy(keys, keys_here, sems.at[GROUPS + 1]),
+        pltpu.make_async_copy(latent, packed.at[pl.ds(0, LAT), :], sems.at[GROUPS + 2]),
     ]
     for d in range(GROUPS):
         at = pl.ds(pl.multiple_of((place[0] ^ d) * share, share), share)
         here = outs[d].at[:, pl.ds(0, width)]
-        copies.append(pltpu.make_async_copy(query.at[at, :], here, sems.at[3 + d]))
+        copies.append(pltpu.make_async_copy(query.at[at, :], here, sems.at[d]))
     for copy in copies:
         copy.start()
     copies[1].wait()
-    packed[LAT:, :] = keys_here[...].T
-    copies[2].wait()
+    turned = keys_here[...].T
+    packed[LAT:, :] = turned
+    turned_keys[...] = turned
+    copies[0].wait()
     tall = turned_tall(weight_here[...])[:, :count]
     high = tall.astype(jnp.bfloat16)
     middle, low = split(tall - high.astype(jnp.float32))
@@ -219,8 +216,7 @@
     for d in range(GROUPS):
         at = pl.ds(pl.multiple_of((place[0] ^ d) * share, share), share)
         outs[d][:, width:] = kept[at, :]
-    copies[0].wait()
-    for copy in copies[3:]:
+    for copy in copies[2:]:
         copy.wait()
 
 
@@ -292,7 +288,7 @@
 
     keys[:64, :] = jnp.zeros((64, window), jnp.bfloat16)
     keys[64 + LAT:, :] = jnp.zeros((64, window), jnp.bfloat16)
-    for i, block in enumerate((a, c, b, own)):
+    for i, block in enumerate((a, c)):
         keys[64:64 + LAT, i * kb:(i + 1) * kb] = block[:LAT, :]
     out_exp[...] = jnp.exp(turned_tall(outside[...], NEGATIVE))
     mass[...] = jnp.zeros_like(mass)
@@ -318,20 +314,20 @@
 
     def mass_unit(j, r, w):
         buffer = j % BUFFERS
-        total = mass[r:r + 32, w:w + 256]
+        total = mass[r:r + 32, w:w + 2 * kb]
         for i in range(half):
             at = i * rows + r
             if w // kb in done:
                 first = j * half * rows + at
-                piece = done[w // kb][first:first + 32, w % kb:w % kb + 256]
+                piece = jnp.concatenate([done[w // kb + k][first:first + 32, :] for k in range(2)], 1)
             else:
-                piece = e[buffer][at:at + 32, w:w + 256]
+                piece = e[buffer][at:at + 32, :]
             scale = inv[buffer][at:at + 32, :]
-            total = total + piece * jnp.concatenate([scale, scale], 1)
-        mass[r:r + 32, w:w + 256] = total
+            total = total + piece * jnp.concatenate([scale] * (2 * kb // 128), 1)
+        mass[r:r + 32, w:w + 2 * kb] = total
 
     exps = [(i, r) for i in range(half) for r in range(0, rows, 32)]
-    sums = [(r, w) for r in range(0, rows, 32) for w in range(0, window, 256)]
+    sums = [(r, w) for r in range(0, rows, 32) for w in range(0, window, 2 * kb)]
     thirds = later
     for j in range(chunks + 2):
         if j < chunks:
@@ -350,6 +346,8 @@
 
     @pl.when(jnp.logical_not(jnp.max(worst[0]) < SAFE))
     def _():
+        for i, block in enumerate((b, own)):
+            keys[64:64 + LAT, (later + i) * kb:(later + i + 1) * kb] = block[:LAT, :]
         causal = kpos[...].astype(jnp.float32) <= column(qpos[...], 0, rows)
         seen = [jnp.where(p, jnp.ones((rows, kb), jnp.float32), 0.0) for p in present[:STEPS - 1]]
         visible = jnp.concatenate(seen + [jnp.where(causal, 1.0, 0.0)], 1) > 0
@@ -393,7 +391,7 @@
     pieces, (score, gate, turned, keys) = rest[:GROUPS], rest[GROUPS:]
     share = score.shape[0]
     tile = count * share
-    gathered(place[1], (own, a, b, c), keys, 0)
+    gathered(place[1], (own, a, b, c), keys)
     total = jnp.zeros(score.shape, jnp.float32)
     for d in range(GROUPS):
         piece = pieces[d][...]
@@ -455,7 +453,7 @@
     grad, out, keys, turned, high, low, scale, tall = rest
     share, rows = c0.shape[0], query.shape[0]
     window = keys.shape[1]
-    gathered(place[1], (own, a, b, c), keys, 0)
+    gathered(place[1], (own, a, b, c), keys)
     turned[...] = keys[...].T
     for d, code in enumerate((c0, c1, c2, c3)):
         at = pl.ds(pl.multiple_of((place[0] ^ d) * share, share), share)
@@ -551,26 +549,31 @@
     kpos = key_pos.reshape(1, kb)
     outside = index_outside.reshape(1, rows)
     piece_shape = (share, IDIM * count + 128)
-    pack_shape = (LAT + IDIM, kb)
-    packed, *mine = pl.pallas_call(
+    packed = latent.T
+    to_b = [(i, i + (3 if i % 2 == 0 else 1)) for i in range(n_seq)]
+    to_a = [(i, i + (1 if i % 2 == 0 else 3)) for i in range(n_seq)]
+    to_c = [(i, i ^ 1) for i in range(n_seq)]
+    route_b = along(packed, "seq", to_b)
+    turned_shape = (IDIM, kb)
+    both_shape = (LAT + IDIM, kb)
+    both, turned_keys, *mine = pl.pallas_call(
         pack_kernel,
         grid=(1,),
         in_specs=[SMEM] + [HBM] * 4,
-        out_specs=[pl.BlockSpec(pack_shape, lambda i: (0, 0))]
+        out_specs=[pl.BlockSpec(both_shape, lambda i: (0, 0)), pl.BlockSpec(turned_shape, lambda i: (0, 0))]
         + [pl.BlockSpec(piece_shape, lambda i: (0, 0))] * GROUPS,
-        out_shape=[shape(pack_shape, bf16)] + [shape(piece_shape, bf16)] * GROUPS,
+        out_shape=[shape(both_shape, bf16), shape(turned_shape, bf16)] + [shape(piece_shape, bf16)] * GROUPS,
         scratch_shapes=[
             pltpu.VMEM((rows, 128), bf16),
+            pltpu.VMEM((count, rows), f32),
             pltpu.VMEM((kb, IDIM), bf16),
-            pltpu.VMEM((count, rows), f32),
-            pltpu.SemaphoreType.DMA((3 + GROUPS,)),
+            pltpu.SemaphoreType.DMA((GROUPS + 3,)),
         ],
         compiler_params=params(16),
         cost_estimate=cost(0, 4 * rows * count * IDIM),
         name="pack_rows",
-    )(place, *[held(x) for x in (latent.T, index_keys, index_query, weights)])
-    route_b = along(packed, "seq", [(i, i + (3 if i % 2 == 0 else 1)) for i in range(n_seq)])
-    route_a = along(packed, "seq", [(i, i + (1 if i % 2 == 0 else 3)) for i in range(n_seq)])
+    )(place, *[held(x) for x in (packed, index_keys, index_query, weights)])
+    route_a = along(both, "seq", to_a)
     pieces = [mine[0]] + [exchanged(mine[d], d) for d in range(1, GROUPS)]
 
     half = PER_STEP // 2
@@ -591,7 +594,7 @@
         name="own_block",
     )(held(main_query), packed, held(qpos), held(kpos))
 
-    route_b, own_exp, pieces[1], pieces[2] = lax.optimization_barrier((route_b, own_exp, pieces[1], pieces[2]))
+    route_b, own_exp, pieces[1] = lax.optimization_barrier((route_b, own_exp, pieces[1]))
     b_exp = pl.pallas_call(
         functools.partial(block_kernel, half),
         grid=(1,),
@@ -603,8 +606,11 @@
         cost_estimate=cost(2 * heads * rows * kb * LAT, heads * rows * (2 * LAT + 4 * kb)),
         name="next_block",
     )(main_query, route_b)
-    route_c = along(route_b, "seq", [(i, i ^ 1) for i in range(n_seq)])
+    route_c = along(route_b, "seq", to_c)
     blocks = (packed, route_a, route_b, route_c)
+    sent_keys, b_exp = lax.optimization_barrier((turned_keys, b_exp))
+    keys_b = along(sent_keys, "seq", to_b)
+    key_rows = (turned_keys, route_a, keys_b, along(keys_b, "seq", to_c))
     code_shape = (share, window + 128)
     mass = pl.pallas_call(
         functools.partial(main_kernel, half),
@@ -627,12 +633,10 @@
     masses = [mass[0]] + [exchanged(mass[d], d) for d in range(1, GROUPS)]
 
     tile = count * share
-    key_spec = pl.BlockSpec((IDIM, kb), lambda i: (0, 0))
-    key_rows = [x[LAT:] for x in blocks]
     score, gate, turned = pl.pallas_call(
         functools.partial(index_kernel, count),
         grid=(1,),
-        in_specs=[SMEM] + [key_spec] * 4 + [whole(x) for x in pieces],
+        in_specs=[SMEM] + [whole(x) for x in key_rows] + [whole(x) for x in pieces],
         out_specs=[
             pl.BlockSpec((share, window), lambda i: (0, 0)),
             pl.BlockSpec((GROUPS * tile, window), lambda i: (0, 0)),
@@ -687,7 +691,7 @@
         return pl.pallas_call(
             functools.partial(query_kernel, (first, last), group),
             grid=(1,),
-            in_specs=[SMEM] + [key_spec] * 4
+            in_specs=[SMEM] + [whole(x) for x in key_rows]
             + [whole(x) for x in (index_query, weights, *codes)]
             + [whole(x) for x in before],
             out_specs=[

time: 78.9 us -> 78.4 us (level)
  waiting for transfers between devices: 7.94 us -> 5.85 us
  local copies, waits for them, and re-layouts: 0.07 us -> 1 us
    ppermute x18 -> x20, waiting for transfers between devices: 7.94 us -> 5.85 us  [along(): return lax.ppermute(x, axis, [(i, j % size) for i, j in route])]
    unnamed x16 -> x18, local copies, waits for them, and re-layouts: 0.04 us -> 1 us
    ppermute x18 -> x20, starting transfers between devices: 23.9 us -> 24.6 us  [along(): return lax.ppermute(x, axis, [(i, j % size) for i, j in route])]
  transfers between devices with their start and end apart: 18 -> 20, of which waited for: 7 -> 6; matrix products, arithmetic and copies ran while one was open for 0% -> 0% of each run, Pallas kernels for 53% -> 56%
where the time goes in v4:
time: 78.4 us; the launch traced here: 78.2 us
  Pallas kernels  45.9 us (59%)
  starting transfers between devices  24.6 us (31%)
  waiting for transfers between devices  5.85 us (7%)
  local copies, waits for them, and re-layouts  1 us (1%)
  between operations  0.81 us (1%)
    pallas_call x1, Pallas kernels, shards(): pl.pallas_call(functools.partial(main_kernel, half), grid=(1,), in_specs=...  25.4 us
    ppermute x20, starting transfers between devices, along(): return lax.ppermute(x, axis, [(i, j % size) for i, j in route])  24.6 us
    pallas_call x2, Pallas kernels, query_grads(): pl.pallas_call(functools.partial(query_kernel, (first, last), group), gri...  6.36 us
    ppermute x20, waiting for transfers between devices, along(): return lax.ppermute(x, axis, [(i, j % size) for i, j in route])  5.85 us
    pallas_call x1, Pallas kernels, shards(): pl.pallas_call(functools.partial(own_kernel, half), grid=(1,), in_specs=[...  3.74 us
    pallas_call x1, Pallas kernels, shards(): pl.pallas_call(functools.partial(index_kernel, count), grid=(1,), in_spec...  2.74 us
    pallas_call x1, Pallas kernels, shards(): pl.pallas_call(pack_kernel, grid=(1,), in_specs=[SMEM] + [HBM] * 4, out_s...  2.07 us
    pallas_call x1, Pallas kernels, shards(): pl.pallas_call(functools.partial(keys_kernel, count), grid=(1,), in_specs...  1.94 us
  transfers between devices with their start and end apart: 20, of which 6 were waited for; matrix products, arithmetic and copies ran while one was open for 0% of the time, Pallas kernels for 56%

profile of v4, /device:TPU:0, one launch (start us, length us, event | category | flops | bytes accessed | tf_op | source)
XLA Modules:
  0.0 78.2 jit_solution(2939053679077783216)
XLA Ops:
  0.6 2.4 %collective-permute-start.1 = (bf16[576,256]{1,0:T(8,128)(2,1)}, bf16[576,256]{1,0:T(8,128)(2,1)S(1)}, u32[]{:S(2)}, u32[]{:S(2)}) collective-permute-start(bf16[576,256]{1,0:T(8,128)(2,1)} %bitcast.11), channel_id=1, source_target_pairs={{0,12},{4,8},{8,20},{12,16},{16,28},{20,24},{24,4},{28,0},{1,13},{... | collective-permute-start | bytes 884744 | tf_op jit(solution)/shard_map/ppermute | solution.py:515
  3.1 0.1 pad_add_fusion.place
  3.1 2.1 %pack_rows.1 = (bf16[704,256]{1,0:T(8,128)(2,1)S(1)}, bf16[128,256]{1,0:T(8,128)(2,1)S(1)}, bf16[32,2176]{1,0:T(8,128)(2,1)S(1)}, bf16[32,2176]{1,0:T(8,128)(2,1...) custom-call(s32[2]{0:T(128)S(1)} %pad_add_fusion.place, bf16[576,256]{1,0:T(8,128)(2,1)} %bitcast.12, ...), custom_call_target="tpu_custom_call" | custom-call | flops 1 | bytes 1 | tf_op jit(solution)/shard_map/pack_rows/pallas_call | solution.py:559
  5.2 1.6 %collective-permute-start.2 = (bf16[32,2176]{1,0:T(8,128)(2,1)S(1)}, bf16[32,2176]{1,0:T(8,128)(2,1)S(1)}, u32[]{:S(2)}, u32[]{:S(2)}) collective-permute-start(bf16[32,2176]{1,0:T(8,128)(2,1)S(1)} %get-tuple-element.35), channel_id=1, source_target_pairs={{0,1},{1,0},{2,3},{3,2},{4,5},{5,4},{6,7},{7,6},{8,9},{9,8},{10,11... | collective-permute-start | bytes 417800 | tf_op jit(solution)/shard_map/ppermute | solution.py:515
  6.9 0.4 collective-permute-start
  7.3 1.0 %copy-done.1 = bf16[256,576]{0,1:T(8,128)(2,1)S(1)} copy-done((bf16[256,576]{0,1:T(8,128)(2,1)S(1)}, bf16[256,576]{0,1:T(8,128)(2,1)}, u32[]{:S(2)}) %copy-start.1) | copy-done | bytes 294936
  8.2 3.7 %own_block.1.own_exp = f32[4096,256]{1,0:T(8,128)S(1)} custom-call(bf16[128,18432]{1,0:T(8,128)(2,1)} %q.5, bf16[576,256]{1,0:T(8,128)(2,1)S(1)} %bitcast.13, s32[1,128]{1,0:T(1,128)} %bitcast.22, s32[1,256]{1,0:T(1,128)} %bitcast.19), custom_call_target="tpu_custom_call" | custom-call | flops 1 | bytes 1 | tf_op jit(solution)/shard_map/own_block/pallas_call | solution.py:580
  12.0 0.0 collective-permute-done.1.block.b
  12.0 1.3 %collective-permute-start.5 = (bf16[576,256]{1,0:T(8,128)(2,1)S(1)}, bf16[576,256]{1,0:T(8,128)(2,1)S(1)}, u32[]{:S(2)}, u32[]{:S(2)}) collective-permute-start(bf16[576,256]{1,0:T(8,128)(2,1)S(1)} %collective-permute-done.1.block.b), channel_id=1, source_target_pairs={{0,4},{4,0},{8,12},{12,8},{16,20},{20,16},{24,28},{28,24},{1,5},{5... | collective-permute-start | bytes 884744 | tf_op jit(solution)/shard_map/ppermute | solution.py:515
  13.3 2.6 %collective-permute-start.9 = (bf16[32,2176]{1,0:T(8,128)(2,1)S(1)}, bf16[32,2176]{1,0:T(8,128)(2,1)S(1)}, u32[]{:S(2)}, u32[]{:S(2)}) collective-permute-start(bf16[32,2176]{1,0:T(8,128)(2,1)S(1)} %get-tuple-element.46), channel_id=1, source_target_pairs={{0,2},{1,3},{2,0},{3,1},{4,6},{5,7},{6,4},{7,5},{8,10},{9,11},{10,... | collective-permute-start | bytes 417800 | tf_op jit(solution)/shard_map/ppermute | solution.py:515
  15.9 0.6 collective-permute-start.10
  16.5 1.8 %next_block.1.b_exp = f32[4096,256]{1,0:T(8,128)S(1)} custom-call(bf16[128,18432]{1,0:T(8,128)(2,1)S(1)} %bitcast.10, bf16[576,256]{1,0:T(8,128)(2,1)S(1)} %collective-permute-done.1.block.b), custom_call_target="tpu_custom_call" | custom-call | flops 1 | bytes 1 | tf_op jit(solution)/shard_map/next_block/pallas_call | solution.py:598
  18.4 0.2 collective-permute-start.3
  18.5 0.0 collective-permute-done.a
  18.5 0.0 collective-permute-done.5.c
  18.6 0.0 copy-start.6
  18.6 25.4 %main_mass.1 = (f32[32,1024]{1,0:T(8,128)S(1)}, s16[32,1152]{1,0:T(8,128)(2,1)S(1)}, s16[32,1152]{1,0:T(8,128)(2,1)S(1)}, s16[32,1152]{1,0:T(8,128)(2,1)S(1)}) custom-call(s32[2]{0:T(128)S(1)} %pad_add_fusion.place, bf16[128,18432]{1,0:T(8,128)(2,1)S(1)} %bitcast.10, bf16[576,256]{1,0:T(8,128)(2,1)S(1)} %bitcast.14, ...), custom_call_target="tpu_custom_call" | custom-call | flops 1 | bytes 1 | tf_op jit(solution)/shard_map/main_mass/pallas_call | solution.py:615
  44.0 0.0 copy-start
  44.0 0.0 copy-start.2
  44.0 3.2 %collective-permute-start.6 = (s16[32,1152]{1,0:T(8,128)(2,1)S(1)}, s16[32,1152]{1,0:T(8,128)(2,1)S(1)}, u32[]{:S(2)}, u32[]{:S(2)}) collective-permute-start(s16[32,1152]{1,0:T(8,128)(2,1)S(1)} %get-tuple-element.41), channel_id=1, source_target_pairs={{0,3},{1,2},{2,1},{3,0},{4,7},{5,6},{6,5},{7,4},{8,11},{9,10},{10,... | collective-permute-start | bytes 221192 | tf_op jit(solution)/shard_map/ppermute | solution.py:515
  47.2 1.3 %collective-permute-start.8 = (s16[32,1152]{1,0:T(8,128)(2,1)S(1)}, s16[32,1152]{1,0:T(8,128)(2,1)S(1)}, u32[]{:S(2)}, u32[]{:S(2)}) collective-permute-start(s16[32,1152]{1,0:T(8,128)(2,1)S(1)} %get-tuple-element.43), channel_id=1, source_target_pairs={{0,1},{1,0},{2,3},{3,2},{4,5},{5,4},{6,7},{7,6},{8,9},{9,8},{10,11... | collective-permute-start | bytes 221192 | tf_op jit(solution)/shard_map/ppermute | solution.py:515
  48.5 0.0 collective-permute-done.10.rest_3_
  48.5 1.2 %collective-permute-done.4.c = bf16[128,256]{1,0:T(8,128)(2,1)S(1)} collective-permute-done((bf16[128,256]{1,0:T(8,128)(2,1)S(1)}, bf16[128,256]{1,0:T(8,128)(2,1)S(1)}, u32[]{:S(2)}, u32[]{:S(2)}) %collective-permute-start.4) | collective-permute-done | bytes 65568 | tf_op jit(solution)/shard_map/ppermute | solution.py:515
  49.7 2.7 %index_scores.1 = (f32[32,1024]{1,0:T(8,128)S(1)}, bf16[2048,1024]{1,0:T(8,128)(2,1)S(1)}, bf16[256,2048]{1,0:T(8,128)(2,1)S(1)}) custom-call(s32[2]{0:T(128)S(1)} %pad_add_fusion.place, bf16[128,256]{1,0:T(8,128)(2,1)S(1)} %get-tuple-element.37.own, bf16[704,256]{1,0:T(8,128)(2,1)S(1)} %collective-permute-done.a, ...), custom_call_target="tpu_custom_call" | custom-call | flops 1 | bytes 1 | tf_op jit(solution)/shard_map/index_scores/pallas_call | solution.py:636
  52.5 1.4 %collective-permute-done.7.m2 = s16[32,1152]{1,0:T(8,128)(2,1)S(1)} collective-permute-done((s16[32,1152]{1,0:T(8,128)(2,1)S(1)}, s16[32,1152]{1,0:T(8,128)(2,1)S(1)}, u32[]{:S(2)}, u32[]{:S(2)}) %collective-permute-start.7) | collective-permute-done | bytes 73760 | tf_op jit(solution)/shard_map/ppermute | solution.py:515
  53.9 0.0 collective-permute-done.8.m1
  53.9 1.0 %dscores.1 = (bf16[2,32,1024]{2,1,0:T(8,128)(2,1)S(1)}, s16[32,1152]{1,0:T(8,128)(2,1)S(1)}) custom-call(s32[2]{0:T(128)S(1)} %pad_add_fusion.place, f32[32,1024]{1,0:T(8,128)S(1)} %get-tuple-element.40.m0, s16[32,1152]{1,0:T(8,128)(2,1)S(1)} %collective-permute-done.6.m3, s16[32,1152]{1,0:T(8,128)(2,1)S(1)} %collective-permute-done.7.m2, ...), custom_call_target="tpu_custom_call" | custom-call | flops 1 | bytes 1 | tf_op jit(solution)/shard_map/dscores/pallas_call | solution.py:656
  54.9 1.0 %collective-permute-start.12 = (s16[32,1152]{1,0:T(8,128)(2,1)S(1)}, s16[32,1152]{1,0:T(8,128)(2,1)S(1)}, u32[]{:S(2)}, u32[]{:S(2)}) collective-permute-start(s16[32,1152]{1,0:T(8,128)(2,1)S(1)} %get-tuple-element.49.c0), channel_id=1, source_target_pairs={{0,2},{1,3},{2,0},{3,1},{4,6},{5,7},{6,4},{7,5},{8,10},{9,11},{10,... | collective-permute-start | bytes 221192 | tf_op jit(solution)/shard_map/ppermute | solution.py:515
  55.9 2.7 %collective-permute-start.13 = (s16[32,1152]{1,0:T(8,128)(2,1)S(1)}, s16[32,1152]{1,0:T(8,128)(2,1)S(1)}, u32[]{:S(2)}, u32[]{:S(2)}) collective-permute-start(s16[32,1152]{1,0:T(8,128)(2,1)S(1)} %get-tuple-element.49.c0), channel_id=1, source_target_pairs={{0,3},{1,2},{2,1},{3,0},{4,7},{5,6},{6,5},{7,4},{8,11},{9,10},{10,... | collective-permute-start | bytes 221192 | tf_op jit(solution)/shard_map/ppermute | solution.py:515
  58.6 0.0 collective-permute-start.11
  58.6 1.9 %key_grads.1 = (s16[272,128]{1,0:T(8,128)(2,1)S(1)}, s16[272,128]{1,0:T(8,128)(2,1)S(1)}, s16[272,128]{1,0:T(8,128)(2,1)S(1)}, f32[256,128]{1,0:T(8,128)S(1)}) custom-call(bf16[2048,1024]{1,0:T(8,128)(2,1)S(1)} %get-tuple-element.50.gate, bf16[256,2048]{1,0:T(8,128)(2,1)S(1)} %get-tuple-element.51.turned, bf16[2,32,1024]{2,1,0:T(8,128)(2,1)S(1)} %get-tuple-element.52.spread), custom_call_target="tpu_custom_call" | custom-call | flops 1 | bytes 1 | tf_op jit(solution)/shard_map/key_grads/pallas_call | solution.py:672
  60.6 1.5 %collective-permute-start.14 = (s16[272,128]{1,0:T(8,128)(2,1)S(1)}, s16[272,128]{1,0:T(8,128)(2,1)S(1)}, u32[]{:S(2)}, u32[]{:S(2)}) collective-permute-start(s16[272,128]{1,0:T(8,128)(2,1)S(1)} %get-tuple-element.60), channel_id=1, source_target_pairs={{0,28},{4,0},{8,4},{12,8},{16,12},{20,16},{24,20},{28,24},{1,29},{... | collective-permute-start | bytes 208904 | tf_op jit(solution)/shard_map/ppermute | solution.py:515
  62.1 0.9 %collective-permute-start.15 = (s16[272,128]{1,0:T(8,128)(2,1)S(1)}, s16[272,128]{1,0:T(8,128)(2,1)S(1)}, u32[]{:S(2)}, u32[]{:S(2)}) collective-permute-start(s16[272,128]{1,0:T(8,128)(2,1)S(1)} %get-tuple-element.61), channel_id=1, source_target_pairs={{0,24},{4,28},{8,0},{12,4},{16,8},{20,12},{24,16},{28,20},{1,25},{... | collective-permute-start | bytes 208904 | tf_op jit(solution)/shard_map/ppermute | solution.py:515
  63.0 0.8 %collective-permute-done.12.c2 = s16[32,1152]{1,0:T(8,128)(2,1)S(1)} collective-permute-done((s16[32,1152]{1,0:T(8,128)(2,1)S(1)}, s16[32,1152]{1,0:T(8,128)(2,1)S(1)}, u32[]{:S(2)}, u32[]{:S(2)}) %collective-permute-start.12) | collective-permute-done | bytes 73760 | tf_op jit(solution)/shard_map/ppermute | solution.py:515
  63.8 0.3 collective-permute-start.16
  64.2 2.0 %query_grads.2 = (bf16[128,2048]{1,0:T(8,128)(2,1)S(1)}, f32[128,128]{1,0:T(8,128)S(1)}) custom-call(s32[2]{0:T(128)S(1)} %pad_add_fusion.place, bf16[128,256]{1,0:T(8,128)(2,1)S(1)} %get-tuple-element.37.own, bf16[704,256]{1,0:T(8,128)(2,1)S(1)} %collective-permute-done.a, bf16[128,256]{1,0:T(8,128)(2,1)S(1)} %collective-permute-done.3.b, ...), custom_call_target="tpu_custom_call" | custom-call | flops 1 | bytes 1 | tf_op jit(solution)/shard_map/query_grads/pallas_call | solution.py:691
  66.1 0.0 collective-permute-done.14.c1
  66.2 0.3 collective-permute-done.15.c2
  66.4 1.1 %collective-permute-done.16.c3 = s16[272,128]{1,0:T(8,128)(2,1)S(1)} collective-permute-done((s16[272,128]{1,0:T(8,128)(2,1)S(1)}, s16[272,128]{1,0:T(8,128)(2,1)S(1)}, u32[]{:S(2)}, u32[]{:S(2)}) %collective-permute-start.16) | collective-permute-done | bytes 69664 | tf_op jit(solution)/shard_map/ppermute | solution.py:515
  67.5 0.1 owned_keys.1.c0
  67.7 2.2 %collective-permute-start.19 = (s16[272,128]{1,0:T(8,128)(2,1)S(1)}, s16[272,128]{1,0:T(8,128)(2,1)S(1)}, u32[]{:S(2)}, u32[]{:S(2)}) collective-permute-start(s16[272,128]{1,0:T(8,128)(2,1)S(1)} %owned_keys.1.c0), channel_id=1, source_target_pairs={{0,3},{1,2},{2,1},{3,0},{4,7},{5,6},{6,5},{7,4},{8,11},{9,10},{10,... | collective-permute-start | bytes 208904 | tf_op jit(solution)/shard_map/ppermute | solution.py:515
  69.8 0.7 collective-permute-start.18
  70.5 1.6 %collective-permute-start.17 = (s16[272,128]{1,0:T(8,128)(2,1)S(1)}, s16[272,128]{1,0:T(8,128)(2,1)S(1)}, u32[]{:S(2)}, u32[]{:S(2)}) collective-permute-start(s16[272,128]{1,0:T(8,128)(2,1)S(1)} %owned_keys.1.c0), channel_id=1, source_target_pairs={{0,1},{1,0},{2,3},{3,2},{4,5},{5,4},{6,7},{7,6},{8,9},{9,8},{10,11... | collective-permute-start | bytes 208904 | tf_op jit(solution)/shard_map/ppermute | solution.py:515
  72.1 4.4 %query_grads.3 = (bf16[128,2048]{1,0:T(8,128)(2,1)}, f32[16,128]{1,0:T(8,128)}) custom-call(s32[2]{0:T(128)S(1)} %pad_add_fusion.place, bf16[128,256]{1,0:T(8,128)(2,1)S(1)} %get-tuple-element.37.own, bf16[704,256]{1,0:T(8,128)(2,1)S(1)} %collective-permute-done.a, bf16[128,256]{1,0:T(8,128)(2,1)S(1)} %collective-permute-done.3.b, ...), custom_call_target="tpu_custom_call" | custom-call | flops 1 | bytes 1 | tf_op jit(solution)/shard_map/query_grads/pallas_call | solution.py:691
  76.5 0.0 collective-permute-done.19.c3
  76.5 1.0 %collective-permute-done.18.c2 = s16[272,128]{1,0:T(8,128)(2,1)S(1)} collective-permute-done((s16[272,128]{1,0:T(8,128)(2,1)S(1)}, s16[272,128]{1,0:T(8,128)(2,1)S(1)}, u32[]{:S(2)}, u32[]{:S(2)}) %collective-permute-start.18) | collective-permute-done | bytes 69664 | tf_op jit(solution)/shard_map/ppermute | solution.py:515
  77.5 0.0 collective-permute-done.17.c1
  77.5 0.7 total_keys.1
  (23 shorter events, 0.0 us)
Async XLA Ops:
  0.6 11.4 %collective-permute-start.1 = (bf16[576,256]{1,0:T(8,128)(2,1)}, bf16[576,256]{1,0:T(8,128)(2,1)S(1)}, u32[]{:S(2)}, u32[]{:S(2)}) collective-permute-start(bf16[576,256]{1,0:T(8,128)(2,1)} %bitcast.11), channel_id=1, source_target_pairs={{0,12},{4,8},{8,20},{12,16},{16,28},{20,24},{24,4},{28,0},{1,13},{... | collective-permute-start | bytes 884744 | tf_op jit(solution)/shard_map/ppermute | solution.py:515
  3.1 13.4 %slice-start = ((s8[4718592]{0:T(1024)(128)(4,1)}), s8[4194304]{0:T(1024)(128)(4,1)S(1)}, s32[]{:S(2)}) async-start(s8[4718592]{0:T(1024)(128)(4,1)} %bitcast.9), calls=%async_computation | async-start | bytes 8388608
  5.2 6.8 %collective-permute-start.2 = (bf16[32,2176]{1,0:T(8,128)(2,1)S(1)}, bf16[32,2176]{1,0:T(8,128)(2,1)S(1)}, u32[]{:S(2)}, u32[]{:S(2)}) collective-permute-start(bf16[32,2176]{1,0:T(8,128)(2,1)S(1)} %get-tuple-element.35), channel_id=1, source_target_pairs={{0,1},{1,0},{2,3},{3,2},{4,5},{5,4},{6,7},{7,6},{8,9},{9,8},{10,11... | collective-permute-start | bytes 417800 | tf_op jit(solution)/shard_map/ppermute | solution.py:515
  6.9 11.7 %collective-permute-start = (bf16[704,256]{1,0:T(8,128)(2,1)S(1)}, bf16[704,256]{1,0:T(8,128)(2,1)S(1)}, u32[]{:S(2)}, u32[]{:S(2)}) collective-permute-start(bf16[704,256]{1,0:T(8,128)(2,1)S(1)} %get-tuple-element.34), channel_id=1, source_target_pairs={{0,4},{4,16},{8,12},{12,24},{16,20},{20,0},{24,28},{28,8},{1,5},{5... | collective-permute-start | bytes 1081352 | tf_op jit(solution)/shard_map/ppermute | solution.py:515
  7.3 1.0 %copy-start.1 = (bf16[256,576]{0,1:T(8,128)(2,1)S(1)}, bf16[256,576]{0,1:T(8,128)(2,1)}, u32[]{:S(2)}) copy-start(bf16[256,576]{0,1:T(8,128)(2,1)} %param.10) | copy-start | bytes 884740
  8.2 8.3 %slice-start.1 = ((s8[4718592]{0:T(1024)(128)(4,1)}), s8[524288]{0:T(1024)(128)(4,1)S(1)}, s32[]{:S(2)}) async-start(s8[4718592]{0:T(1024)(128)(4,1)} %bitcast.9), calls=%async_computation.1 | async-start | bytes 1048576
  12.0 6.5 %collective-permute-start.5 = (bf16[576,256]{1,0:T(8,128)(2,1)S(1)}, bf16[576,256]{1,0:T(8,128)(2,1)S(1)}, u32[]{:S(2)}, u32[]{:S(2)}) collective-permute-start(bf16[576,256]{1,0:T(8,128)(2,1)S(1)} %collective-permute-done.1.block.b), channel_id=1, source_target_pairs={{0,4},{4,0},{8,12},{12,8},{16,20},{20,16},{24,28},{28,24},{1,5},{5... | collective-permute-start | bytes 884744 | tf_op jit(solution)/shard_map/ppermute | solution.py:515
  13.3 33.9 %collective-permute-start.9 = (bf16[32,2176]{1,0:T(8,128)(2,1)S(1)}, bf16[32,2176]{1,0:T(8,128)(2,1)S(1)}, u32[]{:S(2)}, u32[]{:S(2)}) collective-permute-start(bf16[32,2176]{1,0:T(8,128)(2,1)S(1)} %get-tuple-element.46), channel_id=1, source_target_pairs={{0,2},{1,3},{2,0},{3,1},{4,6},{5,7},{6,4},{7,5},{8,10},{9,11},{10,... | collective-permute-start | bytes 417800 | tf_op jit(solution)/shard_map/ppermute | solution.py:515
  15.9 2.7 %copy-start.3 = (f32[128,32]{0,1:T(8,128)S(1)}, f32[128,32]{0,1:T(8,128)}, u32[]{:S(2)}) copy-start(f32[128,32]{0,1:T(8,128)} %param.11) | copy-start | bytes 49156
  15.9 2.7 %copy-start.4 = (s32[256]{0:T(256)S(1)}, s32[256]{0:T(256)}, u32[]{:S(2)}) copy-start(s32[256]{0:T(256)} %param.17) | copy-start | bytes 3076
  15.9 2.7 %copy-start.5 = (s32[128]{0:T(128)S(1)}, s32[128]{0:T(128)}, u32[]{:S(2)}) copy-start(s32[128]{0:T(128)} %param.16) | copy-start | bytes 1540
  15.9 32.6 %collective-permute-start.10 = (bf16[32,2176]{1,0:T(8,128)(2,1)S(1)}, bf16[32,2176]{1,0:T(8,128)(2,1)S(1)}, u32[]{:S(2)}, u32[]{:S(2)}) collective-permute-start(bf16[32,2176]{1,0:T(8,128)(2,1)S(1)} %get-tuple-element.47), channel_id=1, source_target_pairs={{0,3},{1,2},{2,1},{3,0},{4,7},{5,6},{6,5},{7,4},{8,11},{9,10},{10,... | collective-permute-start | bytes 417800 | tf_op jit(solution)/shard_map/ppermute | solution.py:515
  18.4 30.1 %collective-permute-start.3 = (bf16[128,256]{1,0:T(8,128)(2,1)S(1)}, bf16[128,256]{1,0:T(8,128)(2,1)S(1)}, u32[]{:S(2)}, u32[]{:S(2)}) collective-permute-start(bf16[128,256]{1,0:T(8,128)(2,1)S(1)} %get-tuple-element.37.own), channel_id=1, source_target_pairs={{0,12},{4,8},{8,20},{12,16},{16,28},{20,24},{24,4},{28,0},{1,13},{... | collective-permute-start | bytes 196616 | tf_op jit(solution)/shard_map/ppermute | solution.py:515
  18.6 35.3 %copy-start.6 = (f32[128]{0:T(128)S(1)}, f32[128]{0:T(128)}, u32[]{:S(2)}) copy-start(f32[128]{0:T(128)} %param.15) | copy-start | bytes 1540
  44.0 20.1 %copy-start = (bf16[128,2048]{1,0:T(8,128)(2,1)S(1)}, bf16[128,2048]{1,0:T(8,128)(2,1)}, u32[]{:S(2)}) copy-start(bf16[128,2048]{1,0:T(8,128)(2,1)} %query.5) | copy-start | bytes 1572868
  44.0 20.1 %copy-start.2 = (f32[128,16]{0,1:T(8,128)S(1)}, f32[128,16]{0,1:T(8,128)}, u32[]{:S(2)}) copy-start(f32[128,16]{0,1:T(8,128)} %param.13) | copy-start | bytes 24580
  44.0 8.5 %collective-permute-start.6 = (s16[32,1152]{1,0:T(8,128)(2,1)S(1)}, s16[32,1152]{1,0:T(8,128)(2,1)S(1)}, u32[]{:S(2)}, u32[]{:S(2)}) collective-permute-start(s16[32,1152]{1,0:T(8,128)(2,1)S(1)} %get-tuple-element.41), channel_id=1, source_target_pairs={{0,3},{1,2},{2,1},{3,0},{4,7},{5,6},{6,5},{7,4},{8,11},{9,10},{10,... | collective-permute-start | bytes 221192 | tf_op jit(solution)/shard_map/ppermute | solution.py:515
  47.2 6.7 %collective-permute-start.7 = (s16[32,1152]{1,0:T(8,128)(2,1)S(1)}, s16[32,1152]{1,0:T(8,128)(2,1)S(1)}, u32[]{:S(2)}, u32[]{:S(2)}) collective-permute-start(s16[32,1152]{1,0:T(8,128)(2,1)S(1)} %get-tuple-element.42), channel_id=1, source_target_pairs={{0,2},{1,3},{2,0},{3,1},{4,6},{5,7},{6,4},{7,5},{8,10},{9,11},{10,... | collective-permute-start | bytes 221192 | tf_op jit(solution)/shard_map/ppermute | solution.py:515
  47.2 6.7 %collective-permute-start.8 = (s16[32,1152]{1,0:T(8,128)(2,1)S(1)}, s16[32,1152]{1,0:T(8,128)(2,1)S(1)}, u32[]{:S(2)}, u32[]{:S(2)}) collective-permute-start(s16[32,1152]{1,0:T(8,128)(2,1)S(1)} %get-tuple-element.43), channel_id=1, source_target_pairs={{0,1},{1,0},{2,3},{3,2},{4,5},{5,4},{6,7},{7,6},{8,9},{9,8},{10,11... | collective-permute-start | bytes 221192 | tf_op jit(solution)/shard_map/ppermute | solution.py:515
  48.5 1.3 %collective-permute-start.4 = (bf16[128,256]{1,0:T(8,128)(2,1)S(1)}, bf16[128,256]{1,0:T(8,128)(2,1)S(1)}, u32[]{:S(2)}, u32[]{:S(2)}) collective-permute-start(bf16[128,256]{1,0:T(8,128)(2,1)S(1)} %collective-permute-done.3.b), channel_id=1, source_target_pairs={{0,4},{4,0},{8,12},{12,8},{16,20},{20,16},{24,28},{28,24},{1,5},{5... | collective-permute-start | bytes 196616 | tf_op jit(solution)/shard_map/ppermute | solution.py:515
  54.9 8.9 %collective-permute-start.12 = (s16[32,1152]{1,0:T(8,128)(2,1)S(1)}, s16[32,1152]{1,0:T(8,128)(2,1)S(1)}, u32[]{:S(2)}, u32[]{:S(2)}) collective-permute-start(s16[32,1152]{1,0:T(8,128)(2,1)S(1)} %get-tuple-element.49.c0), channel_id=1, source_target_pairs={{0,2},{1,3},{2,0},{3,1},{4,6},{5,7},{6,4},{7,5},{8,10},{9,11},{10,... | collective-permute-start | bytes 221192 | tf_op jit(solution)/shard_map/ppermute | solution.py:515
  55.9 8.2 %collective-permute-start.13 = (s16[32,1152]{1,0:T(8,128)(2,1)S(1)}, s16[32,1152]{1,0:T(8,128)(2,1)S(1)}, u32[]{:S(2)}, u32[]{:S(2)}) collective-permute-start(s16[32,1152]{1,0:T(8,128)(2,1)S(1)} %get-tuple-element.49.c0), channel_id=1, source_target_pairs={{0,3},{1,2},{2,1},{3,0},{4,7},{5,6},{6,5},{7,4},{8,11},{9,10},{10,... | collective-permute-start | bytes 221192 | tf_op jit(solution)/shard_map/ppermute | solution.py:515
  58.6 5.5 %collective-permute-start.11 = (s16[32,1152]{1,0:T(8,128)(2,1)S(1)}, s16[32,1152]{1,0:T(8,128)(2,1)S(1)}, u32[]{:S(2)}, u32[]{:S(2)}) collective-permute-start(s16[32,1152]{1,0:T(8,128)(2,1)S(1)} %get-tuple-element.49.c0), channel_id=1, source_target_pairs={{0,1},{1,0},{2,3},{3,2},{4,5},{5,4},{6,7},{7,6},{8,9},{9,8},{10,11... | collective-permute-start | bytes 221192 | tf_op jit(solution)/shard_map/ppermute | solution.py:515
  60.6 5.6 %collective-permute-start.14 = (s16[272,128]{1,0:T(8,128)(2,1)S(1)}, s16[272,128]{1,0:T(8,128)(2,1)S(1)}, u32[]{:S(2)}, u32[]{:S(2)}) collective-permute-start(s16[272,128]{1,0:T(8,128)(2,1)S(1)} %get-tuple-element.60), channel_id=1, source_target_pairs={{0,28},{4,0},{8,4},{12,8},{16,12},{20,16},{24,20},{28,24},{1,29},{... | collective-permute-start | bytes 208904 | tf_op jit(solution)/shard_map/ppermute | solution.py:515
  62.1 4.3 %collective-permute-start.15 = (s16[272,128]{1,0:T(8,128)(2,1)S(1)}, s16[272,128]{1,0:T(8,128)(2,1)S(1)}, u32[]{:S(2)}, u32[]{:S(2)}) collective-permute-start(s16[272,128]{1,0:T(8,128)(2,1)S(1)} %get-tuple-element.61), channel_id=1, source_target_pairs={{0,24},{4,28},{8,0},{12,4},{16,8},{20,12},{24,16},{28,20},{1,25},{... | collective-permute-start | bytes 208904 | tf_op jit(solution)/shard_map/ppermute | solution.py:515
  63.8 3.7 %collective-permute-start.16 = (s16[272,128]{1,0:T(8,128)(2,1)S(1)}, s16[272,128]{1,0:T(8,128)(2,1)S(1)}, u32[]{:S(2)}, u32[]{:S(2)}) collective-permute-start(s16[272,128]{1,0:T(8,128)(2,1)S(1)} %get-tuple-element.62), channel_id=1, source_target_pairs={{0,20},{4,24},{8,28},{12,0},{16,4},{20,8},{24,12},{28,16},{1,21},{... | collective-permute-start | bytes 208904 | tf_op jit(solution)/shard_map/ppermute | solution.py:515
  67.7 8.8 %collective-permute-start.19 = (s16[272,128]{1,0:T(8,128)(2,1)S(1)}, s16[272,128]{1,0:T(8,128)(2,1)S(1)}, u32[]{:S(2)}, u32[]{:S(2)}) collective-permute-start(s16[272,128]{1,0:T(8,128)(2,1)S(1)} %owned_keys.1.c0), channel_id=1, source_target_pairs={{0,3},{1,2},{2,1},{3,0},{4,7},{5,6},{6,5},{7,4},{8,11},{9,10},{10,... | collective-permute-start | bytes 208904 | tf_op jit(solution)/shard_map/ppermute | solution.py:515
  69.8 7.6 %collective-permute-start.18 = (s16[272,128]{1,0:T(8,128)(2,1)S(1)}, s16[272,128]{1,0:T(8,128)(2,1)S(1)}, u32[]{:S(2)}, u32[]{:S(2)}) collective-permute-start(s16[272,128]{1,0:T(8,128)(2,1)S(1)} %owned_keys.1.c0), channel_id=1, source_target_pairs={{0,2},{1,3},{2,0},{3,1},{4,6},{5,7},{6,4},{7,5},{8,10},{9,11},{10,... | collective-permute-start | bytes 208904 | tf_op jit(solution)/shard_map/ppermute | solution.py:515
  70.5 6.9 %collective-permute-start.17 = (s16[272,128]{1,0:T(8,128)(2,1)S(1)}, s16[272,128]{1,0:T(8,128)(2,1)S(1)}, u32[]{:S(2)}, u32[]{:S(2)}) collective-permute-start(s16[272,128]{1,0:T(8,128)(2,1)S(1)} %owned_keys.1.c0), channel_id=1, source_target_pairs={{0,1},{1,0},{2,3},{3,2},{4,5},{5,4},{6,7},{7,6},{8,9},{9,8},{10,11... | collective-permute-start | bytes 208904 | tf_op jit(solution)/shard_map/ppermute | solution.py:515

commit v5 on v4

--- a/solution.py
+++ b/solution.py
@@ -475,10 +475,10 @@
             grad[:, lanes] = (mine * tall[:, j:j + 1]).astype(jnp.bfloat16)
             product = jnp.sum(mine * query[:, lanes].astype(jnp.float32), axis=1, keepdims=True)
             total = jnp.where(lane == j, product, total)
-    out[...] = total.T[:out.shape[0], :] if first else total
-
-
-def owned_kernel(p0, c1, c2, c3, after, code):
+    out[...] = total.T[:out.shape[0], :] if out.shape[0] < rows else total
+
+
+def owned_kernel(p0, c1, c2, c3, code):
     kb = p0.shape[0]
     moved = [restored_columns(c, kb) for c in (c1, c2, c3)]
     coded_columns(code, (p0[...] + moved[0]) + (moved[1] + moved[2]))
@@ -666,7 +666,6 @@
         cost_estimate=cost(0, 12 * share * window),
         name="dscores",
     )(place, masses[0], *masses[:0:-1], score, outside, qpos, kpos)
-    codes = [code] + [exchanged(code, d) for d in range(1, GROUPS)]
 
     sum_shape = (kb + 16, IDIM)
     parts = pl.pallas_call(
@@ -680,14 +679,15 @@
         cost_estimate=cost(8 * GROUPS * tile * window * IDIM, GROUPS * tile * window * 2),
         name="key_grads",
     )(gate, turned, spread)
+    own_part, code = lax.optimization_barrier((parts[STEPS - 1], code))
+    codes = [code] + [exchanged(code, d) for d in range(1, GROUPS)]
     sent = [parts[STEPS - 1 - distance] for distance in range(1, STEPS)]
-    sent[-1], codes[2] = lax.optimization_barrier((sent[-1], codes[2]))
     moved = [along(x, "seq", [(i, i - d - 1) for i in range(n_seq)]) for d, x in enumerate(sent)]
 
     group = count // 4
 
     def query_grads(first, last, before):
-        sums_shape = (count, rows) if first else (rows, 128)
+        sums_shape = (count, rows) if last == count else (rows, 128)
         return pl.pallas_call(
             functools.partial(query_kernel, (first, last), group),
             grid=(1,),
@@ -712,19 +712,18 @@
             name="query_grads",
         )(place, *key_rows, index_query, weights, *codes, *before)
 
-    begun = query_grads(0, group, ())
-    grad_query, grad_weight = query_grads(group, count, begun)
+    grad_query, grad_weight = query_grads(0, count, ())
 
     owned = pl.pallas_call(
         owned_kernel,
         grid=(1,),
-        in_specs=[whole(x) for x in (parts[STEPS - 1], *moved, begun[1])],
+        in_specs=[whole(x) for x in (own_part, *moved)],
         out_specs=pl.BlockSpec(sum_shape, lambda i: (0, 0)),
         out_shape=shape(sum_shape, int16),
         compiler_params=params(16),
         cost_estimate=cost(0, 20 * kb * IDIM),
         name="owned_keys",
-    )(parts[STEPS - 1], *moved, begun[1])
+    )(own_part, *moved)
     owners = [owned] + [exchanged(owned, d) for d in range(1, GROUPS)]
     grad_keys = pl.pallas_call(
         total_kernel,

time: 78.4 us -> 76.6 us (0.977)
  waiting for transfers between devices: 5.85 us -> 3.97 us
  starting transfers between devices: 24.6 us -> 26 us
  Pallas kernels: 45.9 us -> 44.6 us
    ppermute x20, waiting for transfers between devices: 5.85 us -> 3.97 us  [along(): return lax.ppermute(x, axis, [(i, j % size) for i, j in route])]
    ppermute x20, starting transfers between devices: 24.6 us -> 26 us  [along(): return lax.ppermute(x, axis, [(i, j % size) for i, j in route])]
    pallas_call x2 -> x1, Pallas kernels: 6.36 us -> 5.04 us  [query_grads(): pl.pallas_call(functools.partial(query_kernel, (first, last), group), gri...]
  transfers between devices with their start and end apart: 20 -> 20, of which waited for: 6 -> 4; matrix products, arithmetic and copies ran while one was open for 0% -> 0% of each run, Pallas kernels for 56% -> 54%
where the time goes in v5:
time: 76.6 us; the launch traced here: 76.4 us
  Pallas kernels  44.6 us (58%)
  starting transfers between devices  26 us (34%)
  waiting for transfers between devices  3.97 us (5%)
  local copies, waits for them, and re-layouts  1 us (1%)
  between operations  0.81 us (1%)
    ppermute x20, starting transfers between devices, along(): return lax.ppermute(x, axis, [(i, j % size) for i, j in route])  26 us
    pallas_call x1, Pallas kernels, shards(): pl.pallas_call(functools.partial(main_kernel, half), grid=(1,), in_specs=...  25.4 us
    pallas_call x1, Pallas kernels, query_grads(): pl.pallas_call(functools.partial(query_kernel, (first, last), group), gri...  5.04 us
    ppermute x20, waiting for transfers between devices, along(): return lax.ppermute(x, axis, [(i, j % size) for i, j in route])  3.97 us
    pallas_call x1, Pallas kernels, shards(): pl.pallas_call(functools.partial(own_kernel, half), grid=(1,), in_specs=[...  3.74 us
    pallas_call x1, Pallas kernels, shards(): pl.pallas_call(functools.partial(index_kernel, count), grid=(1,), in_spec...  2.74 us
    pallas_call x1, Pallas kernels, shards(): pl.pallas_call(pack_kernel, grid=(1,), in_specs=[SMEM] + [HBM] * 4, out_s...  2.07 us
    pallas_call x1, Pallas kernels, shards(): pl.pallas_call(functools.partial(keys_kernel, count), grid=(1,), in_specs...  1.98 us
  transfers between devices with their start and end apart: 20, of which 4 were waited for; matrix products, arithmetic and copies ran while one was open for 0% of the time, Pallas kernels for 54%

profile of v5, /device:TPU:0, one launch (start us, length us, event | category | flops | bytes accessed | tf_op | source)
XLA Modules:
  0.0 76.4 jit_solution(3102334816180229793)
XLA Ops:
  0.6 2.4 %collective-permute-start.1 = (bf16[576,256]{1,0:T(8,128)(2,1)}, bf16[576,256]{1,0:T(8,128)(2,1)S(1)}, u32[]{:S(2)}, u32[]{:S(2)}) collective-permute-start(bf16[576,256]{1,0:T(8,128)(2,1)} %bitcast.11), channel_id=1, source_target_pairs={{0,12},{4,8},{8,20},{12,16},{16,28},{20,24},{24,4},{28,0},{1,13},{... | collective-permute-start | bytes 884744 | tf_op jit(solution)/shard_map/ppermute | solution.py:515
  3.1 0.1 pad_add_fusion.place
  3.1 2.1 %pack_rows.1 = (bf16[704,256]{1,0:T(8,128)(2,1)S(1)}, bf16[128,256]{1,0:T(8,128)(2,1)S(1)}, bf16[32,2176]{1,0:T(8,128)(2,1)S(1)}, bf16[32,2176]{1,0:T(8,128)(2,1...) custom-call(s32[2]{0:T(128)S(1)} %pad_add_fusion.place, bf16[576,256]{1,0:T(8,128)(2,1)} %bitcast.12, ...), custom_call_target="tpu_custom_call" | custom-call | flops 1 | bytes 1 | tf_op jit(solution)/shard_map/pack_rows/pallas_call | solution.py:559
  5.2 1.6 %collective-permute-start.2 = (bf16[32,2176]{1,0:T(8,128)(2,1)S(1)}, bf16[32,2176]{1,0:T(8,128)(2,1)S(1)}, u32[]{:S(2)}, u32[]{:S(2)}) collective-permute-start(bf16[32,2176]{1,0:T(8,128)(2,1)S(1)} %get-tuple-element.33), channel_id=1, source_target_pairs={{0,1},{1,0},{2,3},{3,2},{4,5},{5,4},{6,7},{7,6},{8,9},{9,8},{10,11... | collective-permute-start | bytes 417800 | tf_op jit(solution)/shard_map/ppermute | solution.py:515
  6.9 0.4 collective-permute-start
  7.3 1.0 %copy-done = bf16[256,576]{0,1:T(8,128)(2,1)S(1)} copy-done((bf16[256,576]{0,1:T(8,128)(2,1)S(1)}, bf16[256,576]{0,1:T(8,128)(2,1)}, u32[]{:S(2)}) %copy-start) | copy-done | bytes 294936
  8.2 3.7 %own_block.1.own_exp = f32[4096,256]{1,0:T(8,128)S(1)} custom-call(bf16[128,18432]{1,0:T(8,128)(2,1)} %q.5, bf16[576,256]{1,0:T(8,128)(2,1)S(1)} %bitcast.13, s32[1,128]{1,0:T(1,128)} %bitcast.21, s32[1,256]{1,0:T(1,128)} %bitcast.18), custom_call_target="tpu_custom_call" | custom-call | flops 1 | bytes 1 | tf_op jit(solution)/shard_map/own_block/pallas_call | solution.py:580
  12.0 0.0 collective-permute-done.2.rest_1_
  12.0 1.3 %collective-permute-start.7 = (bf16[576,256]{1,0:T(8,128)(2,1)S(1)}, bf16[576,256]{1,0:T(8,128)(2,1)S(1)}, u32[]{:S(2)}, u32[]{:S(2)}) collective-permute-start(bf16[576,256]{1,0:T(8,128)(2,1)S(1)} %collective-permute-done.1.block.b), channel_id=1, source_target_pairs={{0,4},{4,0},{8,12},{12,8},{16,20},{20,16},{24,28},{28,24},{1,5},{5... | collective-permute-start | bytes 884744 | tf_op jit(solution)/shard_map/ppermute | solution.py:515
  13.3 2.6 %collective-permute-start.5 = (bf16[32,2176]{1,0:T(8,128)(2,1)S(1)}, bf16[32,2176]{1,0:T(8,128)(2,1)S(1)}, u32[]{:S(2)}, u32[]{:S(2)}) collective-permute-start(bf16[32,2176]{1,0:T(8,128)(2,1)S(1)} %get-tuple-element.38), channel_id=1, source_target_pairs={{0,2},{1,3},{2,0},{3,1},{4,6},{5,7},{6,4},{7,5},{8,10},{9,11},{10,... | collective-permute-start | bytes 417800 | tf_op jit(solution)/shard_map/ppermute | solution.py:515
  15.9 0.6 collective-permute-start.6
  16.5 1.8 %next_block.1.b_exp = f32[4096,256]{1,0:T(8,128)S(1)} custom-call(bf16[128,18432]{1,0:T(8,128)(2,1)S(1)} %bitcast.10, bf16[576,256]{1,0:T(8,128)(2,1)S(1)} %collective-permute-done.1.block.b), custom_call_target="tpu_custom_call" | custom-call | flops 1 | bytes 1 | tf_op jit(solution)/shard_map/next_block/pallas_call | solution.py:598
  18.4 0.2 collective-permute-start.3
  18.6 0.0 copy-start.6
  18.6 25.4 %main_mass.1 = (f32[32,1024]{1,0:T(8,128)S(1)}, s16[32,1152]{1,0:T(8,128)(2,1)S(1)}, s16[32,1152]{1,0:T(8,128)(2,1)S(1)}, s16[32,1152]{1,0:T(8,128)(2,1)S(1)}) custom-call(s32[2]{0:T(128)S(1)} %pad_add_fusion.place, bf16[128,18432]{1,0:T(8,128)(2,1)S(1)} %bitcast.10, bf16[576,256]{1,0:T(8,128)(2,1)S(1)} %bitcast.14, ...), custom_call_target="tpu_custom_call" | custom-call | flops 1 | bytes 1 | tf_op jit(solution)/shard_map/main_mass/pallas_call | solution.py:615
  44.0 0.0 copy-start.1
  44.0 0.0 copy-start.2
  44.0 3.2 %collective-permute-start.8 = (s16[32,1152]{1,0:T(8,128)(2,1)S(1)}, s16[32,1152]{1,0:T(8,128)(2,1)S(1)}, u32[]{:S(2)}, u32[]{:S(2)}) collective-permute-start(s16[32,1152]{1,0:T(8,128)(2,1)S(1)} %get-tuple-element.45), channel_id=1, source_target_pairs={{0,3},{1,2},{2,1},{3,0},{4,7},{5,6},{6,5},{7,4},{8,11},{9,10},{10,... | collective-permute-start | bytes 221192 | tf_op jit(solution)/shard_map/ppermute | solution.py:515
  47.2 0.0 collective-permute-start.9
  47.2 0.0 collective-permute-done.5.rest_2_
  47.2 1.3 %collective-permute-start.10 = (s16[32,1152]{1,0:T(8,128)(2,1)S(1)}, s16[32,1152]{1,0:T(8,128)(2,1)S(1)}, u32[]{:S(2)}, u32[]{:S(2)}) collective-permute-start(s16[32,1152]{1,0:T(8,128)(2,1)S(1)} %get-tuple-element.47), channel_id=1, source_target_pairs={{0,1},{1,0},{2,3},{3,2},{4,5},{5,4},{6,7},{7,6},{8,9},{9,8},{10,11... | collective-permute-start | bytes 221192 | tf_op jit(solution)/shard_map/ppermute | solution.py:515
  48.5 0.0 collective-permute-done.3.b
  48.5 0.0 collective-permute-start.4
  48.5 0.0 collective-permute-done.6.rest_3_
  48.5 1.2 %collective-permute-done.4.c = bf16[128,256]{1,0:T(8,128)(2,1)S(1)} collective-permute-done((bf16[128,256]{1,0:T(8,128)(2,1)S(1)}, bf16[128,256]{1,0:T(8,128)(2,1)S(1)}, u32[]{:S(2)}, u32[]{:S(2)}) %collective-permute-start.4) | collective-permute-done | bytes 65568 | tf_op jit(solution)/shard_map/ppermute | solution.py:515
  49.7 2.7 %index_scores.1 = (f32[32,1024]{1,0:T(8,128)S(1)}, bf16[2048,1024]{1,0:T(8,128)(2,1)S(1)}, bf16[256,2048]{1,0:T(8,128)(2,1)S(1)}) custom-call(s32[2]{0:T(128)S(1)} %pad_add_fusion.place, bf16[128,256]{1,0:T(8,128)(2,1)S(1)} %get-tuple-element.35.own, bf16[704,256]{1,0:T(8,128)(2,1)S(1)} %collective-permute-done.a, ...), custom_call_target="tpu_custom_call" | custom-call | flops 1 | bytes 1 | tf_op jit(solution)/shard_map/index_scores/pallas_call | solution.py:636
  52.5 0.0 collective-permute-done.8.m3
  52.5 1.4 %collective-permute-done.9.m2 = s16[32,1152]{1,0:T(8,128)(2,1)S(1)} collective-permute-done((s16[32,1152]{1,0:T(8,128)(2,1)S(1)}, s16[32,1152]{1,0:T(8,128)(2,1)S(1)}, u32[]{:S(2)}, u32[]{:S(2)}) %collective-permute-start.9) | collective-permute-done | bytes 73760 | tf_op jit(solution)/shard_map/ppermute | solution.py:515
  53.9 1.0 %dscores.1 = (bf16[2,32,1024]{2,1,0:T(8,128)(2,1)S(1)}, s16[32,1152]{1,0:T(8,128)(2,1)S(1)}) custom-call(s32[2]{0:T(128)S(1)} %pad_add_fusion.place, f32[32,1024]{1,0:T(8,128)S(1)} %get-tuple-element.44.m0, s16[32,1152]{1,0:T(8,128)(2,1)S(1)} %collective-permute-done.8.m3, s16[32,1152]{1,0:T(8,128)(2,1)S(1)} %collective-permute-done.9.m2, ...), custom_call_target="tpu_custom_call" | custom-call | flops 1 | bytes 1 | tf_op jit(solution)/shard_map/dscores/pallas_call | solution.py:656
  54.9 2.0 %key_grads.1 = (s16[272,128]{1,0:T(8,128)(2,1)S(1)}, s16[272,128]{1,0:T(8,128)(2,1)S(1)}, s16[272,128]{1,0:T(8,128)(2,1)S(1)}, f32[256,128]{1,0:T(8,128)S(1)}) custom-call(bf16[2048,1024]{1,0:T(8,128)(2,1)S(1)} %get-tuple-element.40.gate, bf16[256,2048]{1,0:T(8,128)(2,1)S(1)} %get-tuple-element.41.turned, bf16[2,32,1024]{2,1,0:T(8,128)(2,1)S(1)} %get-tuple-element.49.spread), custom_call_target="tpu_custom_call" | custom-call | flops 1 | bytes 1 | tf_op jit(solution)/shard_map/key_grads/pallas_call | solution.py:671
  56.9 2.0 %collective-permute-start.14 = (s16[272,128]{1,0:T(8,128)(2,1)S(1)}, s16[272,128]{1,0:T(8,128)(2,1)S(1)}, u32[]{:S(2)}, u32[]{:S(2)}) collective-permute-start(s16[272,128]{1,0:T(8,128)(2,1)S(1)} %get-tuple-element.56), channel_id=1, source_target_pairs={{0,28},{4,0},{8,4},{12,8},{16,12},{20,16},{24,20},{28,24},{1,29},{... | collective-permute-start | bytes 208904 | tf_op jit(solution)/shard_map/ppermute | solution.py:515
  58.9 2.1 %collective-permute-start.13 = (s16[32,1152]{1,0:T(8,128)(2,1)S(1)}, s16[32,1152]{1,0:T(8,128)(2,1)S(1)}, u32[]{:S(2)}, u32[]{:S(2)}) collective-permute-start(s16[32,1152]{1,0:T(8,128)(2,1)S(1)} %get-tuple-element.52.c0), channel_id=1, source_target_pairs={{0,3},{1,2},{2,1},{3,0},{4,7},{5,6},{6,5},{7,4},{8,11},{9,10},{10,... | collective-permute-start | bytes 221192 | tf_op jit(solution)/shard_map/ppermute | solution.py:515
  61.0 1.0 %collective-permute-start.15 = (s16[272,128]{1,0:T(8,128)(2,1)S(1)}, s16[272,128]{1,0:T(8,128)(2,1)S(1)}, u32[]{:S(2)}, u32[]{:S(2)}) collective-permute-start(s16[272,128]{1,0:T(8,128)(2,1)S(1)} %get-tuple-element.57), channel_id=1, source_target_pairs={{0,24},{4,28},{8,0},{12,4},{16,8},{20,12},{24,16},{28,20},{1,25},{... | collective-permute-start | bytes 208904 | tf_op jit(solution)/shard_map/ppermute | solution.py:515
  61.9 0.9 %collective-permute-start.16 = (s16[272,128]{1,0:T(8,128)(2,1)S(1)}, s16[272,128]{1,0:T(8,128)(2,1)S(1)}, u32[]{:S(2)}, u32[]{:S(2)}) collective-permute-start(s16[272,128]{1,0:T(8,128)(2,1)S(1)} %get-tuple-element.58), channel_id=1, source_target_pairs={{0,20},{4,24},{8,28},{12,0},{16,4},{20,8},{24,12},{28,16},{1,21},{... | collective-permute-start | bytes 208904 | tf_op jit(solution)/shard_map/ppermute | solution.py:515
  62.8 0.0 collective-permute-start.12
  62.8 0.0 collective-permute-done.14.c1
  62.8 1.9 %collective-permute-start.11 = (s16[32,1152]{1,0:T(8,128)(2,1)S(1)}, s16[32,1152]{1,0:T(8,128)(2,1)S(1)}, u32[]{:S(2)}, u32[]{:S(2)}) collective-permute-start(s16[32,1152]{1,0:T(8,128)(2,1)S(1)} %get-tuple-element.52.c0), channel_id=1, source_target_pairs={{0,1},{1,0},{2,3},{3,2},{4,5},{5,4},{6,7},{7,6},{8,9},{9,8},{10,11... | collective-permute-start | bytes 221192 | tf_op jit(solution)/shard_map/ppermute | solution.py:515
  64.7 1.0 %collective-permute-done.15.c2 = s16[272,128]{1,0:T(8,128)(2,1)S(1)} collective-permute-done((s16[272,128]{1,0:T(8,128)(2,1)S(1)}, s16[272,128]{1,0:T(8,128)(2,1)S(1)}, u32[]{:S(2)}, u32[]{:S(2)}) %collective-permute-start.15) | collective-permute-done | bytes 69664 | tf_op jit(solution)/shard_map/ppermute | solution.py:515
  65.7 0.3 collective-permute-done.16.c3
  66.0 0.1 owned_keys.1.c0
  66.1 1.8 %collective-permute-start.19 = (s16[272,128]{1,0:T(8,128)(2,1)S(1)}, s16[272,128]{1,0:T(8,128)(2,1)S(1)}, u32[]{:S(2)}, u32[]{:S(2)}) collective-permute-start(s16[272,128]{1,0:T(8,128)(2,1)S(1)} %owned_keys.1.c0), channel_id=1, source_target_pairs={{0,3},{1,2},{2,1},{3,0},{4,7},{5,6},{6,5},{7,4},{8,11},{9,10},{10,... | collective-permute-start | bytes 208904 | tf_op jit(solution)/shard_map/ppermute | solution.py:515
  67.9 0.0 collective-permute-done.13.c3
  67.9 2.7 %collective-permute-start.17 = (s16[272,128]{1,0:T(8,128)(2,1)S(1)}, s16[272,128]{1,0:T(8,128)(2,1)S(1)}, u32[]{:S(2)}, u32[]{:S(2)}) collective-permute-start(s16[272,128]{1,0:T(8,128)(2,1)S(1)} %owned_keys.1.c0), channel_id=1, source_target_pairs={{0,1},{1,0},{2,3},{3,2},{4,5},{5,4},{6,7},{7,6},{8,9},{9,8},{10,11... | collective-permute-start | bytes 208904 | tf_op jit(solution)/shard_map/ppermute | solution.py:515
  70.6 0.0 collective-permute-done.12.c2
  70.6 5.0 %query_grads.1 = (bf16[128,2048]{1,0:T(8,128)(2,1)}, f32[16,128]{1,0:T(8,128)}) custom-call(s32[2]{0:T(128)S(1)} %pad_add_fusion.place, bf16[128,256]{1,0:T(8,128)(2,1)S(1)} %get-tuple-element.35.own, bf16[704,256]{1,0:T(8,128)(2,1)S(1)} %collective-permute-done.a, bf16[128,256]{1,0:T(8,128)(2,1)S(1)} %collective-permute-done.3.b, ...), custom_call_target="tpu_custom_call" | custom-call | flops 1 | bytes 1 | tf_op jit(solution)/shard_map/query_grads/pallas_call | solution.py:691
  75.7 0.0 collective-permute-done.19.c3
  75.7 0.0 collective-permute-done.18.c2
  75.7 0.7 total_keys.1
  (22 shorter events, 0.0 us)
Async XLA Ops:
  0.6 11.4 %collective-permute-start.1 = (bf16[576,256]{1,0:T(8,128)(2,1)}, bf16[576,256]{1,0:T(8,128)(2,1)S(1)}, u32[]{:S(2)}, u32[]{:S(2)}) collective-permute-start(bf16[576,256]{1,0:T(8,128)(2,1)} %bitcast.11), channel_id=1, source_target_pairs={{0,12},{4,8},{8,20},{12,16},{16,28},{20,24},{24,4},{28,0},{1,13},{... | collective-permute-start | bytes 884744 | tf_op jit(solution)/shard_map/ppermute | solution.py:515
  3.1 13.4 %slice-start = ((s8[4718592]{0:T(1024)(128)(4,1)}), s8[4194304]{0:T(1024)(128)(4,1)S(1)}, s32[]{:S(2)}) async-start(s8[4718592]{0:T(1024)(128)(4,1)} %bitcast.9), calls=%async_computation | async-start | bytes 8388608
  5.2 6.8 %collective-permute-start.2 = (bf16[32,2176]{1,0:T(8,128)(2,1)S(1)}, bf16[32,2176]{1,0:T(8,128)(2,1)S(1)}, u32[]{:S(2)}, u32[]{:S(2)}) collective-permute-start(bf16[32,2176]{1,0:T(8,128)(2,1)S(1)} %get-tuple-element.33), channel_id=1, source_target_pairs={{0,1},{1,0},{2,3},{3,2},{4,5},{5,4},{6,7},{7,6},{8,9},{9,8},{10,11... | collective-permute-start | bytes 417800 | tf_op jit(solution)/shard_map/ppermute | solution.py:515
  6.9 11.7 %collective-permute-start = (bf16[704,256]{1,0:T(8,128)(2,1)S(1)}, bf16[704,256]{1,0:T(8,128)(2,1)S(1)}, u32[]{:S(2)}, u32[]{:S(2)}) collective-permute-start(bf16[704,256]{1,0:T(8,128)(2,1)S(1)} %get-tuple-element.32), channel_id=1, source_target_pairs={{0,4},{4,16},{8,12},{12,24},{16,20},{20,0},{24,28},{28,8},{1,5},{5... | collective-permute-start | bytes 1081352 | tf_op jit(solution)/shard_map/ppermute | solution.py:515
  7.3 1.0 %copy-start = (bf16[256,576]{0,1:T(8,128)(2,1)S(1)}, bf16[256,576]{0,1:T(8,128)(2,1)}, u32[]{:S(2)}) copy-start(bf16[256,576]{0,1:T(8,128)(2,1)} %param.10) | copy-start | bytes 884740
  8.2 8.3 %slice-start.1 = ((s8[4718592]{0:T(1024)(128)(4,1)}), s8[524288]{0:T(1024)(128)(4,1)S(1)}, s32[]{:S(2)}) async-start(s8[4718592]{0:T(1024)(128)(4,1)} %bitcast.9), calls=%async_computation.1 | async-start | bytes 1048576
  12.0 6.5 %collective-permute-start.7 = (bf16[576,256]{1,0:T(8,128)(2,1)S(1)}, bf16[576,256]{1,0:T(8,128)(2,1)S(1)}, u32[]{:S(2)}, u32[]{:S(2)}) collective-permute-start(bf16[576,256]{1,0:T(8,128)(2,1)S(1)} %collective-permute-done.1.block.b), channel_id=1, source_target_pairs={{0,4},{4,0},{8,12},{12,8},{16,20},{20,16},{24,28},{28,24},{1,5},{5... | collective-permute-start | bytes 884744 | tf_op jit(solution)/shard_map/ppermute | solution.py:515
  13.3 33.9 %collective-permute-start.5 = (bf16[32,2176]{1,0:T(8,128)(2,1)S(1)}, bf16[32,2176]{1,0:T(8,128)(2,1)S(1)}, u32[]{:S(2)}, u32[]{:S(2)}) collective-permute-start(bf16[32,2176]{1,0:T(8,128)(2,1)S(1)} %get-tuple-element.38), channel_id=1, source_target_pairs={{0,2},{1,3},{2,0},{3,1},{4,6},{5,7},{6,4},{7,5},{8,10},{9,11},{10,... | collective-permute-start | bytes 417800 | tf_op jit(solution)/shard_map/ppermute | solution.py:515
  15.9 2.7 %copy-start.3 = (f32[128,32]{0,1:T(8,128)S(1)}, f32[128,32]{0,1:T(8,128)}, u32[]{:S(2)}) copy-start(f32[128,32]{0,1:T(8,128)} %param.11) | copy-start | bytes 49156
  15.9 2.7 %copy-start.4 = (s32[256]{0:T(256)S(1)}, s32[256]{0:T(256)}, u32[]{:S(2)}) copy-start(s32[256]{0:T(256)} %param.17) | copy-start | bytes 3076
  15.9 2.7 %copy-start.5 = (s32[128]{0:T(128)S(1)}, s32[128]{0:T(128)}, u32[]{:S(2)}) copy-start(s32[128]{0:T(128)} %param.16) | copy-start | bytes 1540
  15.9 32.6 %collective-permute-start.6 = (bf16[32,2176]{1,0:T(8,128)(2,1)S(1)}, bf16[32,2176]{1,0:T(8,128)(2,1)S(1)}, u32[]{:S(2)}, u32[]{:S(2)}) collective-permute-start(bf16[32,2176]{1,0:T(8,128)(2,1)S(1)} %get-tuple-element.39), channel_id=1, source_target_pairs={{0,3},{1,2},{2,1},{3,0},{4,7},{5,6},{6,5},{7,4},{8,11},{9,10},{10,... | collective-permute-start | bytes 417800 | tf_op jit(solution)/shard_map/ppermute | solution.py:515
  18.4 30.1 %collective-permute-start.3 = (bf16[128,256]{1,0:T(8,128)(2,1)S(1)}, bf16[128,256]{1,0:T(8,128)(2,1)S(1)}, u32[]{:S(2)}, u32[]{:S(2)}) collective-permute-start(bf16[128,256]{1,0:T(8,128)(2,1)S(1)} %get-tuple-element.35.own), channel_id=1, source_target_pairs={{0,12},{4,8},{8,20},{12,16},{16,28},{20,24},{24,4},{28,0},{1,13},{... | collective-permute-start | bytes 196616 | tf_op jit(solution)/shard_map/ppermute | solution.py:515
  18.6 35.4 %copy-start.6 = (f32[128]{0:T(128)S(1)}, f32[128]{0:T(128)}, u32[]{:S(2)}) copy-start(f32[128]{0:T(128)} %param.15) | copy-start | bytes 1540
  44.0 26.6 %copy-start.1 = (bf16[128,2048]{1,0:T(8,128)(2,1)S(1)}, bf16[128,2048]{1,0:T(8,128)(2,1)}, u32[]{:S(2)}) copy-start(bf16[128,2048]{1,0:T(8,128)(2,1)} %query.3) | copy-start | bytes 1572868
  44.0 26.6 %copy-start.2 = (f32[128,16]{0,1:T(8,128)S(1)}, f32[128,16]{0,1:T(8,128)}, u32[]{:S(2)}) copy-start(f32[128,16]{0,1:T(8,128)} %param.13) | copy-start | bytes 24580
  44.0 8.5 %collective-permute-start.8 = (s16[32,1152]{1,0:T(8,128)(2,1)S(1)}, s16[32,1152]{1,0:T(8,128)(2,1)S(1)}, u32[]{:S(2)}, u32[]{:S(2)}) collective-permute-start(s16[32,1152]{1,0:T(8,128)(2,1)S(1)} %get-tuple-element.45), channel_id=1, source_target_pairs={{0,3},{1,2},{2,1},{3,0},{4,7},{5,6},{6,5},{7,4},{8,11},{9,10},{10,... | collective-permute-start | bytes 221192 | tf_op jit(solution)/shard_map/ppermute | solution.py:515
  47.2 6.7 %collective-permute-start.9 = (s16[32,1152]{1,0:T(8,128)(2,1)S(1)}, s16[32,1152]{1,0:T(8,128)(2,1)S(1)}, u32[]{:S(2)}, u32[]{:S(2)}) collective-permute-start(s16[32,1152]{1,0:T(8,128)(2,1)S(1)} %get-tuple-element.46), channel_id=1, source_target_pairs={{0,2},{1,3},{2,0},{3,1},{4,6},{5,7},{6,4},{7,5},{8,10},{9,11},{10,... | collective-permute-start | bytes 221192 | tf_op jit(solution)/shard_map/ppermute | solution.py:515
  47.2 6.7 %collective-permute-start.10 = (s16[32,1152]{1,0:T(8,128)(2,1)S(1)}, s16[32,1152]{1,0:T(8,128)(2,1)S(1)}, u32[]{:S(2)}, u32[]{:S(2)}) collective-permute-start(s16[32,1152]{1,0:T(8,128)(2,1)S(1)} %get-tuple-element.47), channel_id=1, source_target_pairs={{0,1},{1,0},{2,3},{3,2},{4,5},{5,4},{6,7},{7,6},{8,9},{9,8},{10,11... | collective-permute-start | bytes 221192 | tf_op jit(solution)/shard_map/ppermute | solution.py:515
  48.5 1.3 %collective-permute-start.4 = (bf16[128,256]{1,0:T(8,128)(2,1)S(1)}, bf16[128,256]{1,0:T(8,128)(2,1)S(1)}, u32[]{:S(2)}, u32[]{:S(2)}) collective-permute-start(bf16[128,256]{1,0:T(8,128)(2,1)S(1)} %collective-permute-done.3.b), channel_id=1, source_target_pairs={{0,4},{4,0},{8,12},{12,8},{16,20},{20,16},{24,28},{28,24},{1,5},{5... | collective-permute-start | bytes 196616 | tf_op jit(solution)/shard_map/ppermute | solution.py:515
  56.9 6.0 %collective-permute-start.14 = (s16[272,128]{1,0:T(8,128)(2,1)S(1)}, s16[272,128]{1,0:T(8,128)(2,1)S(1)}, u32[]{:S(2)}, u32[]{:S(2)}) collective-permute-start(s16[272,128]{1,0:T(8,128)(2,1)S(1)} %get-tuple-element.56), channel_id=1, source_target_pairs={{0,28},{4,0},{8,4},{12,8},{16,12},{20,16},{24,20},{28,24},{1,29},{... | collective-permute-start | bytes 208904 | tf_op jit(solution)/shard_map/ppermute | solution.py:515
  58.9 9.1 %collective-permute-start.13 = (s16[32,1152]{1,0:T(8,128)(2,1)S(1)}, s16[32,1152]{1,0:T(8,128)(2,1)S(1)}, u32[]{:S(2)}, u32[]{:S(2)}) collective-permute-start(s16[32,1152]{1,0:T(8,128)(2,1)S(1)} %get-tuple-element.52.c0), channel_id=1, source_target_pairs={{0,3},{1,2},{2,1},{3,0},{4,7},{5,6},{6,5},{7,4},{8,11},{9,10},{10,... | collective-permute-start | bytes 221192 | tf_op jit(solution)/shard_map/ppermute | solution.py:515
  61.0 4.8 %collective-permute-start.15 = (s16[272,128]{1,0:T(8,128)(2,1)S(1)}, s16[272,128]{1,0:T(8,128)(2,1)S(1)}, u32[]{:S(2)}, u32[]{:S(2)}) collective-permute-start(s16[272,128]{1,0:T(8,128)(2,1)S(1)} %get-tuple-element.57), channel_id=1, source_target_pairs={{0,24},{4,28},{8,0},{12,4},{16,8},{20,12},{24,16},{28,20},{1,25},{... | collective-permute-start | bytes 208904 | tf_op jit(solution)/shard_map/ppermute | solution.py:515
  61.9 4.1 %collective-permute-start.16 = (s16[272,128]{1,0:T(8,128)(2,1)S(1)}, s16[272,128]{1,0:T(8,128)(2,1)S(1)}, u32[]{:S(2)}, u32[]{:S(2)}) collective-permute-start(s16[272,128]{1,0:T(8,128)(2,1)S(1)} %get-tuple-element.58), channel_id=1, source_target_pairs={{0,20},{4,24},{8,28},{12,0},{16,4},{20,8},{24,12},{28,16},{1,21},{... | collective-permute-start | bytes 208904 | tf_op jit(solution)/shard_map/ppermute | solution.py:515
  62.8 7.8 %collective-permute-start.12 = (s16[32,1152]{1,0:T(8,128)(2,1)S(1)}, s16[32,1152]{1,0:T(8,128)(2,1)S(1)}, u32[]{:S(2)}, u32[]{:S(2)}) collective-permute-start(s16[32,1152]{1,0:T(8,128)(2,1)S(1)} %get-tuple-element.52.c0), channel_id=1, source_target_pairs={{0,2},{1,3},{2,0},{3,1},{4,6},{5,7},{6,4},{7,5},{8,10},{9,11},{10,... | collective-permute-start | bytes 221192 | tf_op jit(solution)/shard_map/ppermute | solution.py:515
  62.8 7.8 %collective-permute-start.11 = (s16[32,1152]{1,0:T(8,128)(2,1)S(1)}, s16[32,1152]{1,0:T(8,128)(2,1)S(1)}, u32[]{:S(2)}, u32[]{:S(2)}) collective-permute-start(s16[32,1152]{1,0:T(8,128)(2,1)S(1)} %get-tuple-element.52.c0), channel_id=1, source_target_pairs={{0,1},{1,0},{2,3},{3,2},{4,5},{5,4},{6,7},{7,6},{8,9},{9,8},{10,11... | collective-permute-start | bytes 221192 | tf_op jit(solution)/shard_map/ppermute | solution.py:515
  66.1 9.5 %collective-permute-start.19 = (s16[272,128]{1,0:T(8,128)(2,1)S(1)}, s16[272,128]{1,0:T(8,128)(2,1)S(1)}, u32[]{:S(2)}, u32[]{:S(2)}) collective-permute-start(s16[272,128]{1,0:T(8,128)(2,1)S(1)} %owned_keys.1.c0), channel_id=1, source_target_pairs={{0,3},{1,2},{2,1},{3,0},{4,7},{5,6},{6,5},{7,4},{8,11},{9,10},{10,... | collective-permute-start | bytes 208904 | tf_op jit(solution)/shard_map/ppermute | solution.py:515
  67.9 7.7 %collective-permute-start.18 = (s16[272,128]{1,0:T(8,128)(2,1)S(1)}, s16[272,128]{1,0:T(8,128)(2,1)S(1)}, u32[]{:S(2)}, u32[]{:S(2)}) collective-permute-start(s16[272,128]{1,0:T(8,128)(2,1)S(1)} %owned_keys.1.c0), channel_id=1, source_target_pairs={{0,2},{1,3},{2,0},{3,1},{4,6},{5,7},{6,4},{7,5},{8,10},{9,11},{10,... | collective-permute-start | bytes 208904 | tf_op jit(solution)/shard_map/ppermute | solution.py:515
  67.9 7.7 %collective-permute-start.17 = (s16[272,128]{1,0:T(8,128)(2,1)S(1)}, s16[272,128]{1,0:T(8,128)(2,1)S(1)}, u32[]{:S(2)}, u32[]{:S(2)}) collective-permute-start(s16[272,128]{1,0:T(8,128)(2,1)S(1)} %owned_keys.1.c0), channel_id=1, source_target_pairs={{0,1},{1,0},{2,3},{3,2},{4,5},{5,4},{6,7},{7,6},{8,9},{9,8},{10,11... | collective-permute-start | bytes 208904 | tf_op jit(solution)/shard_map/ppermute | solution.py:515
